TPU v7x, 32 devices: a whole 2x2x4 slice. The times are simulated.
32 devices in a mesh: dp: 4 (over y, x), ctx: 8 (over z, core).
Axes of the slice: x: 2, y: 2, z: 4, core: 2. Of those that a mesh axis runs over, the one named last changes fastest.
Arguments:
- query_rows: bfloat16 [4, 1024, 4096], P('dp', 'ctx'), may hold values from -6 to 6
- key_rows: bfloat16 [4, 1024, 4096], P('dp', 'ctx'), may hold values from -6 to 6
- value_rows: bfloat16 [4, 1024, 4096], P('dp', 'ctx'), may hold values from -6 to 6
- cotangent: bfloat16 [4, 1024, 4096], P('dp', 'ctx'), may hold values from -6 to 6
- feature_taps: float32 [7, 3, 4096], replicated, may hold values from -2 to 2
- filter_taps: float32 [256, 128], replicated, may hold values from -0.5 to 0.5
- skip_gain: float32 [4096], replicated, may hold values from -4 to 4
Outputs:
- mixer_out: bfloat16 [4, 1024, 4096], P('dp', 'ctx')
- grad_query: bfloat16 [4, 1024, 4096], P('dp', 'ctx')
- grad_key: bfloat16 [4, 1024, 4096], P('dp', 'ctx')
- grad_value: bfloat16 [4, 1024, 4096], P('dp', 'ctx')
- grad_feature_taps: float32 [7, 3, 4096], replicated
- grad_filter_taps: float32 [256, 128], replicated
- grad_skip_gain: float32 [4096], replicated
All inputs are finite; a program needn't handle non-finite values.
Results may differ from a plain program's by a relative error of at most 0.0075.
Values may be sent and summed in bfloat16 or wider, within the bound.
No kernel may reach another device: no remote copies, remote signals or barrier semaphores. Data moves between devices by JAX's collectives and lax.ppermute only.
A program may use at most 256 MiB of HBM per device.

v0:
```python
import jax
import jax.numpy as jnp
from jax import lax
from jax.sharding import PartitionSpec as P


def toeplitz(taps_bf, block_len):
    group_count = taps_bf.shape[0]
    window_len = block_len + taps_bf.shape[1] - 1
    padded_line = jnp.concatenate(
        [
            jnp.zeros((group_count, block_len - 1), taps_bf.dtype),
            taps_bf,
            jnp.zeros((group_count, block_len), taps_bf.dtype),
        ],
        axis=1,
    )
    line_len = padded_line.shape[1]
    flattened = jnp.broadcast_to(
        padded_line[:, None, :], (group_count, block_len, line_len)
    ).reshape(group_count, block_len * line_len)
    trimmed = flattened[:, block_len - 1 : block_len - 1 + block_len * (line_len - 1)].reshape(
        group_count, block_len, line_len - 1
    )
    return trimmed[:, :, :window_len]


def apply_filter(blocks, edges, matrix, before):
    block_count, block_len, channel_count = blocks.shape
    group_count = matrix.shape[0]
    if before:
        window = jnp.concatenate([edges, blocks], axis=1)
    else:
        window = jnp.concatenate([blocks, edges], axis=1)
    shaped = window.reshape(block_count, window.shape[1], group_count, channel_count // group_count)
    result = jnp.einsum("gts,bsgc->btgc", matrix, shaped, preferred_element_type=jnp.float32)
    return (result.reshape(block_count, block_len, channel_count), window)


def filter_grad(grad_blocks, window, group_count, taps_len):
    block_count, block_len, channel_count = grad_blocks.shape
    window_len = window.shape[1]
    left = grad_blocks.reshape(block_count, block_len, group_count, channel_count // group_count)
    right = window.reshape(block_count, window_len, group_count, channel_count // group_count)
    products = jnp.einsum("btgc,bsgc->gts", left, right, preferred_element_type=jnp.float32)
    flattened = products.reshape(group_count, block_len * window_len)
    flattened = jnp.concatenate(
        [flattened, jnp.zeros((group_count, block_len), jnp.float32)], axis=1
    )
    skewed = flattened.reshape(group_count, block_len, window_len + 1)
    return jnp.sum(skewed[:, :, :taps_len], axis=1)[:, ::-1]


def featurize(extended, weights, row_count):
    feat_depth = weights.shape[0] - 1
    running = jnp.zeros((row_count, extended.shape[1]), jnp.float32)
    for lag_index in range(weights.shape[0]):
        offset_row = feat_depth - lag_index
        running = running + weights[lag_index] * extended[
            offset_row : offset_row + row_count
        ].astype(jnp.float32)
    return running


def unfeaturize(extended, weights, row_count):
    running = jnp.zeros((row_count, extended.shape[1]), jnp.float32)
    for lag_index in range(weights.shape[0]):
        running = running + weights[lag_index] * extended[lag_index : lag_index + row_count]
    return running


def blank_rows(piece):
    return jnp.zeros_like(piece)


def mixer_core(
    query_part,
    key_part,
    value_part,
    cot_part,
    taps,
    filters,
    gains,
    grad_scale,
    fetch_before,
    fetch_mixer,
    fetch_after,
    fetch_feature,
):
    row_count, channel_count = query_part.shape
    feat_depth = taps.shape[0] - 1
    taps_len = filters.shape[1]
    group_count = filters.shape[0]
    cut_row = row_count - feat_depth
    stacked = jnp.stack([query_part[cut_row:], key_part[cut_row:], value_part[cut_row:]])
    before_rows = fetch_before(stacked)
    query_ext = jnp.concatenate([before_rows[0], query_part], axis=0)
    key_ext = jnp.concatenate([before_rows[1], key_part], axis=0)
    value_ext = jnp.concatenate([before_rows[2], value_part], axis=0)
    query_feat = featurize(query_ext, taps[:, 0], row_count)
    key_feat = featurize(key_ext, taps[:, 1], row_count)
    value_feat = featurize(value_ext, taps[:, 2], row_count)
    mix_in = (key_feat * value_feat).astype(jnp.bfloat16)
    block_count = row_count // taps_len
    blocks = mix_in.reshape(block_count, taps_len, channel_count)
    edge_rows = fetch_mixer(mix_in[row_count - (taps_len - 1) :])
    tail_rows = jnp.concatenate([edge_rows[None], blocks[:-1, 1:]], axis=0)
    taps_bf = filters.astype(jnp.bfloat16)
    convolved, window = apply_filter(blocks, tail_rows, toeplitz(taps_bf[:, ::-1], taps_len), True)
    filtered = convolved.reshape(row_count, channel_count) + gains * mix_in.astype(jnp.float32)
    mixer_out = (query_feat * filtered).astype(jnp.bfloat16)
    cot_wide = cot_part.astype(jnp.float32)
    grad_qfeat = cot_wide * filtered
    grad_filtered = (cot_wide * query_feat).astype(jnp.bfloat16)
    grad_blocks = grad_filtered.reshape(block_count, taps_len, channel_count)
    head_rows = fetch_after(grad_filtered[: taps_len - 1])
    lead_rows = jnp.concatenate([grad_blocks[1:, : taps_len - 1], head_rows[None]], axis=0)
    backward, unused = apply_filter(grad_blocks, lead_rows, toeplitz(taps_bf, taps_len), False)
    grad_mixin = backward.reshape(row_count, channel_count) + gains * grad_filtered.astype(
        jnp.float32
    )
    grad_kfeat = grad_mixin * value_feat
    grad_vfeat = grad_mixin * key_feat
    after_rows = fetch_feature(
        jnp.stack([grad_qfeat[:feat_depth], grad_kfeat[:feat_depth], grad_vfeat[:feat_depth]])
    )
    grad_query = unfeaturize(
        jnp.concatenate([grad_qfeat, after_rows[0]], axis=0), taps[:, 0], row_count
    ).astype(jnp.bfloat16)
    grad_key = unfeaturize(
        jnp.concatenate([grad_kfeat, after_rows[1]], axis=0), taps[:, 1], row_count
    ).astype(jnp.bfloat16)
    grad_value = unfeaturize(
        jnp.concatenate([grad_vfeat, after_rows[2]], axis=0), taps[:, 2], row_count
    ).astype(jnp.bfloat16)
    lag_rows = []
    for lag_index in range(feat_depth + 1):
        offset_row = feat_depth - lag_index
        lag_rows.append(
            jnp.stack(
                [
                    jnp.sum(
                        grad_qfeat
                        * query_ext[offset_row : offset_row + row_count].astype(jnp.float32),
                        axis=0,
                    ),
                    jnp.sum(
                        grad_kfeat
                        * key_ext[offset_row : offset_row + row_count].astype(jnp.float32),
                        axis=0,
                    ),
                    jnp.sum(
                        grad_vfeat
                        * value_ext[offset_row : offset_row + row_count].astype(jnp.float32),
                        axis=0,
                    ),
                ]
            )
        )
    grad_feat = jnp.stack(lag_rows) * grad_scale
    grad_filter = filter_grad(grad_blocks, window, group_count, taps_len) * grad_scale
    grad_skip = (
        jnp.sum(mix_in.astype(jnp.float32) * grad_filtered.astype(jnp.float32), axis=0) * grad_scale
    )
    return (mixer_out, grad_query, grad_key, grad_value, grad_feat, grad_filter, grad_skip)


def body(query_rows, key_rows, value_rows, cotangent, feature_taps, filter_taps, skip_gain):
    row_count = query_rows.shape[1]
    channel_count = query_rows.shape[2]
    group_count = filter_taps.shape[0]
    per_group = channel_count // group_count
    grad_scale = float(lax.axis_size("dp") * lax.axis_size("ctx") * row_count) ** (-0.5)
    query_cols, key_cols, value_cols, cot_cols = (
        lax.all_to_all(query_rows, "ctx", split_axis=2, concat_axis=1, tiled=True),
        lax.all_to_all(key_rows, "ctx", split_axis=2, concat_axis=1, tiled=True),
        lax.all_to_all(value_rows, "ctx", split_axis=2, concat_axis=1, tiled=True),
        lax.all_to_all(cotangent, "ctx", split_axis=2, concat_axis=1, tiled=True),
    )
    local_count = query_cols.shape[2]
    local_groups = local_count // per_group
    offset = lax.axis_index("ctx") * local_count
    group_offset = lax.axis_index("ctx") * local_groups
    local_taps = lax.dynamic_slice_in_dim(feature_taps, offset, local_count, 2)
    local_filters = lax.dynamic_slice_in_dim(filter_taps, group_offset, local_groups, 0)
    local_gains = lax.dynamic_slice_in_dim(skip_gain, offset, local_count, 0)
    results = mixer_core(
        query_cols[0],
        key_cols[0],
        value_cols[0],
        cot_cols[0],
        local_taps,
        local_filters,
        local_gains,
        grad_scale,
        blank_rows,
        blank_rows,
        blank_rows,
        blank_rows,
    )
    outputs = (
        lax.all_to_all(results[0][None], "ctx", split_axis=1, concat_axis=2, tiled=True),
        lax.all_to_all(results[1][None], "ctx", split_axis=1, concat_axis=2, tiled=True),
        lax.all_to_all(results[2][None], "ctx", split_axis=1, concat_axis=2, tiled=True),
        lax.all_to_all(results[3][None], "ctx", split_axis=1, concat_axis=2, tiled=True),
    )
    grad_feat = lax.dynamic_update_slice_in_dim(
        jnp.zeros(feature_taps.shape, jnp.float32), results[4], offset, 2
    )
    grad_filter = lax.dynamic_update_slice_in_dim(
        jnp.zeros(filter_taps.shape, jnp.float32), results[5], group_offset, 0
    )
    grad_skip = lax.dynamic_update_slice_in_dim(
        jnp.zeros(skip_gain.shape, jnp.float32), results[6], offset, 0
    )
    summed = lax.psum((grad_feat, grad_filter, grad_skip), ("dp", "ctx"))
    return (outputs[0], outputs[1], outputs[2], outputs[3], summed[0], summed[1], summed[2])


def solution(mesh):
    return jax.shard_map(
        body,
        mesh=mesh,
        in_specs=(
            P("dp", "ctx", None),
            P("dp", "ctx", None),
            P("dp", "ctx", None),
            P("dp", "ctx", None),
            P(),
            P(),
            P(),
        ),
        out_specs=(
            P("dp", "ctx", None),
            P("dp", "ctx", None),
            P("dp", "ctx", None),
            P("dp", "ctx", None),
            P(),
            P(),
            P(),
        ),
        check_vma=False,
    )
```

profile of v0, /device:TPU:0, one launch (start us, length us, event | category | flops | bytes accessed | tf_op | source)
XLA Modules:
  0.0 529.8 jit_solution(13893612155256407654)
XLA Ops:
  7.2 5.1 copy.93
  12.8 22.4 %reduce = bf16[4096,128]{1,0:T(8,128)(2,1)S(1)} reduce(bf16[4096,1,128]{2,1,0:T(2,128)(2,1)S(1)} %bitcast.202, bf16[]{:T(256)} %broadcast.38), dimensions={1}, to_apply=%bitcast.153.reduce_sub_computation | reduce | bytes 2097154
  36.3 6.3 %all-to-all-start = ((bf16[8,2,32768]{2,1,0:T(2,128)(2,1)}), bf16[8,2,32768]{2,1,0:T(2,128)(2,1)S(1)}, u32[]{:S(2)}, u32[]{:S(2)}) async-start(bf16[8,2,32768]{2,1,0:T(2,128)(2,1)} %reshape.113), calls=%async_computation | async-start | bytes 2097152 | tf_op jit(solution)/shard_map/all_to_all | solution.py:175
  42.6 5.0 copy.107
  47.6 23.4 %reduce.1 = bf16[4096,128]{1,0:T(8,128)(2,1)} reduce(bf16[4096,1,128]{2,1,0:T(2,128)(2,1)S(1)} %bitcast.211, bf16[]{:T(256)} %broadcast.38), dimensions={1}, to_apply=%bitcast.161.reduce_sub_computation | reduce | bytes 2097154
  71.0 2.1 reshape.121
  73.1 5.4 %all-to-all-start.4 = ((bf16[8,2,32768]{2,1,0:T(2,128)(2,1)}), bf16[8,2,32768]{2,1,0:T(2,128)(2,1)}, u32[]{:S(2)}, u32[]{:S(2)}) async-start(bf16[8,2,32768]{2,1,0:T(2,128)(2,1)} %reshape.121), calls=%async_computation.4 | async-start | bytes 2097152 | tf_op jit(solution)/shard_map/all_to_all | solution.py:178
  78.5 5.0 copy.97
  83.6 22.4 %reduce.2 = bf16[4096,128]{1,0:T(8,128)(2,1)S(1)} reduce(bf16[4096,1,128]{2,1,0:T(2,128)(2,1)S(1)} %bitcast.212, bf16[]{:T(256)} %broadcast.38), dimensions={1}, to_apply=%bitcast.157.reduce_sub_computation | reduce | bytes 2097154
  107.1 5.1 all-to-all-start.2
  112.2 5.0 copy.95
  117.2 23.4 %reduce.3 = bf16[4096,128]{1,0:T(8,128)(2,1)} reduce(bf16[4096,1,128]{2,1,0:T(2,128)(2,1)S(1)} %bitcast.213, bf16[]{:T(256)} %broadcast.38), dimensions={1}, to_apply=%bitcast.155.reduce_sub_computation | reduce | bytes 2097154
  140.6 2.1 reshape.115
  142.7 5.6 %all-to-all-start.1 = ((bf16[8,2,32768]{2,1,0:T(2,128)(2,1)}), bf16[8,2,32768]{2,1,0:T(2,128)(2,1)}, u32[]{:S(2)}, u32[]{:S(2)}) async-start(bf16[8,2,32768]{2,1,0:T(2,128)(2,1)} %reshape.115), calls=%async_computation.1 | async-start | bytes 2097152 | tf_op jit(solution)/shard_map/all_to_all | solution.py:176
  148.9 4.7 reshape.101
  153.6 2.8 slice.344
  156.4 9.1 %reshape.102 = bf16[32,128,382]{2,1,0:T(8,128)(2,1)} reshape(bf16[32,48896]{1,0:T(8,128)(2,1)S(1)} %slice.344) | data formatting | bytes 6258688 | tf_op jit(solution)/shard_map/reshape | solution.py:22
  167.5 4.3 reshape.114
  173.3 4.3 reshape.122
  179.2 2.0 copy.109
  181.2 3.5 reshape.118
  184.7 2.7 copy.139
  188.9 5.8 %reshape.116 = bf16[4096,1,128]{2,1,0:T(2,128)(2,1)} reshape(bf16[8,2,32768]{2,1,0:T(2,128)(2,1)} %all-to-all-done.1) | data formatting | bytes 2097152
  194.7 2.7 copy.138
  197.4 2.3 copy.96
  199.7 12.2 %fusion.41 = (f32[512]{0:T(512)S(1)}, bf16[1024,512]{1,0:T(8,128)(2,1)}, bf16[1024,512]{1,0:T(8,128)(2,1)}, f32[1024,512]{1,0:T(8,128)}, f32[1024,512]{1,0:T(8,128)}, /*index=5*/f32[1024,512]{1,0:T(8,128)}) fusion(f32[1,8,128,512]{3,2,1,0:T(8,128)S(1)} %copy.109, f32[512]{0:T(512)S(1)} %bitcast.258, f32[512]{0:T(512)S(1)} %bitcast.232, f32[512]{0:T(512)S(1)} %bitcast.234, ...), kind=kLoop, calls=%fused_computation.87 | loop fusion | flops 35651072 | bytes 13676544 | tf_op jit(solution)/shard_map/reduce_sum | solution.py:163
  211.9 2.3 copy.100
  218.1 2.4 copy.144
  222.0 3.1 fusion.49
  225.9 1.8 copy.168
  227.8 3.0 copy.104
  230.7 7.5 %fusion.12 = (f32[512]{0:T(512)S(1)}, f32[512]{0:T(512)S(1)}, f32[512]{0:T(512)S(1)}, f32[512]{0:T(512)S(1)}, f32[512]{0:T(512)S(1)}, /*index=5*/f32[512]{0:T(51...) fusion(bf16[1024,512]{1,0:T(8,128)(2,1)} %bitcast.188, bf16[1,8,128,512]{3,2,1,0:T(8,128)(2,1)} %copy.94, ...), kind=kLoop, calls=%fused_computation.58 | loop fusion | flops 14152192 | bytes 12599296 | tf_op jit(solution)/shard_map/reduce_sum | solution.py:142
  239.9 8.0 %reduce.4 = bf16[1024,512]{1,0:T(8,128)(2,1)} reduce(bf16[1024,1,512]{2,1,0:T(2,128)(2,1)S(1)} %bitcast.206, bf16[]{:T(256)} %broadcast.38), dimensions={1}, to_apply=%bitcast.181.reduce_sub_computation | reduce | bytes 2097154
  247.9 2.6 reshape.119
  250.6 5.6 %all-to-all-start.3 = ((bf16[8,2,32768]{2,1,0:T(2,128)(2,1)}), bf16[8,2,32768]{2,1,0:T(2,128)(2,1)}, u32[]{:S(2)}, u32[]{:S(2)}) async-start(bf16[8,2,32768]{2,1,0:T(2,128)(2,1)} %reshape.119), calls=%async_computation.3 | async-start | bytes 2097152 | tf_op jit(solution)/shard_map/all_to_all | solution.py:202
  256.1 1.9 broadcast_in_dim.39
  258.1 7.1 %reshape.104 = bf16[32,49024]{1,0:T(8,128)(2,1)} reshape(bf16[32,128,383]{2,1,0:T(8,128)(2,1)} %broadcast_in_dim.39) | data formatting | bytes 6275072 | tf_op jit(solution)/shard_map/reshape | solution.py:21
  265.2 4.4 slice.347
  269.6 10.1 %reshape.105 = bf16[32,128,382]{2,1,0:T(8,128)(2,1)} reshape(bf16[32,48896]{1,0:T(8,128)(2,1)} %slice.347) | data formatting | bytes 6258688 | tf_op jit(solution)/shard_map/reshape | solution.py:22
  281.5 3.0 copy.171
  284.5 8.1 %reduce.5 = bf16[1024,512]{1,0:T(8,128)(2,1)S(1)} reduce(bf16[1024,1,512]{2,1,0:T(2,128)(2,1)} %bitcast.207, bf16[]{:T(256)} %broadcast.38), dimensions={1}, to_apply=%bitcast.180.reduce_sub_computation | reduce | bytes 2097154
  299.4 2.3 copy.145
  301.6 2.4 concatenate.59
  304.1 5.2 all-to-all-start.5
  309.3 2.6 fusion.50
  312.8 1.9 copy.167
  314.7 3.0 copy.117
  317.7 6.1 %fusion.38 = (f32[512]{0:T(512)S(1)}, f32[512]{0:T(512)S(1)}, f32[512]{0:T(512)S(1)}, f32[512]{0:T(512)S(1)}, f32[512]{0:T(512)S(1)}, /*index=5*/f32[512]{0:T(51...) fusion(bf16[1024,512]{1,0:T(8,128)(2,1)S(1)} %bitcast.184, ...), kind=kLoop, calls=%fused_computation.84 | loop fusion | flops 24634368 | bytes 15759360 | tf_op jit(solution)/shard_map/reduce_sum | solution.py:152
  323.8 4.4 fusion.57
  329.9 7.0 %reduce.6 = bf16[1024,512]{1,0:T(8,128)(2,1)S(1)} reduce(bf16[1024,1,512]{2,1,0:T(2,128)(2,1)S(1)} %bitcast.210, bf16[]{:T(256)} %broadcast.38), dimensions={1}, to_apply=%bitcast.179.reduce_sub_computation | reduce | bytes 2097154
  338.5 5.3 %all-to-all-start.6 = ((bf16[8,2,32768]{2,1,0:T(2,128)(2,1)}), bf16[8,2,32768]{2,1,0:T(2,128)(2,1)S(1)}, u32[]{:S(2)}, u32[]{:S(2)}) async-start(bf16[8,2,32768]{2,1,0:T(2,128)(2,1)} %reshape.125), calls=%async_computation.6 | async-start | bytes 2097152 | tf_op jit(solution)/shard_map/all_to_all | solution.py:204
  343.9 2.8 copy.169
  346.7 8.0 %reduce.7 = bf16[1024,512]{1,0:T(8,128)(2,1)} reduce(bf16[1024,1,512]{2,1,0:T(2,128)(2,1)S(1)} %bitcast.203, bf16[]{:T(256)} %broadcast.38), dimensions={1}, to_apply=%bitcast.178.reduce_sub_computation | reduce | bytes 2097154
  354.7 2.8 reshape.127
  357.6 12.8 %all-to-all-done.6 = bf16[8,2,32768]{2,1,0:T(2,128)(2,1)S(1)} async-done(((bf16[8,2,32768]{2,1,0:T(2,128)(2,1)}), bf16[8,2,32768]{2,1,0:T(2,128)(2,1)S(1)}, u32[]{:S(2)}, u32[]{:S(2)}) %all-to-all-start.6) | async-done | bytes 1048608 | tf_op jit(solution)/shard_map/all_to_all | solution.py:204
  370.4 4.2 all-to-all-start.7
  376.1 2.9 convolution_bitcast_fusion
  379.0 5.5 %reshape.106 = f32[32,32640]{1,0:T(8,128)} reshape(f32[32,128,255]{2,1,0:T(8,128)} %convolution_bitcast_fusion) | data formatting | bytes 8355840 | tf_op jit(solution)/shard_map/reshape | solution.py:46
  384.5 2.5 concatenate.65
  389.6 40.7 %psum.23 = f32[4096]{0:T(1024)} all-reduce(f32[4096]{0:T(1024)S(1)} %multiply_dynamic-update-slice_fusion.2), channel_id=1, replica_groups=mesh['dp'=4,'ctx'=8] {'dp','ctx'}, use_global_device_ids=true, to_apply=%region_25.0 | all-reduce | flops 4096 | bytes 32768 | tf_op jit(solution)/shard_map/psum | solution.py:216
  430.3 4.3 reshape.120
  438.8 4.3 reshape.124
  450.6 4.3 reshape.128
  457.2 62.0 %all-reduce.12.cloned.1.call-done = (f32[7,3,4096]{2,0,1:T(8,128)}, f32[256,128]{1,0:T(8,128)}) async-done(((f32[7,3,4096]{2,0,1:T(8,128)}, f32[256,128]{1,0:T(8,128)}), (f32[7,3,4096]{2,0,1:T(8,128)}, f32[256,128]{1,0:T(8,128)})) %all-reduce.12.cloned.1.call-update) | async-done | bytes 475152 | tf_op jit(solution)/shard_map/psum | solution.py:216
  (116 shorter events, 51.6 us)
Async XLA Ops:
  7.2 141.2 %copy-start = (f32[256,128]{1,0:T(8,128)S(1)}, f32[256,128]{1,0:T(8,128)}, u32[]{:S(2)}) copy-start(f32[256,128]{1,0:T(8,128)} %param.12) | copy-start | bytes 393220
  36.3 36.9 %all-to-all-start = ((bf16[8,2,32768]{2,1,0:T(2,128)(2,1)}), bf16[8,2,32768]{2,1,0:T(2,128)(2,1)S(1)}, u32[]{:S(2)}, u32[]{:S(2)}) async-start(bf16[8,2,32768]{2,1,0:T(2,128)(2,1)} %reshape.113), calls=%async_computation | async-start | bytes 2097152 | tf_op jit(solution)/shard_map/all_to_all | solution.py:175
  73.1 10.4 %copy-start.8 = (bf16[8,2,32768]{2,1,0:T(2,128)(2,1)}, bf16[8,2,32768]{2,1,0:T(2,128)(2,1)S(1)}, u32[]{:S(2)}) copy-start(bf16[8,2,32768]{2,1,0:T(2,128)(2,1)S(1)} %all-to-all-done) | copy-start | bytes 3145732
  73.1 33.9 %all-to-all-start.4 = ((bf16[8,2,32768]{2,1,0:T(2,128)(2,1)}), bf16[8,2,32768]{2,1,0:T(2,128)(2,1)}, u32[]{:S(2)}, u32[]{:S(2)}) async-start(bf16[8,2,32768]{2,1,0:T(2,128)(2,1)} %reshape.121), calls=%async_computation.4 | async-start | bytes 2097152 | tf_op jit(solution)/shard_map/all_to_all | solution.py:178
  107.1 35.6 %all-to-all-start.2 = ((bf16[8,2,32768]{2,1,0:T(2,128)(2,1)}), bf16[8,2,32768]{2,1,0:T(2,128)(2,1)S(1)}, u32[]{:S(2)}, u32[]{:S(2)}) async-start(bf16[8,2,32768]{2,1,0:T(2,128)(2,1)} %reshape.117), calls=%async_computation.2 | async-start | bytes 2097152 | tf_op jit(solution)/shard_map/all_to_all | solution.py:177
  142.7 5.9 %copy-start.9 = (bf16[8,2,32768]{2,1,0:T(2,128)(2,1)}, bf16[8,2,32768]{2,1,0:T(2,128)(2,1)S(1)}, u32[]{:S(2)}) copy-start(bf16[8,2,32768]{2,1,0:T(2,128)(2,1)S(1)} %all-to-all-done.2) | copy-start | bytes 3145732
  142.7 46.2 %all-to-all-start.1 = ((bf16[8,2,32768]{2,1,0:T(2,128)(2,1)}), bf16[8,2,32768]{2,1,0:T(2,128)(2,1)}, u32[]{:S(2)}, u32[]{:S(2)}) async-start(bf16[8,2,32768]{2,1,0:T(2,128)(2,1)} %reshape.115), calls=%async_computation.1 | async-start | bytes 2097152 | tf_op jit(solution)/shard_map/all_to_all | solution.py:176
  179.2 2.0 copy-start.10
  214.2 2.8 copy-start.4
  222.0 3.1 copy-start.12
  250.6 53.5 %all-to-all-start.3 = ((bf16[8,2,32768]{2,1,0:T(2,128)(2,1)}), bf16[8,2,32768]{2,1,0:T(2,128)(2,1)}, u32[]{:S(2)}, u32[]{:S(2)}) async-start(bf16[8,2,32768]{2,1,0:T(2,128)(2,1)} %reshape.119), calls=%async_computation.3 | async-start | bytes 2097152 | tf_op jit(solution)/shard_map/all_to_all | solution.py:202
  269.6 10.1 %copy-start.7 = (f32[1024,512]{1,0:T(8,128)S(1)}, f32[1024,512]{1,0:T(8,128)}, u32[]{:S(2)}) copy-start(f32[1024,512]{1,0:T(8,128)} %get-tuple-element.57) | copy-start | bytes 6291460
  284.5 9.7 %copy-start.3 = (bf16[1024,512]{1,0:T(8,128)(2,1)S(1)}, bf16[1024,512]{1,0:T(8,128)(2,1)}, u32[]{:S(2)}) copy-start(bf16[1024,512]{1,0:T(8,128)(2,1)} %get-tuple-element.52) | copy-start | bytes 3145732
  297.0 4.6 copy-start.5
  304.1 5.2 copy-start.15
  304.1 34.5 %all-to-all-start.5 = ((bf16[8,2,32768]{2,1,0:T(2,128)(2,1)}), bf16[8,2,32768]{2,1,0:T(2,128)(2,1)}, u32[]{:S(2)}, u32[]{:S(2)}) async-start(bf16[8,2,32768]{2,1,0:T(2,128)(2,1)} %reshape.123), calls=%async_computation.5 | async-start | bytes 2097152 | tf_op jit(solution)/shard_map/all_to_all | solution.py:203
  314.7 3.0 copy-start.2
  338.5 31.9 %all-to-all-start.6 = ((bf16[8,2,32768]{2,1,0:T(2,128)(2,1)}), bf16[8,2,32768]{2,1,0:T(2,128)(2,1)S(1)}, u32[]{:S(2)}, u32[]{:S(2)}) async-start(bf16[8,2,32768]{2,1,0:T(2,128)(2,1)} %reshape.125), calls=%async_computation.6 | async-start | bytes 2097152 | tf_op jit(solution)/shard_map/all_to_all | solution.py:204
  354.7 20.2 %copy-start.11 = (bf16[8,128,32,16]{1,3,0,2:T(8,128)(2,1)S(1)}, bf16[8,128,32,16]{1,3,0,2:T(8,128)(2,1)}, u32[]{:S(2)}) copy-start(bf16[8,128,32,16]{1,3,0,2:T(8,128)(2,1)} %copy.102) | copy-start | bytes 3145732
  354.7 20.2 %copy-start.13 = (bf16[8,127,512]{1,2,0:T(8,128)(2,1)S(1)}, bf16[8,127,512]{1,2,0:T(8,128)(2,1)}, u32[]{:S(2)}) copy-start(bf16[8,127,512]{1,2,0:T(8,128)(2,1)} %copy-done.12) | copy-start | bytes 3121156
  370.4 80.2 %all-to-all-start.7 = ((bf16[8,2,32768]{2,1,0:T(2,128)(2,1)}), bf16[8,2,32768]{2,1,0:T(2,128)(2,1)}, u32[]{:S(2)}, u32[]{:S(2)}) async-start(bf16[8,2,32768]{2,1,0:T(2,128)(2,1)} %reshape.127), calls=%async_computation.7 | async-start | bytes 2097152 | tf_op jit(solution)/shard_map/all_to_all | solution.py:205
  374.7 144.5 %all-reduce.12.cloned.1.call-start = ((), (), s32[]{:S(2)}) async-start(), calls=%async_computation.8 | async-start | bytes 1048576 | tf_op jit(solution)/shard_map/psum | solution.py:216
  374.9 1.2 copy-start.6
  388.6 0.7 copy-start.16
  388.7 0.7 copy-start.14
  455.2 67.4 %copy-start.1 = (f32[256,128]{1,0:T(8,128)S(1)}, f32[256,128]{1,0:T(8,128)}, u32[]{:S(2)}) copy-start(f32[256,128]{1,0:T(8,128)} %param.12) | copy-start | bytes 393220
Sparse Core Ops, SparseCore 0:
  389.6 129.5 all-reduce.11
where the time goes:
time: 540 us; the launch traced here: 530 us
  local copies, waits for them, and re-layouts  190 us (35%)
  other arithmetic  158 us (29%)
  waiting for transfers between devices  74.9 us (14%)
  starting transfers between devices  42.8 us (8%)
  blocking collectives  40.7 us (8%)
  between operations  15.2 us (3%)
  matrix products  8.59 us (2%)
    unnamed x8, other arithmetic  123 us
    unnamed x75, local copies, waits for them, and re-layouts  98.6 us
    psum x1, waiting for transfers between devices, body(): summed = lax.psum((grad_feat, grad_filter, grad_skip), ('dp', 'ctx'))  62 us
    psum x1, blocking collectives, body(): summed = lax.psum((grad_feat, grad_filter, grad_skip), ('dp', 'ctx'))  40.7 us
    reshape x2, local copies, waits for them, and re-layouts, toeplitz(): flattened[:, block_len - 1:block_len - 1 + block_len * (line_len - 1)]  19.2 us
    all_to_all x1, waiting for transfers between devices, body(): lax.all_to_all(results[2][None], 'ctx', split_axis=1, concat_axis=2, tile...  12.8 us
    reduce_sum x1, other arithmetic, mixer_core(): jnp.sum(mix_in.astype(jnp.float32) * grad_filtered.astype(jnp.float32), a...  12.2 us
    reshape x2, local copies, waits for them, and re-layouts, toeplitz(): flattened = jnp.broadcast_to(padded_line[:, None, :], (group_count, block...  11.8 us
  transfers between devices with their start and end apart: 9, of which 2 were waited for; matrix products, arithmetic and copies ran while one was open for 49% of the time, Pallas kernels for 0%

commit v1 on v0

v1 whole, which is shorter than its diff:
```python
import functools

import jax
import jax.numpy as jnp
from jax import lax
from jax.experimental import pallas as pl
from jax.experimental.pallas import tpu as pltpu
from jax.sharding import PartitionSpec as P

LANES = 128
HALO = 8
VMEM = 56 * 1024 * 1024


def params():
    return pltpu.CompilerParams(
        dimension_semantics=("arbitrary",), vmem_limit_bytes=VMEM
    )


def cols(tile):
    return pl.ds(pl.multiple_of(tile * LANES, LANES), LANES)


def diagonals(square):
    height = square.shape[0]
    total = square[:8]
    for first in range(8, height, 8):
        total = total + pltpu.roll(square[first:first + 8], LANES - first, 1)
    sub = lax.broadcasted_iota(jnp.int32, total.shape, 0)
    for bit in (1, 2, 4):
        total = jnp.where((sub & bit) > 0, pltpu.roll(total, LANES - bit, 1), total)
    return jnp.sum(total, axis=0, keepdims=True)


def feat_kernel(rows, taps_count, tiles, q_ref, k_ref, v_ref, cot_ref, tail_ref, taps_ref,
                mix_ref, gf_ref, qf_ref, kf_ref, vf_ref, ext):
    def one(tile, carry):
        lanes = cols(tile)
        tails = tail_ref[:, lanes].astype(jnp.float32)
        feats = []
        for which, src in enumerate((q_ref, k_ref, v_ref)):
            ext[which, pl.ds(0, HALO), :] = tails[which * HALO:(which + 1) * HALO]
            ext[which, pl.ds(HALO, rows), :] = src[:, lanes].astype(jnp.float32)
            total = None
            for lag in range(taps_count):
                weight = taps_ref[pl.ds(lag * 3 + which, 1), lanes]
                term = weight * ext[which, pl.ds(HALO - lag, rows), :]
                total = term if total is None else total + term
            feats.append(total)
        qf_ref[:, lanes] = feats[0]
        kf_ref[:, lanes] = feats[1]
        vf_ref[:, lanes] = feats[2]
        mix_ref[:, lanes] = (feats[1] * feats[2]).astype(jnp.bfloat16)
        gf_ref[:, lanes] = (cot_ref[:, lanes].astype(jnp.float32) * feats[0]).astype(jnp.bfloat16)
        return carry

    lax.fori_loop(0, tiles, one, 0)


def mix_kernel(rows, taps_count, tiles, per_group, place_ref, q_ref, k_ref, v_ref, cot_ref, tail_ref,
               mix_ref, gf_ref, qf_ref, kf_ref, vf_ref, prev_ref, next_ref, rev_ref, fwd_ref, gain_ref,
               out_ref, gq_ref, gk_ref, gv_ref, head_ref, grad_ref, ext, part):
    half = rows // 2
    groups = LANES // per_group
    f32, bf16 = jnp.float32, jnp.bfloat16
    row_id = lax.broadcasted_iota(jnp.int32, (half, LANES), 0)
    lane_id = lax.broadcasted_iota(jnp.int32, (half, LANES), 1)
    wide_group = lax.broadcasted_iota(jnp.int32, (half, 2 * LANES), 1) % LANES // per_group
    later = lane_id > row_id
    zero = jnp.zeros((half, LANES), f32)

    def one(tile, carry):
        lanes = cols(tile)
        mix = mix_ref[:, lanes]
        prev = prev_ref[:, lanes]
        gf = gf_ref[:, lanes]
        nxt = next_ref[:, lanes]
        before = jnp.concatenate([
            jnp.concatenate([prev, mix], axis=0),
            jnp.concatenate([prev[half:], mix, mix[:half]], axis=0)], axis=1)
        after = jnp.concatenate([
            jnp.concatenate([gf, nxt], axis=0),
            jnp.concatenate([gf[half:], nxt, nxt[:half]], axis=0)], axis=1)
        gf_wide = jnp.concatenate([gf[:half], gf[half:]], axis=1)
        first = pl.multiple_of(tile * groups, groups)
        rev = rev_ref[pl.ds(first, groups), :]
        fwd = fwd_ref[pl.ds(first, groups), :]
        conv = None
        back = None
        for group in range(groups):
            mine = wide_group == group
            circ = pltpu.roll(jnp.broadcast_to(rev[group:group + 1], (half, LANES)), 0, 1,
                              stride=1, stride_axis=0)
            matrix = jnp.concatenate([jnp.where(later, circ, zero), jnp.where(later, zero, circ)],
                                     axis=1).astype(bf16)
            found = jnp.dot(matrix, before, preferred_element_type=f32)
            conv = found if conv is None else jnp.where(mine, found, conv)
            circ = pltpu.roll(jnp.broadcast_to(fwd[group:group + 1], (half, LANES)), 0, 1,
                              stride=1, stride_axis=0)
            early = lane_id < row_id
            matrix = jnp.concatenate([jnp.where(early, zero, circ), jnp.where(early, circ, zero)],
                                     axis=1).astype(bf16)
            found = jnp.dot(matrix, after, preferred_element_type=f32)
            back = found if back is None else jnp.where(mine, found, back)
            masked = jnp.where(mine, gf_wide, jnp.zeros_like(gf_wide))
            prod = lax.dot_general(masked, before, (((1,), (1,)), ((), ())),
                                   preferred_element_type=f32)
            folded = jnp.where(later, prod[:, :LANES], prod[:, LANES:])
            part[pl.ds(24 + group, 1), :] = diagonals(folded)
        gain = gain_ref[:, lanes]
        mix_wide = mix.astype(f32)
        gf_f32 = gf.astype(f32)
        filtered = jnp.concatenate([conv[:, :LANES], conv[:, LANES:]], axis=0) + gain * mix_wide
        grad_mix = jnp.concatenate([back[:, :LANES], back[:, LANES:]], axis=0) + gain * gf_f32
        part[pl.ds(21, 1), :] = jnp.sum(mix_wide * gf_f32, axis=0, keepdims=True)
        part[pl.ds(22, 2), :] = jnp.zeros((2, LANES), f32)
        out_ref[:, lanes] = (qf_ref[:, lanes] * filtered).astype(bf16)
        grads = (cot_ref[:, lanes].astype(f32) * filtered, grad_mix * vf_ref[:, lanes],
                 grad_mix * kf_ref[:, lanes])
        tails = tail_ref[:, lanes].astype(f32)
        for which, (src, grad, dest) in enumerate(zip((q_ref, k_ref, v_ref), grads, (gq_ref, gk_ref, gv_ref))):
            dest[:, lanes] = grad
            ext[which, pl.ds(0, HALO), :] = tails[which * HALO:(which + 1) * HALO]
            ext[which, pl.ds(HALO, rows), :] = src[:, lanes].astype(f32)
            for lag in range(taps_count):
                part[pl.ds(lag * 3 + which, 1), :] = jnp.sum(
                    grad * ext[which, pl.ds(HALO - lag, rows), :], axis=0, keepdims=True)
        head_ref[:, lanes] = jnp.concatenate([grad[:HALO] for grad in grads], axis=0).astype(bf16)
        grad_ref[tile] = part[...].astype(bf16)
        return carry

    lax.fori_loop(0, tiles, one, 0)


def back_kernel(rows, taps_count, tiles, gq_ref, gk_ref, gv_ref, head_ref, taps_ref, dq_ref, dk_ref, dv_ref, ext):
    def one(tile, carry):
        lanes = cols(tile)
        heads = head_ref[:, lanes].astype(jnp.float32)
        for which, (src, dest) in enumerate(((gq_ref, dq_ref), (gk_ref, dk_ref), (gv_ref, dv_ref))):
            ext[which, pl.ds(0, rows), :] = src[:, lanes]
            ext[which, pl.ds(rows, HALO), :] = heads[which * HALO:(which + 1) * HALO]
            total = None
            for lag in range(taps_count):
                weight = taps_ref[pl.ds(lag * 3 + which, 1), lanes]
                term = weight * ext[which, pl.ds(lag, rows), :]
                total = term if total is None else total + term
            dest[:, lanes] = total.astype(jnp.bfloat16)
        return carry

    lax.fori_loop(0, tiles, one, 0)


def unpack_kernel(taps_count, scale, count, place_ref, grad_ref, taps_ref, filt_ref, skip_ref):
    groups = filt_ref.shape[0] // count
    for tile in range(count):
        block = grad_ref[place_ref[tile]].astype(jnp.float32) * scale
        lanes = pl.ds(tile * LANES, LANES)
        for lag in range(taps_count):
            taps_ref[lag, :, lanes] = block[lag * 3:lag * 3 + 3]
        skip_ref[:, lanes] = block[21:22]
        filt_ref[pl.ds(tile * groups, groups), :] = block[24:24 + groups]


def swaps(size, mask):
    return [(i, i ^ mask) for i in range(size)]


def reduce_all(share, ctx_count, dp_count):
    f32, bf16 = jnp.float32, jnp.bfloat16
    half = share[0].astype(f32) + lax.ppermute(share[1], "ctx", swaps(ctx_count, 1)).astype(f32)
    sent = half.astype(bf16)
    mine = half[0]
    for mask in range(1, dp_count):
        mine = mine + lax.ppermute(sent[mask], "dp", swaps(dp_count, mask)).astype(f32)
    mask = 2
    while mask < ctx_count:
        low = mine.astype(bf16)
        if mask * 2 < ctx_count:
            picks = (mask, 2 * mask, 3 * mask)
            mask *= 4
        else:
            picks = (mask,)
            mask *= 2
        for pick in picks:
            mine = mine + lax.ppermute(low, "ctx", swaps(ctx_count, pick)).astype(f32)
    low = mine.astype(bf16)
    quarter = [low]
    for mask in range(1, dp_count):
        quarter.append(lax.ppermute(low, "dp", swaps(dp_count, mask)))
    whole = jnp.stack(quarter)
    return jnp.stack([whole, lax.ppermute(whole, "ctx", swaps(ctx_count, 1))])


def body(query_rows, key_rows, value_rows, cotangent, feature_taps, filter_taps, skip_gain):
    f32, bf16 = jnp.float32, jnp.bfloat16
    rows, channels = query_rows.shape[1:]
    taps_count = feature_taps.shape[0]
    group_count, taps_len = filter_taps.shape
    per_group = channels // group_count
    ctx_count, dp_count = lax.axis_size("ctx"), lax.axis_size("dp")
    assert rows == taps_len == LANES and taps_count <= HALO
    scale = float(dp_count * ctx_count * rows) ** (-0.5)
    count = channels // LANES
    tiles = 4
    steps = count // tiles
    wide = tiles * LANES
    query, key, value, cot = query_rows[0], key_rows[0], value_rows[0], cotangent[0]
    onward = [(i, i + 1) for i in range(ctx_count - 1)]
    backward = [(i + 1, i) for i in range(ctx_count - 1)]

    taps = feature_taps.reshape(taps_count * 3, channels)
    gains = skip_gain.reshape(1, channels)
    fwd = filter_taps.astype(bf16).astype(f32)
    rev = jnp.roll(fwd[:, ::-1], 1, axis=1)

    tails = lax.ppermute(
        jnp.concatenate([query[rows - HALO:], key[rows - HALO:], value[rows - HALO:]], axis=0), "ctx", onward)

    def block(height):
        return pl.BlockSpec((height, wide), lambda step, *_: (0, step))

    def shape(height, kind):
        return jax.ShapeDtypeStruct((height, channels), kind)

    mix, gf, qf, kf, vf = pl.pallas_call(
        functools.partial(feat_kernel, rows, taps_count, tiles),
        grid=(steps,),
        in_specs=[block(rows)] * 4 + [block(3 * HALO), block(3 * taps_count)],
        out_specs=[block(rows)] * 5,
        out_shape=[shape(rows, bf16)] * 2 + [shape(rows, f32)] * 3,
        scratch_shapes=[pltpu.VMEM((3, rows + HALO, LANES), f32)],
        compiler_params=params(),
        name="features",
    )(query, key, value, cot, tails, taps)

    prev = lax.ppermute(mix, "ctx", onward)
    following = lax.ppermute(gf, "ctx", backward)

    tile_of = jnp.arange(count, dtype=jnp.int32)
    in_half = count // 2
    in_quarter = in_half // dp_count
    core = lax.rem(lax.axis_index("ctx"), 2)
    place = (((tile_of // in_half) ^ core) * in_half
             + ((tile_of % in_half // in_quarter) ^ lax.axis_index("dp")) * in_quarter
             + tile_of % in_quarter).astype(jnp.int32)
    blocks_in_quarter = in_quarter // tiles
    filter_block = pl.BlockSpec((group_count // steps, taps_len), lambda step, *_: (step, 0))
    out, gq, gk, gv, heads, share = pl.pallas_call(
        functools.partial(mix_kernel, rows, taps_count, tiles, per_group),
        grid_spec=pltpu.PrefetchScalarGridSpec(
            num_scalar_prefetch=1,
            grid=(steps,),
            in_specs=[block(rows)] * 4 + [block(3 * HALO)] + [block(rows)] * 7
            + [filter_block, filter_block, block(1)],
            out_specs=[block(rows)] * 4 + [block(3 * HALO)]
            + [pl.BlockSpec((tiles, 32, LANES), lambda step, where: (where[step * tiles] // tiles, 0, 0))],
            scratch_shapes=[pltpu.VMEM((3, rows + HALO, LANES), f32), pltpu.VMEM((32, LANES), f32)],
        ),
        out_shape=[shape(rows, bf16)] + [shape(rows, f32)] * 3 + [shape(3 * HALO, bf16)]
        + [jax.ShapeDtypeStruct((count, 32, LANES), bf16)],
        compiler_params=params(),
        name="filters",
    )(place, query, key, value, cot, tails, mix, gf, qf, kf, vf, prev, following, rev, fwd, gains)

    next_heads = lax.ppermute(heads, "ctx", backward)
    total = reduce_all(share.reshape(2, dp_count, in_quarter, 32, LANES), ctx_count, dp_count)

    dq, dk, dv = pl.pallas_call(
        functools.partial(back_kernel, rows, taps_count, tiles),
        grid=(steps,),
        in_specs=[block(rows)] * 3 + [block(3 * HALO), block(3 * taps_count)],
        out_specs=[block(rows)] * 3,
        out_shape=[shape(rows, bf16)] * 3,
        scratch_shapes=[pltpu.VMEM((3, rows + HALO, LANES), f32)],
        compiler_params=params(),
        name="features_back",
    )(gq, gk, gv, next_heads, taps)

    whole = pl.BlockSpec(memory_space=pltpu.VMEM)
    grad_taps, grad_filter, grad_skip = pl.pallas_call(
        functools.partial(unpack_kernel, taps_count, scale, count),
        in_specs=[pl.BlockSpec(memory_space=pltpu.SMEM), whole],
        out_specs=[whole] * 3,
        out_shape=[jax.ShapeDtypeStruct(feature_taps.shape, f32), jax.ShapeDtypeStruct(filter_taps.shape, f32),
                   jax.ShapeDtypeStruct((1, channels), f32)],
        compiler_params=pltpu.CompilerParams(vmem_limit_bytes=VMEM),
        name="unpack",
    )(place, total.reshape(count, 32, LANES))
    grad_filter = jnp.roll(grad_filter[:, ::-1], 1, axis=1)
    return (out[None], dq[None], dk[None], dv[None], grad_taps, grad_filter, grad_skip.reshape(channels))


def solution(mesh):
    rows = P("dp", "ctx", None)
    return jax.shard_map(
        body,
        mesh=mesh,
        in_specs=(rows, rows, rows, rows, P(), P(), P()),
        out_specs=(rows, rows, rows, rows, P(), P(), P()),
        check_vma=False,
    )
```

time: 540 us -> 127 us (0.24)
  the two profiles are of different devices: /device:TPU:0 before, /device:TPU:1 now
where the time goes in v1:
time: 127 us; the launch traced here: 126 us
  Pallas kernels  61.6 us (49%)
  starting transfers between devices  27.8 us (22%)
  waiting for transfers between devices  21.7 us (17%)
  local copies, waits for them, and re-layouts  10.7 us (8%)
  other arithmetic  3.91 us (3%)
    pallas_call x1, Pallas kernels, body(): pl.pallas_call(functools.partial(mix_kernel, rows, taps_count, tiles, per...  41.5 us
    pallas_call x1, Pallas kernels, body(): pl.pallas_call(functools.partial(feat_kernel, rows, taps_count, tiles), g...  9.85 us
    ppermute x1, waiting for transfers between devices, body(): prev = lax.ppermute(mix, 'ctx', onward)  8.42 us
    pallas_call x1, Pallas kernels, body(): pl.pallas_call(functools.partial(back_kernel, rows, taps_count, tiles), g...  8.41 us
    ppermute x1, starting transfers between devices, body(): next_heads = lax.ppermute(heads, 'ctx', backward)  6.28 us
    unnamed x14, local copies, waits for them, and re-layouts  5.58 us
    ppermute x1, starting transfers between devices, body(): lax.ppermute(jnp.concatenate([query[rows - HALO:], key[rows - HALO:], val...  4.59 us
    ppermute x1, starting transfers between devices, body(): prev = lax.ppermute(mix, 'ctx', onward)  4.38 us
  transfers between devices with their start and end apart: 15, of which 11 were waited for; matrix products, arithmetic and copies ran while one was open for 3% of the time, Pallas kernels for 7%

profile of v1, /device:TPU:1, one launch (start us, length us, event | category | flops | bytes accessed | tf_op | source)
XLA Modules:
  0.0 126.5 jit_solution(7586319359236861976)
XLA Ops:
  0.6 0.8 slice_bitcast_fusion.3
  1.5 0.9 slice_bitcast_fusion.1
  2.4 4.6 %collective-permute-start = (bf16[24,4096]{1,0:T(8,128)(2,1)S(1)}, bf16[24,4096]{1,0:T(8,128)(2,1)S(1)}, u32[]{:S(2)}, u32[]{:S(2)}) collective-permute-start(bf16[24,4096]{1,0:T(8,128)(2,1)S(1)} %pad_maximum_fusion.1), channel_id=1, source_target_pairs={{0,1},{1,2},{2,3},{3,4},{4,5},{5,6},{6,7},{8,9},{9,10},{10,11},{11... | collective-permute-start | bytes 589832 | tf_op jit(solution)/shard_map/ppermute | solution.py:217
  7.0 1.2 copy.16
  8.2 0.9 reshape.36.taps_ref
  9.1 0.4 collective-permute-done.tail_ref
  9.6 0.0 copy-start.3
  9.6 0.7 copy-done.3
  10.3 0.0 copy-start.5
  10.3 9.9 %features.1 = (bf16[128,4096]{1,0:T(8,128)(2,1)}, bf16[128,4096]{1,0:T(8,128)(2,1)}, f32[128,4096]{1,0:T(8,128)}, f32[128,4096]{1,0:T(8,128)}, f32[128,4096]{1,0:T(8,128)}) custom-call(bf16[128,4096]{1,0:T(8,128)(2,1)} %bitcast.47, bf16[128,4096]{1,0:T(8,128)(2,1)} %bitcast.49, bf16[128,4096]{1,0:T(8,128)(2,1)} %bitcast.51, bf16[128,4096]{1,0:T(8,128)(2,1)} %bitcast.53, ...), custom_call_target="tpu_custom_call" | custom-call | tf_op jit(solution)/shard_map/features/pallas_call | solution.py:226
  20.1 4.4 %collective-permute-start.1 = (bf16[128,4096]{1,0:T(8,128)(2,1)}, bf16[128,4096]{1,0:T(8,128)(2,1)S(1)}, u32[]{:S(2)}, u32[]{:S(2)}) collective-permute-start(bf16[128,4096]{1,0:T(8,128)(2,1)} %get-tuple-element.24.mix_ref), channel_id=1, source_target_pairs={{0,1},{1,2},{2,3},{3,4},{4,5},{5,6},{6,7},{8,9},{9,10},{10,11},{11... | collective-permute-start | bytes 3145736 | tf_op jit(solution)/shard_map/ppermute | solution.py:237
  24.5 1.9 %collective-permute-start.2 = (bf16[128,4096]{1,0:T(8,128)(2,1)}, bf16[128,4096]{1,0:T(8,128)(2,1)S(1)}, u32[]{:S(2)}, u32[]{:S(2)}) collective-permute-start(bf16[128,4096]{1,0:T(8,128)(2,1)} %get-tuple-element.25.gf_ref), channel_id=1, source_target_pairs={{1,0},{2,1},{3,2},{4,3},{5,4},{6,5},{7,6},{9,8},{10,9},{11,10},{12... | collective-permute-start | bytes 3145736 | tf_op jit(solution)/shard_map/ppermute | solution.py:238
  26.4 0.0 copy-done.5
  26.5 0.0 copy-start
  26.5 0.1 slice.79
  26.6 0.2 slice.68
  26.7 0.6 fusion.4.place_ref
  27.4 0.8 pad_maximum_fusion.2.rev_ref
  28.1 8.4 %collective-permute-done.1.prev_ref = bf16[128,4096]{1,0:T(8,128)(2,1)S(1)} collective-permute-done((bf16[128,4096]{1,0:T(8,128)(2,1)}, bf16[128,4096]{1,0:T(8,128)(2,1)S(1)}, u32[]{:S(2)}, u32[]{:S(2)}) %collective-permute-start.1) | collective-permute-done | bytes 1048608 | tf_op jit(solution)/shard_map/ppermute | solution.py:237
  36.5 0.0 copy-start.1
  36.5 4.3 %collective-permute-done.2.next_ref = bf16[128,4096]{1,0:T(8,128)(2,1)S(1)} collective-permute-done((bf16[128,4096]{1,0:T(8,128)(2,1)}, bf16[128,4096]{1,0:T(8,128)(2,1)S(1)}, u32[]{:S(2)}, u32[]{:S(2)}) %collective-permute-start.2) | collective-permute-done | bytes 1048608 | tf_op jit(solution)/shard_map/ppermute | solution.py:238
  40.8 0.0 copy-start.2
  40.8 0.0 copy-done
  40.8 0.0 copy-done.1
  40.8 1.0 copy-done.2
  41.8 41.5 %filters.1 = (bf16[128,4096]{1,0:T(8,128)(2,1)}, f32[128,4096]{1,0:T(8,128)}, f32[128,4096]{1,0:T(8,128)}, f32[128,4096]{1,0:T(8,128)}, bf16[24,4096]{1,0:T(8,128)(2,1)}, /*index=5*/bf16[32,32,128]{2,1,0:T(8,128)(2,1)}) custom-call(s32[32]{0:T(128)} %fusion.4.place_ref, bf16[128,4096]{1,0:T(8,128)(2,1)} %bitcast.48, bf16[128,4096]{1,0:T(8,128)(2,1)} %bitcast.50, ...), custom_call_target="tpu_custom_call" | custom-call | tf_op jit(solution)/shard_map/filters/pallas_call | solution.py:249
  83.3 1.0 fusion.10
  84.3 0.1 collective-permute-start.4
  84.4 1.3 %collective-permute-done.4 = bf16[4,4,32,128]{3,2,1,0:T(8,128)(2,1)S(1)} collective-permute-done((bf16[4,4,32,128]{3,2,1,0:T(8,128)(2,1)S(1)}, bf16[4,4,32,128]{3,2,1,0:T(8,128)(2,1)S(1)}, u32[]{:S(2)}, u32[]{:S(2)}) %collective-permute-start.4) | collective-permute-done | bytes 131104 | tf_op jit(solution)/shard_map/ppermute | solution.py:171
  85.8 1.3 %collective-permute-start.5 = (bf16[4,32,128]{2,1,0:T(8,128)(2,1)S(1)}, bf16[4,32,128]{2,1,0:T(8,128)(2,1)S(1)}, u32[]{:S(2)}, u32[]{:S(2)}) collective-permute-start(bf16[4,32,128]{2,1,0:T(8,128)(2,1)S(1)} %get-tuple-element.61), channel_id=1, source_target_pairs={{0,8},{8,0},{16,24},{24,16},{1,9},{9,1},{17,25},{25,17},{2,10},{10... | collective-permute-start | bytes 98312 | tf_op jit(solution)/shard_map/ppermute | solution.py:175
  87.0 1.2 collective-permute-start.7
  88.3 0.2 collective-permute-start.6
  88.5 0.1 collective-permute-done.5
  88.6 2.1 %collective-permute-done.7 = bf16[4,32,128]{2,1,0:T(8,128)(2,1)S(1)} collective-permute-done((bf16[4,32,128]{2,1,0:T(8,128)(2,1)S(1)}, bf16[4,32,128]{2,1,0:T(8,128)(2,1)S(1)}, u32[]{:S(2)}, u32[]{:S(2)}) %collective-permute-start.7) | collective-permute-done | bytes 32800 | tf_op jit(solution)/shard_map/ppermute | solution.py:175
  90.7 0.4 collective-permute-done.6
  91.1 1.8 %collective-permute-start.10 = (bf16[4,32,128]{2,1,0:T(8,128)(2,1)S(1)}, bf16[4,32,128]{2,1,0:T(8,128)(2,1)S(1)}, u32[]{:S(2)}, u32[]{:S(2)}) collective-permute-start(bf16[4,32,128]{2,1,0:T(8,128)(2,1)S(1)} %fusion.3), channel_id=1, source_target_pairs={{0,6},{1,7},{2,4},{3,5},{4,2},{5,3},{6,0},{7,1},{8,14},{9,15},{10,... | collective-permute-start | bytes 98312 | tf_op jit(solution)/shard_map/ppermute | solution.py:186
  92.9 0.7 collective-permute-start.9
  93.6 1.1 collective-permute-start.8
  94.7 1.0 collective-permute-done.10
  95.7 1.0 collective-permute-done.9
  96.7 0.1 collective-permute-done.8
  96.8 1.3 %collective-permute-start.13 = (bf16[4,32,128]{2,1,0:T(8,128)(2,1)S(1)}, bf16[4,32,128]{2,1,0:T(8,128)(2,1)S(1)}, u32[]{:S(2)}, u32[]{:S(2)}) collective-permute-start(bf16[4,32,128]{2,1,0:T(8,128)(2,1)S(1)} %add_convert_fusion), channel_id=1, source_target_pairs={{0,24},{8,16},{16,8},{24,0},{1,25},{9,17},{17,9},{25,1},{2,26},{10... | collective-permute-start | bytes 98312 | tf_op jit(solution)/shard_map/ppermute | solution.py:190
  98.1 1.1 collective-permute-start.12
  99.2 0.3 collective-permute-start.11
  99.5 6.3 %collective-permute-start.3 = (bf16[24,4096]{1,0:T(8,128)(2,1)}, bf16[24,4096]{1,0:T(8,128)(2,1)S(1)}, u32[]{:S(2)}, u32[]{:S(2)}) collective-permute-start(bf16[24,4096]{1,0:T(8,128)(2,1)} %get-tuple-element.33), channel_id=1, source_target_pairs={{1,0},{2,1},{3,2},{4,3},{5,4},{6,5},{7,6},{9,8},{10,9},{11,10},{12... | collective-permute-start | bytes 589832 | tf_op jit(solution)/shard_map/ppermute | solution.py:266
  105.8 0.0 collective-permute-done.13
  105.8 0.0 collective-permute-done.12
  105.8 0.0 collective-permute-done.11
  105.8 1.5 %collective-permute-start.14 = (bf16[4,4,32,128]{3,2,1,0:T(8,128)(2,1)S(1)}, bf16[4,4,32,128]{3,2,1,0:T(8,128)(2,1)S(1)}, u32[]{:S(2)}, u32[]{:S(2)}) collective-permute-start(bf16[4,4,32,128]{3,2,1,0:T(8,128)(2,1)S(1)} %get-tuple-element.60), channel_id=1, source_target_pairs={{0,1},{1,0},{2,3},{3,2},{4,5},{5,4},{6,7},{7,6},{8,9},{9,8},{10,11... | collective-permute-start | bytes 393224 | tf_op jit(solution)/shard_map/ppermute | solution.py:192
  107.3 2.6 %collective-permute-done.3.head_ref = bf16[24,4096]{1,0:T(8,128)(2,1)S(1)} collective-permute-done((bf16[24,4096]{1,0:T(8,128)(2,1)}, bf16[24,4096]{1,0:T(8,128)(2,1)S(1)}, u32[]{:S(2)}, u32[]{:S(2)}) %collective-permute-start.3) | collective-permute-done | bytes 196640 | tf_op jit(solution)/shard_map/ppermute | solution.py:266
  109.9 0.0 copy-start.4
  109.9 0.7 copy-done.4
  110.6 8.4 %features_back.1 = (bf16[128,4096]{1,0:T(8,128)(2,1)}, bf16[128,4096]{1,0:T(8,128)(2,1)}, bf16[128,4096]{1,0:T(8,128)(2,1)}) custom-call(f32[128,4096]{1,0:T(8,128)} %get-tuple-element.30.gq_ref, f32[128,4096]{1,0:T(8,128)} %get-tuple-element.31.gk_ref, f32[128,4096]{1,0:T(8,128)} %get-tuple-element.32.gv_ref, bf16[24,4096]{1,0:T(8,128)(2,1)} %copy-done.4, ...), custom_call_target="tpu_custom_call" | custom-call | tf_op jit(solution)/shard_map/features_back/pallas_call | solution.py:269
  119.0 0.0 collective-permute-done.14
  119.0 0.7 pad_maximum_fusion
  119.8 1.9 %unpack.1 = (f32[7,3,4096]{2,1,0:T(4,128)}, f32[256,128]{1,0:T(8,128)}, f32[1,4096]{1,0:T(1,128)}) custom-call(s32[32]{0:T(128)} %fusion.4.place_ref, bf16[32,32,128]{2,1,0:T(8,128)(2,1)} %bitcast.56), custom_call_target="tpu_custom_call" | custom-call | tf_op jit(solution)/shard_map/unpack/pallas_call | solution.py:281
  121.7 2.0 %copy.17 = f32[7,3,4096]{2,0,1:T(8,128)} copy(f32[7,3,4096]{2,1,0:T(4,128)} %get-tuple-element.52) | data formatting | bytes 688128
  123.6 1.0 slice.76
  124.6 0.2 slice.77
  124.8 1.7 %pad_maximum_fusion.4 = f32[256,128]{1,0:T(8,128)} fusion(f32[256,127]{1,0:T(8,128)S(1)} %slice.77, f32[256,1]{1,0:T(8,128)} %bitcast.57), kind=kLoop, calls=%fused_computation.5 | loop fusion | flops 32768 | bytes 262144 | tf_op jit(solution)/shard_map/jit(_roll_static)/concatenate | solution.py:290
  (7 shorter events, 0.2 us)
Async XLA Ops:
  2.4 7.2 %collective-permute-start = (bf16[24,4096]{1,0:T(8,128)(2,1)S(1)}, bf16[24,4096]{1,0:T(8,128)(2,1)S(1)}, u32[]{:S(2)}, u32[]{:S(2)}) collective-permute-start(bf16[24,4096]{1,0:T(8,128)(2,1)S(1)} %pad_maximum_fusion.1), channel_id=1, source_target_pairs={{0,1},{1,2},{2,3},{3,4},{4,5},{5,6},{6,7},{8,9},{9,10},{10,11},{11... | collective-permute-start | bytes 589832 | tf_op jit(solution)/shard_map/ppermute | solution.py:217
  9.6 0.7 copy-start.3
  10.3 16.2 %copy-start.5 = (f32[256,128]{1,0:T(8,128)S(1)}, f32[256,128]{1,0:T(8,128)}, u32[]{:S(2)}) copy-start(f32[256,128]{1,0:T(8,128)} %param.12) | copy-start | bytes 393220
  20.1 16.4 %collective-permute-start.1 = (bf16[128,4096]{1,0:T(8,128)(2,1)}, bf16[128,4096]{1,0:T(8,128)(2,1)S(1)}, u32[]{:S(2)}, u32[]{:S(2)}) collective-permute-start(bf16[128,4096]{1,0:T(8,128)(2,1)} %get-tuple-element.24.mix_ref), channel_id=1, source_target_pairs={{0,1},{1,2},{2,3},{3,4},{4,5},{5,6},{6,7},{8,9},{9,10},{10,11},{11... | collective-permute-start | bytes 3145736 | tf_op jit(solution)/shard_map/ppermute | solution.py:237
  24.5 16.3 %collective-permute-start.2 = (bf16[128,4096]{1,0:T(8,128)(2,1)}, bf16[128,4096]{1,0:T(8,128)(2,1)S(1)}, u32[]{:S(2)}, u32[]{:S(2)}) collective-permute-start(bf16[128,4096]{1,0:T(8,128)(2,1)} %get-tuple-element.25.gf_ref), channel_id=1, source_target_pairs={{1,0},{2,1},{3,2},{4,3},{5,4},{6,5},{7,6},{9,8},{10,9},{11,10},{12... | collective-permute-start | bytes 3145736 | tf_op jit(solution)/shard_map/ppermute | solution.py:238
  26.5 14.4 %copy-start = (f32[256,128]{1,0:T(8,128)}, f32[256,128]{1,0:T(8,128)S(1)}, u32[]{:S(2)}) copy-start(f32[256,128]{1,0:T(8,128)S(1)} %convert_convert_fusion.fwd_ref) | copy-start | bytes 393220
  36.5 4.3 %copy-start.1 = (bf16[128,4096]{1,0:T(8,128)(2,1)}, bf16[128,4096]{1,0:T(8,128)(2,1)S(1)}, u32[]{:S(2)}) copy-start(bf16[128,4096]{1,0:T(8,128)(2,1)S(1)} %collective-permute-done.1.prev_ref) | copy-start | bytes 3145732
  40.8 1.0 copy-start.2
  84.3 1.4 %collective-permute-start.4 = (bf16[4,4,32,128]{3,2,1,0:T(8,128)(2,1)S(1)}, bf16[4,4,32,128]{3,2,1,0:T(8,128)(2,1)S(1)}, u32[]{:S(2)}, u32[]{:S(2)}) collective-permute-start(bf16[4,4,32,128]{3,2,1,0:T(8,128)(2,1)S(1)} %bitcast.61), channel_id=1, source_target_pairs={{0,1},{1,0},{2,3},{3,2},{4,5},{5,4},{6,7},{7,6},{8,9},{9,8},{10,11... | collective-permute-start | bytes 393224 | tf_op jit(solution)/shard_map/ppermute | solution.py:171
  85.8 2.8 %collective-permute-start.5 = (bf16[4,32,128]{2,1,0:T(8,128)(2,1)S(1)}, bf16[4,32,128]{2,1,0:T(8,128)(2,1)S(1)}, u32[]{:S(2)}, u32[]{:S(2)}) collective-permute-start(bf16[4,32,128]{2,1,0:T(8,128)(2,1)S(1)} %get-tuple-element.61), channel_id=1, source_target_pairs={{0,8},{8,0},{16,24},{24,16},{1,9},{9,1},{17,25},{25,17},{2,10},{10... | collective-permute-start | bytes 98312 | tf_op jit(solution)/shard_map/ppermute | solution.py:175
  87.0 3.7 %collective-permute-start.7 = (bf16[4,32,128]{2,1,0:T(8,128)(2,1)S(1)}, bf16[4,32,128]{2,1,0:T(8,128)(2,1)S(1)}, u32[]{:S(2)}, u32[]{:S(2)}) collective-permute-start(bf16[4,32,128]{2,1,0:T(8,128)(2,1)S(1)} %get-tuple-element.62), channel_id=1, source_target_pairs={{0,24},{8,16},{16,8},{24,0},{1,25},{9,17},{17,9},{25,1},{2,26},{10... | collective-permute-start | bytes 98312 | tf_op jit(solution)/shard_map/ppermute | solution.py:175
  88.3 2.8 %collective-permute-start.6 = (bf16[4,32,128]{2,1,0:T(8,128)(2,1)S(1)}, bf16[4,32,128]{2,1,0:T(8,128)(2,1)S(1)}, u32[]{:S(2)}, u32[]{:S(2)}) collective-permute-start(bf16[4,32,128]{2,1,0:T(8,128)(2,1)S(1)} %get-tuple-element.63), channel_id=1, source_target_pairs={{0,16},{8,24},{16,0},{24,8},{1,17},{9,25},{17,1},{25,9},{2,18},{10... | collective-permute-start | bytes 98312 | tf_op jit(solution)/shard_map/ppermute | solution.py:175
  91.1 4.6 %collective-permute-start.10 = (bf16[4,32,128]{2,1,0:T(8,128)(2,1)S(1)}, bf16[4,32,128]{2,1,0:T(8,128)(2,1)S(1)}, u32[]{:S(2)}, u32[]{:S(2)}) collective-permute-start(bf16[4,32,128]{2,1,0:T(8,128)(2,1)S(1)} %fusion.3), channel_id=1, source_target_pairs={{0,6},{1,7},{2,4},{3,5},{4,2},{5,3},{6,0},{7,1},{8,14},{9,15},{10,... | collective-permute-start | bytes 98312 | tf_op jit(solution)/shard_map/ppermute | solution.py:186
  92.9 3.8 %collective-permute-start.9 = (bf16[4,32,128]{2,1,0:T(8,128)(2,1)S(1)}, bf16[4,32,128]{2,1,0:T(8,128)(2,1)S(1)}, u32[]{:S(2)}, u32[]{:S(2)}) collective-permute-start(bf16[4,32,128]{2,1,0:T(8,128)(2,1)S(1)} %fusion.3), channel_id=1, source_target_pairs={{0,4},{1,5},{2,6},{3,7},{4,0},{5,1},{6,2},{7,3},{8,12},{9,13},{10,... | collective-permute-start | bytes 98312 | tf_op jit(solution)/shard_map/ppermute | solution.py:186
  93.6 3.1 %collective-permute-start.8 = (bf16[4,32,128]{2,1,0:T(8,128)(2,1)S(1)}, bf16[4,32,128]{2,1,0:T(8,128)(2,1)S(1)}, u32[]{:S(2)}, u32[]{:S(2)}) collective-permute-start(bf16[4,32,128]{2,1,0:T(8,128)(2,1)S(1)} %fusion.3), channel_id=1, source_target_pairs={{0,2},{1,3},{2,0},{3,1},{4,6},{5,7},{6,4},{7,5},{8,10},{9,11},{10,... | collective-permute-start | bytes 98312 | tf_op jit(solution)/shard_map/ppermute | solution.py:186
  96.8 9.0 %collective-permute-start.13 = (bf16[4,32,128]{2,1,0:T(8,128)(2,1)S(1)}, bf16[4,32,128]{2,1,0:T(8,128)(2,1)S(1)}, u32[]{:S(2)}, u32[]{:S(2)}) collective-permute-start(bf16[4,32,128]{2,1,0:T(8,128)(2,1)S(1)} %add_convert_fusion), channel_id=1, source_target_pairs={{0,24},{8,16},{16,8},{24,0},{1,25},{9,17},{17,9},{25,1},{2,26},{10... | collective-permute-start | bytes 98312 | tf_op jit(solution)/shard_map/ppermute | solution.py:190
  98.1 7.7 %collective-permute-start.12 = (bf16[4,32,128]{2,1,0:T(8,128)(2,1)S(1)}, bf16[4,32,128]{2,1,0:T(8,128)(2,1)S(1)}, u32[]{:S(2)}, u32[]{:S(2)}) collective-permute-start(bf16[4,32,128]{2,1,0:T(8,128)(2,1)S(1)} %add_convert_fusion), channel_id=1, source_target_pairs={{0,16},{8,24},{16,0},{24,8},{1,17},{9,25},{17,1},{25,9},{2,18},{10... | collective-permute-start | bytes 98312 | tf_op jit(solution)/shard_map/ppermute | solution.py:190
  99.2 6.6 %collective-permute-start.11 = (bf16[4,32,128]{2,1,0:T(8,128)(2,1)S(1)}, bf16[4,32,128]{2,1,0:T(8,128)(2,1)S(1)}, u32[]{:S(2)}, u32[]{:S(2)}) collective-permute-start(bf16[4,32,128]{2,1,0:T(8,128)(2,1)S(1)} %add_convert_fusion), channel_id=1, source_target_pairs={{0,8},{8,0},{16,24},{24,16},{1,9},{9,1},{17,25},{25,17},{2,10},{10... | collective-permute-start | bytes 98312 | tf_op jit(solution)/shard_map/ppermute | solution.py:190
  99.5 10.4 %collective-permute-start.3 = (bf16[24,4096]{1,0:T(8,128)(2,1)}, bf16[24,4096]{1,0:T(8,128)(2,1)S(1)}, u32[]{:S(2)}, u32[]{:S(2)}) collective-permute-start(bf16[24,4096]{1,0:T(8,128)(2,1)} %get-tuple-element.33), channel_id=1, source_target_pairs={{1,0},{2,1},{3,2},{4,3},{5,4},{6,5},{7,6},{9,8},{10,9},{11,10},{12... | collective-permute-start | bytes 589832 | tf_op jit(solution)/shard_map/ppermute | solution.py:266
  105.8 13.2 %collective-permute-start.14 = (bf16[4,4,32,128]{3,2,1,0:T(8,128)(2,1)S(1)}, bf16[4,4,32,128]{3,2,1,0:T(8,128)(2,1)S(1)}, u32[]{:S(2)}, u32[]{:S(2)}) collective-permute-start(bf16[4,4,32,128]{3,2,1,0:T(8,128)(2,1)S(1)} %get-tuple-element.60), channel_id=1, source_target_pairs={{0,1},{1,0},{2,3},{3,2},{4,5},{5,4},{6,7},{7,6},{8,9},{9,8},{10,11... | collective-permute-start | bytes 393224 | tf_op jit(solution)/shard_map/ppermute | solution.py:192
  109.9 0.7 copy-start.4

commit v2 on v1

v2 whole, which is shorter than its diff:
```python
import functools

import jax
import jax.numpy as jnp
from jax import lax
from jax.experimental import pallas as pl
from jax.experimental.pallas import tpu as pltpu
from jax.sharding import PartitionSpec as P

LANES = 128
HALO = 8
TILES = 4
WIDE = TILES * LANES
SHARE = 32
VMEM = 40 * 1024 * 1024
F32, BF16 = jnp.float32, jnp.bfloat16
HBM = pl.BlockSpec(memory_space=pl.ANY)
WHOLE = pl.BlockSpec(memory_space=pltpu.VMEM)
SCALARS = pl.BlockSpec(memory_space=pltpu.SMEM)


def lanes_at(first, width=LANES):
    if isinstance(first, int):
        return pl.ds(first, width)
    return pl.ds(pl.multiple_of(first, LANES), width)


def stream(pieces, sources, stores, in_sem, out_sem, work):
    def fetch(index, piece):
        ref, first, buffer = sources[index]
        return pltpu.make_async_copy(
            ref.at[:, lanes_at(first + piece * WIDE, WIDE)],
            buffer.at[:, lanes_at(piece * WIDE, WIDE)], in_sem.at[index, piece])

    def store(index, piece):
        buffer, ref, first = stores[index]
        return pltpu.make_async_copy(
            buffer.at[:, lanes_at(piece * WIDE, WIDE)],
            ref.at[:, lanes_at(first + piece * WIDE, WIDE)], out_sem.at[index, piece])

    def begin(piece, carry):
        for index in range(len(sources)):
            fetch(index, piece).start()
        return carry

    def step(piece, carry):
        for index in range(len(sources)):
            fetch(index, piece).wait()
        work(piece)
        for index in range(len(stores)):
            store(index, piece).start()
        return carry

    def end(piece, carry):
        for index in range(len(stores)):
            store(index, piece).wait()
        return carry

    lax.fori_loop(0, pieces, begin, 0)
    lax.fori_loop(0, pieces, step, 0)
    lax.fori_loop(0, pieces, end, 0)


def per_tile(piece, unroll, one):
    def run(index, carry):
        one(piece * TILES + index)
        return carry

    lax.fori_loop(0, TILES, run, 0, unroll=unroll)


def tails_kernel(q_ref, k_ref, v_ref, out_ref):
    out_ref[...] = jnp.concatenate(
        [ref[...].astype(F32)[HALO:] for ref in (q_ref, k_ref, v_ref)], axis=0).astype(BF16)


def feat_kernel(first, rows, taps_count, pieces, q_hbm, k_hbm, v_hbm, cot_hbm, tail_ref, taps_ref,
                mix_hbm, gf_hbm, qf_hbm, kf_hbm, vf_hbm, *scratch):
    q_ref, k_ref, v_ref, cot_ref, mix_ref, gf_ref, qf_ref, kf_ref, vf_ref, ext, in_sem, out_sem = scratch

    def one(tile):
        lanes = lanes_at(tile * LANES)
        far = lanes_at(first + tile * LANES)
        tails = tail_ref[:, far].astype(F32)
        feats = []
        for which, src in enumerate((q_ref, k_ref, v_ref)):
            ext[which, pl.ds(0, HALO), :] = tails[which * HALO:(which + 1) * HALO]
            ext[which, pl.ds(HALO, rows), :] = src[:, lanes].astype(F32)
            total = None
            for lag in range(taps_count):
                term = taps_ref[lag, which:which + 1, far] * ext[which, pl.ds(HALO - lag, rows), :]
                total = term if total is None else total + term
            feats.append(total)
        qf_ref[:, lanes] = feats[0].astype(BF16)
        kf_ref[:, lanes] = feats[1].astype(BF16)
        vf_ref[:, lanes] = feats[2].astype(BF16)
        mix_ref[:, lanes] = (feats[1] * feats[2]).astype(BF16)
        gf_ref[:, lanes] = (cot_ref[:, lanes].astype(F32) * feats[0]).astype(BF16)

    stream(pieces,
           [(q_hbm, first, q_ref), (k_hbm, first, k_ref), (v_hbm, first, v_ref), (cot_hbm, first, cot_ref)],
           [(mix_ref, mix_hbm, 0), (gf_ref, gf_hbm, 0), (qf_ref, qf_hbm, 0), (kf_ref, kf_hbm, 0),
            (vf_ref, vf_hbm, 0)],
           in_sem, out_sem, lambda piece: per_tile(piece, 1, one))


def turned(size):
    row = lax.broadcasted_iota(jnp.int32, (size, size), 0)
    col = lax.broadcasted_iota(jnp.int32, (size, size), 1)
    return jnp.where(lax.rem(row + col, size) == 0, 1.0, 0.0).astype(BF16)


def mix_kernel(first, rows, taps_count, pieces, per_group, place_ref, q_hbm, k_hbm, v_hbm, cot_hbm, tail_ref,
               mix_hbm, gf_hbm, qf_hbm, kf_hbm, vf_hbm, prev_hbm, next_hbm, filt_ref, gain_ref, *rest):
    if first:
        rest = rest[1:]
    out_hbm, gq_hbm, gk_hbm, gv_hbm, head_ref, grad_ref = rest[:6]
    (q_ref, k_ref, v_ref, cot_ref, mix_ref, gf_ref, qf_ref, kf_ref, vf_ref, prev_ref, next_ref,
     out_ref, gq_ref, gk_ref, gv_ref, rev_ref, ext, part, in_sem, out_sem) = rest[6:]
    half = rows // 2
    groups = LANES // per_group
    row_id = lax.broadcasted_iota(jnp.int32, (half, LANES), 0)
    lane_id = lax.broadcasted_iota(jnp.int32, (half, LANES), 1)
    wide_group = lax.broadcasted_iota(jnp.int32, (half, 2 * LANES), 1) % LANES // per_group
    later = lane_id > row_id
    early = lane_id < row_id
    zero = jnp.zeros((half, LANES), F32)
    rev_ref[...] = jnp.dot(filt_ref[...].astype(BF16), turned(filt_ref.shape[1]), preferred_element_type=F32)

    def one(tile):
        lanes = lanes_at(tile * LANES)
        far = lanes_at(first + tile * LANES)
        mix = mix_ref[:, lanes]
        prev = prev_ref[:, lanes]
        gf = gf_ref[:, lanes]
        nxt = next_ref[:, lanes]
        before = jnp.concatenate([
            jnp.concatenate([prev, mix], axis=0),
            jnp.concatenate([prev[half:], mix, mix[:half]], axis=0)], axis=1)
        after = jnp.concatenate([
            jnp.concatenate([gf, nxt], axis=0),
            jnp.concatenate([gf[half:], nxt, nxt[:half]], axis=0)], axis=1)
        gf_wide = jnp.concatenate([gf[:half], gf[half:]], axis=1)
        mine = pl.ds(pl.multiple_of(tile * groups, groups), groups)
        rev = rev_ref[mine, :]
        fwd = filt_ref[mine, :].astype(BF16).astype(F32)
        firsts, seconds, masked = [], [], []
        for group in range(groups):
            circ = pltpu.roll(jnp.broadcast_to(rev[group:group + 1], (half, LANES)), 0, 1,
                              stride=1, stride_axis=0)
            firsts.append(jnp.concatenate(
                [jnp.where(later, circ, zero), jnp.where(later, zero, circ)], axis=1).astype(BF16))
            circ = pltpu.roll(jnp.broadcast_to(fwd[group:group + 1], (half, LANES)), 0, 1,
                              stride=1, stride_axis=0)
            seconds.append(jnp.concatenate(
                [jnp.where(early, zero, circ), jnp.where(early, circ, zero)], axis=1).astype(BF16))
            masked.append(jnp.where(wide_group == group, gf_wide, jnp.zeros_like(gf_wide)))

        def filtered_by(matrices, window):
            found = jnp.dot(jnp.concatenate(matrices, axis=0), window, preferred_element_type=F32)
            picked = found[:half]
            for group in range(1, groups):
                picked = jnp.where(wide_group == group, found[group * half:(group + 1) * half], picked)
            return jnp.concatenate([picked[:, :LANES], picked[:, LANES:]], axis=0)

        conv = filtered_by(firsts, before)
        back = filtered_by(seconds, after)
        prod = lax.dot_general(jnp.concatenate(masked, axis=0), before, (((1,), (1,)), ((), ())),
                               preferred_element_type=F32)
        sums = []
        for group in range(groups):
            own = prod[group * half:(group + 1) * half]
            square = jnp.where(later, own[:, :LANES], own[:, LANES:])
            total = square[:8]
            for start in range(8, half, 8):
                total = total + pltpu.roll(square[start:start + 8], LANES - start, 1)
            sums.append(total)
        sums = jnp.concatenate(sums, axis=0)
        turn = lax.broadcasted_iota(jnp.int32, sums.shape, 0)
        for bit in (1, 2, 4):
            sums = jnp.where((turn & bit) > 0, pltpu.roll(sums, LANES - bit, 1), sums)
        part[pl.ds(SHARE - groups, groups), :] = jnp.sum(sums.reshape(groups, 8, LANES), axis=1)

        gain = gain_ref[:, far]
        mix_wide = mix.astype(F32)
        gf_f32 = gf.astype(F32)
        filtered = conv + gain * mix_wide
        grad_mix = back + gain * gf_f32
        part[pl.ds(3 * taps_count, 1), :] = jnp.sum(mix_wide * gf_f32, axis=0, keepdims=True)
        out_ref[:, lanes] = (qf_ref[:, lanes].astype(F32) * filtered).astype(BF16)
        grads = (cot_ref[:, lanes].astype(F32) * filtered, grad_mix * vf_ref[:, lanes].astype(F32),
                 grad_mix * kf_ref[:, lanes].astype(F32))
        tails = tail_ref[:, far].astype(F32)
        for which, (src, grad, dest) in enumerate(zip((q_ref, k_ref, v_ref), grads, (gq_ref, gk_ref, gv_ref))):
            dest[:, lanes] = grad.astype(BF16)
            ext[which, pl.ds(0, HALO), :] = tails[which * HALO:(which + 1) * HALO]
            ext[which, pl.ds(HALO, rows), :] = src[:, lanes].astype(F32)
            for lag in range(taps_count):
                part[pl.ds(lag * 3 + which, 1), :] = jnp.sum(
                    grad * ext[which, pl.ds(HALO - lag, rows), :], axis=0, keepdims=True)
        head_ref[:, lanes] = jnp.concatenate([grad[:HALO] for grad in grads], axis=0).astype(BF16)
        grad_ref[place_ref[tile]] = part[...].astype(BF16)

    part[...] = jnp.zeros(part.shape, F32)
    stream(pieces,
           [(q_hbm, first, q_ref), (k_hbm, first, k_ref), (v_hbm, first, v_ref), (cot_hbm, first, cot_ref),
            (mix_hbm, 0, mix_ref), (gf_hbm, 0, gf_ref), (qf_hbm, 0, qf_ref), (kf_hbm, 0, kf_ref),
            (vf_hbm, 0, vf_ref), (prev_hbm, 0, prev_ref), (next_hbm, 0, next_ref)],
           [(out_ref, out_hbm, first), (gq_ref, gq_hbm, 0), (gk_ref, gk_hbm, 0), (gv_ref, gv_hbm, 0)],
           in_sem, out_sem, lambda piece: per_tile(piece, TILES, one))


def back_kernel(which, rows, taps_count, pieces, parts, *refs):
    grads, heads, taps_ref, out_hbm = refs[:parts], refs[parts:2 * parts], refs[2 * parts], refs[2 * parts + 1]
    grad_ref, out_ref, ext, in_sem, out_sem = refs[2 * parts + 2:]
    width = pieces * WIDE

    for index in range(parts):
        def one(tile, index=index):
            lanes = lanes_at(index * width + tile * LANES)
            ext[pl.ds(0, rows), :] = grad_ref[:, lanes].astype(F32)
            head = heads[index][:, lanes_at(tile * LANES)].astype(F32)
            ext[pl.ds(rows, HALO), :] = head[which * HALO:(which + 1) * HALO]
            total = None
            for lag in range(taps_count):
                term = taps_ref[lag, which:which + 1, lanes] * ext[pl.ds(lag, rows), :]
                total = term if total is None else total + term
            out_ref[:, lanes] = total.astype(BF16)

        part_in = grad_ref.at[:, pl.ds(index * width, width)]
        part_out = out_ref.at[:, pl.ds(index * width, width)]
        stream(pieces, [(grads[index], 0, part_in)], [(part_out, out_hbm, index * width)],
               in_sem, out_sem, lambda piece, one=one: per_tile(piece, 1, one))


def unpack_kernel(taps_count, scale, place_ref, core_ref, mine_ref, other_ref, taps_ref, filt_ref, skip_ref):
    in_half = mine_ref.shape[0]
    count = 2 * in_half
    groups = filt_ref.shape[0] // count
    flip = turned(filt_ref.shape[1])
    for tile in range(count):
        slot = place_ref[tile % in_half]
        block = jnp.where(core_ref[0] == tile // in_half, mine_ref[slot].astype(F32), other_ref[slot].astype(F32))
        lanes = pl.ds(tile * LANES, LANES)
        for which in range(3):
            for lag in range(taps_count):
                row = lag * 3 + which
                taps_ref[which, lag:lag + 1, lanes] = block[row:row + 1] * scale
        skip_ref[:, lanes] = block[3 * taps_count:3 * taps_count + 1] * scale
        filt_ref[pl.ds(tile * groups, groups), :] = block[SHARE - groups:]
    filt_ref[...] = jnp.dot(filt_ref[...].astype(BF16), flip, preferred_element_type=F32) * scale


def swaps(size, mask):
    return [(i, i ^ mask) for i in range(size)]


def reduce_all(mine, theirs, ctx_count, dp_count):
    half = mine.astype(F32) + lax.ppermute(theirs, "ctx", swaps(ctx_count, 1)).astype(F32)
    sent = half.astype(BF16)
    total = half[0]
    for mask in range(1, dp_count):
        total = total + lax.ppermute(sent[mask], "dp", swaps(dp_count, mask)).astype(F32)
    mask = 2
    while mask < ctx_count:
        low = total.astype(BF16)
        picks = (mask, 2 * mask, 3 * mask) if mask * 2 < ctx_count else (mask,)
        mask *= 4
        for pick in picks:
            total = total + lax.ppermute(low, "ctx", swaps(ctx_count, pick)).astype(F32)
    low = total.astype(BF16)
    quarters = [low]
    for mask in range(1, dp_count):
        quarters.append(lax.ppermute(low, "dp", swaps(dp_count, mask)))
    whole = jnp.stack(quarters)
    return whole, lax.ppermute(whole, "ctx", swaps(ctx_count, 1))


def body(query_rows, key_rows, value_rows, cotangent, feature_taps, filter_taps, skip_gain):
    rows, channels = query_rows.shape[1:]
    taps_count = feature_taps.shape[0]
    group_count, taps_len = filter_taps.shape
    per_group = channels // group_count
    ctx_count, dp_count = lax.axis_size("ctx"), lax.axis_size("dp")
    assert rows == taps_len == LANES and taps_count <= HALO
    scale = float(dp_count * ctx_count * rows) ** (-0.5)
    parts = 2
    width = channels // parts
    pieces = width // WIDE
    in_half = width // LANES
    in_quarter = in_half // dp_count
    query, key, value, cot = query_rows[0], key_rows[0], value_rows[0], cotangent[0]
    onward = [(i, i + 1) for i in range(ctx_count - 1)]
    backward = [(i + 1, i) for i in range(ctx_count - 1)]
    gains = skip_gain.reshape(1, channels)
    core = lax.rem(lax.axis_index("ctx"), 2).astype(jnp.int32)
    tile_of = jnp.arange(in_half, dtype=jnp.int32)
    place = (((tile_of // in_quarter) ^ lax.axis_index("dp").astype(jnp.int32)) * in_quarter
             + tile_of % in_quarter).astype(jnp.int32)

    def shape(height, kind, across=width):
        return jax.ShapeDtypeStruct((height, across), kind)

    def buffers(count):
        return [pltpu.VMEM((rows, width), BF16)] * count

    def sems(ins, outs):
        return [pltpu.SemaphoreType.DMA((ins, pieces)), pltpu.SemaphoreType.DMA((outs, pieces))]

    compiler_params = pltpu.CompilerParams(vmem_limit_bytes=VMEM)
    last = pl.BlockSpec((2 * HALO, channels), lambda step: (rows // (2 * HALO) - 1, 0))
    tails = pl.pallas_call(
        tails_kernel,
        grid=(1,),
        in_specs=[last] * 3,
        out_specs=pl.BlockSpec((3 * HALO, channels), lambda step: (0, 0)),
        out_shape=shape(3 * HALO, BF16, channels),
        compiler_params=compiler_params,
        name="tails",
    )(query, key, value)
    tails = lax.ppermute(tails, "ctx", onward)

    made = []
    for part in range(parts):
        feats = pl.pallas_call(
            functools.partial(feat_kernel, part * width, rows, taps_count, pieces),
            in_specs=[HBM] * 4 + [WHOLE] * 2,
            out_specs=[HBM] * 5,
            out_shape=[shape(rows, BF16)] * 5,
            scratch_shapes=buffers(9) + [pltpu.VMEM((3, rows + HALO, LANES), F32)] + sems(4, 5),
            compiler_params=compiler_params,
            cost_estimate=pl.CostEstimate(flops=50 * rows * width, bytes_accessed=18 * rows * width, transcendentals=0),
            name="features",
        )(query, key, value, cot, tails, feature_taps)
        made.append(feats)

    halos = [(lax.ppermute(feats[0], "ctx", onward), lax.ppermute(feats[1], "ctx", backward)) for feats in made]

    out = None
    results = []
    for part in range(parts):
        found = pl.pallas_call(
            functools.partial(mix_kernel, part * width, rows, taps_count, pieces, per_group),
            in_specs=[SCALARS] + [HBM] * 4 + [WHOLE] + [HBM] * 7 + [WHOLE] * 2 + ([HBM] if part else []),
            out_specs=[HBM] * 4 + [WHOLE] * 2,
            out_shape=[shape(rows, BF16, channels)] + [shape(rows, BF16)] * 3 + [shape(3 * HALO, BF16)]
            + [jax.ShapeDtypeStruct((in_half, SHARE, LANES), BF16)],
            input_output_aliases={15: 0} if part else {},
            scratch_shapes=buffers(15)
            + [pltpu.VMEM((group_count // parts, taps_len), F32), pltpu.VMEM((3, rows + HALO, LANES), F32),
               pltpu.VMEM((SHARE, LANES), F32)] + sems(11, 4),
            compiler_params=compiler_params,
            cost_estimate=pl.CostEstimate(flops=2000 * rows * width, bytes_accessed=30 * rows * width, transcendentals=0),
            name="filters",
        )(place, query, key, value, cot, tails, *made[part], *halos[part],
          filter_taps[part * group_count // parts:(part + 1) * group_count // parts], gains,
          *([out] if part else []))
        out = found[0]
        results.append(found[1:])

    next_heads = [lax.ppermute(found[3], "ctx", backward) for found in results]
    shares = [found[4].reshape(dp_count, in_quarter, SHARE, LANES) for found in results]
    mine, other = reduce_all(jnp.where(core == 0, shares[0], shares[1]), jnp.where(core == 0, shares[1], shares[0]),
                             ctx_count, dp_count)

    grads = []
    for which in range(3):
        grads.append(pl.pallas_call(
            functools.partial(back_kernel, which, rows, taps_count, pieces, parts),
            in_specs=[HBM] * parts + [WHOLE] * (parts + 1),
            out_specs=HBM,
            out_shape=shape(rows, BF16, channels),
            scratch_shapes=[pltpu.VMEM((rows, channels), BF16)] * 2 + [pltpu.VMEM((rows + HALO, LANES), F32)]
            + sems(1, 1),
            compiler_params=compiler_params,
            cost_estimate=pl.CostEstimate(flops=16 * rows * channels, bytes_accessed=4 * rows * channels, transcendentals=0),
            name="features_back",
        )(*[found[which] for found in results], *next_heads, feature_taps))

    grad_taps, grad_filter, grad_skip = pl.pallas_call(
        functools.partial(unpack_kernel, taps_count, scale),
        in_specs=[SCALARS, SCALARS, WHOLE, WHOLE],
        out_specs=[WHOLE] * 3,
        out_shape=[jax.ShapeDtypeStruct((3, taps_count, channels), F32), jax.ShapeDtypeStruct(filter_taps.shape, F32),
                   jax.ShapeDtypeStruct((1, channels), F32)],
        compiler_params=compiler_params,
        name="unpack",
    )(place, core.reshape(1), mine.reshape(in_half, SHARE, LANES), other.reshape(in_half, SHARE, LANES))
    return (out[None], grads[0][None], grads[1][None], grads[2][None], jnp.transpose(grad_taps, (1, 0, 2)),
            grad_filter, grad_skip.reshape(channels))


def solution(mesh):
    rows = P("dp", "ctx", None)
    return jax.shard_map(
        body,
        mesh=mesh,
        in_specs=(rows, rows, rows, rows, P(), P(), P()),
        out_specs=(rows, rows, rows, rows, P(), P(), P()),
        check_vma=False,
    )
```

time: 127 us -> 112 us (0.88)
  Pallas kernels: 61.6 us -> 43 us
  starting transfers between devices: 27.8 us -> 35.3 us
  waiting for transfers between devices: 21.7 us -> 17.5 us
  other arithmetic: 3.91 us -> 0.15 us
  local copies, waits for them, and re-layouts: 10.7 us -> 13.8 us
    pallas_call x4 -> x9, Pallas kernels: 61.6 us -> 43 us  [the longest x2 23.2 us: body(): pl.pallas_call(functools.partial(mix_kernel, part * width, rows, taps_cou...]
    unnamed x14 -> x51, local copies, waits for them, and re-layouts: 5.58 us -> 13.8 us
    ppermute x15 -> x18, starting transfers between devices: 27.8 us -> 35.3 us  [the longest x2 8.01 us: body(): lax.ppermute(feats[0], 'ctx', onward)]
    ppermute x15 -> x18, waiting for transfers between devices: 21.7 us -> 17.5 us  [the longest x3 4.56 us: reduce_all(): total = total + lax.ppermute(low, 'ctx', swaps(ctx_count, pick)).astype(F32)]
    slice x7 -> x1, local copies, waits for them, and re-layouts: 4.17 us -> 0.01 us  [body(): filter_taps[part * group_count // parts:(part + 1) * group_count // parts]]
    concatenate x3 -> x0, other arithmetic: 2.45 us -> none  [the longest x1 1.68 us: body(): grad_filter = jnp.roll(grad_filter[:, ::-1], 1, axis=1)]
  transfers between devices with their start and end apart: 15 -> 18, of which waited for: 11 -> 12; matrix products, arithmetic and copies ran while one was open for 3% -> 0% of each run, Pallas kernels for 7% -> 23%
where the time goes in v2:
time: 112 us; the launch traced here: 111 us
  Pallas kernels  43 us (38%)
  starting transfers between devices  35.3 us (32%)
  waiting for transfers between devices  17.5 us (16%)
  local copies, waits for them, and re-layouts  13.8 us (12%)
    pallas_call x2, Pallas kernels, body(): pl.pallas_call(functools.partial(mix_kernel, part * width, rows, taps_cou...  23.2 us
    unnamed x51, local copies, waits for them, and re-layouts  13.8 us
    pallas_call x3, Pallas kernels, body(): pl.pallas_call(functools.partial(back_kernel, which, rows, taps_count, pi...  9.58 us
    pallas_call x2, Pallas kernels, body(): pl.pallas_call(functools.partial(feat_kernel, part * width, rows, taps_co...  8.69 us
    ppermute x2, starting transfers between devices, body(): lax.ppermute(feats[0], 'ctx', onward)  8.01 us
    ppermute x1, starting transfers between devices, reduce_all(): return (whole, lax.ppermute(whole, 'ctx', swaps(ctx_count, 1)))  5.25 us
    ppermute x1, starting transfers between devices, body(): tails = lax.ppermute(tails, 'ctx', onward)  4.73 us
    ppermute x3, waiting for transfers between devices, reduce_all(): total = total + lax.ppermute(low, 'ctx', swaps(ctx_count, pick)).astype(F32)  4.56 us
  transfers between devices with their start and end apart: 18, of which 12 were waited for; matrix products, arithmetic and copies ran while one was open for 0% of the time, Pallas kernels for 23%

profile of v2, /device:TPU:1, one launch (start us, length us, event | category | flops | bytes accessed | tf_op | source)
XLA Modules:
  0.0 110.9 jit_solution(1062551953653313764)
XLA Ops:
  0.6 0.0 copy-start
  0.6 1.2 %copy-done = bf16[1,128,4096]{2,1,0:T(8,128)(2,1)S(1)} copy-done((bf16[1,128,4096]{2,1,0:T(8,128)(2,1)S(1)}, bf16[1,128,4096]{2,1,0:T(8,128)(2,1)}, u32[]{:S(2)}) %copy-start) | copy-done | bytes 1048600
  1.9 1.2 %copy-done.2 = bf16[1,128,4096]{2,1,0:T(8,128)(2,1)S(1)} copy-done((bf16[1,128,4096]{2,1,0:T(8,128)(2,1)S(1)}, bf16[1,128,4096]{2,1,0:T(8,128)(2,1)}, u32[]{:S(2)}) %copy-start.2) | copy-done | bytes 1048600
  3.1 1.2 %copy-done.4 = bf16[1,128,4096]{2,1,0:T(8,128)(2,1)S(1)} copy-done((bf16[1,128,4096]{2,1,0:T(8,128)(2,1)S(1)}, bf16[1,128,4096]{2,1,0:T(8,128)(2,1)}, u32[]{:S(2)}) %copy-start.4) | copy-done | bytes 1048600
  4.3 4.7 %collective-permute-start = (bf16[24,4096]{1,0:T(8,128)(2,1)S(1)}, bf16[24,4096]{1,0:T(8,128)(2,1)S(1)}, u32[]{:S(2)}, u32[]{:S(2)}) collective-permute-start(bf16[24,4096]{1,0:T(8,128)(2,1)S(1)} %tails.1), channel_id=1, source_target_pairs={{0,1},{1,2},{2,3},{3,4},{4,5},{5,6},{6,7},{8,9},{9,10},{10,11},{11... | collective-permute-start | bytes 589832 | tf_op jit(solution)/shard_map/ppermute | solution.py:321
  9.1 0.2 copy.15.taps_ref.refs_4_
  9.3 2.3 %collective-permute-done.tail_ref = bf16[24,4096]{1,0:T(8,128)(2,1)S(1)} collective-permute-done((bf16[24,4096]{1,0:T(8,128)(2,1)S(1)}, bf16[24,4096]{1,0:T(8,128)(2,1)S(1)}, u32[]{:S(2)}, u32[]{:S(2)}) %collective-permute-start) | collective-permute-done | bytes 196640 | tf_op jit(solution)/shard_map/ppermute | solution.py:321
  11.7 4.4 %features.3 = (bf16[128,2048]{1,0:T(8,128)(2,1)}, bf16[128,2048]{1,0:T(8,128)(2,1)}, bf16[128,2048]{1,0:T(8,128)(2,1)S(1)}, bf16[128,2048]{1,0:T(8,128)(2,1)S(1)}, bf16[128,2048]{1,0:T(8,128)(2,1)S(1)}) custom-call(bf16[128,4096]{1,0:T(8,128)(2,1)S(1)} %bitcast.40, bf16[128,4096]{1,0:T(8,128)(2,1)S(1)} %bitcast.45, bf16[128,4096]{1,0:T(8,128)(2,1)S(1)} %bitcast.50, ...), custom_call_target="tpu_custom_call" | custom-call | flops 13107200 | bytes 4718592 | tf_op jit(solution)/shard_map/features/pallas_call | solution.py:325
  16.0 0.0 copy-start.16
  16.0 0.8 copy-done.16
  16.8 0.8 copy-done.18
  17.6 0.8 copy-done.20
  18.5 4.4 %collective-permute-start.3 = (bf16[128,2048]{1,0:T(8,128)(2,1)}, bf16[128,2048]{1,0:T(8,128)(2,1)}, u32[]{:S(2)}, u32[]{:S(2)}) collective-permute-start(bf16[128,2048]{1,0:T(8,128)(2,1)} %get-tuple-element.37.mix_hbm), channel_id=1, source_target_pairs={{0,1},{1,2},{2,3},{3,4},{4,5},{5,6},{6,7},{8,9},{9,10},{10,11},{11... | collective-permute-start | bytes 1572872 | tf_op jit(solution)/shard_map/ppermute | solution.py:337
  22.8 0.0 copy-start.24
  22.9 0.0 copy-start.1
  22.9 0.0 copy-start.3
  22.9 0.0 copy-start.5
  22.9 2.2 %collective-permute-start.4 = (bf16[128,2048]{1,0:T(8,128)(2,1)}, bf16[128,2048]{1,0:T(8,128)(2,1)}, u32[]{:S(2)}, u32[]{:S(2)}) collective-permute-start(bf16[128,2048]{1,0:T(8,128)(2,1)} %get-tuple-element.38.gf_hbm), channel_id=1, source_target_pairs={{1,0},{2,1},{3,2},{4,3},{5,4},{6,5},{7,6},{9,8},{10,9},{11,10},{12... | collective-permute-start | bytes 1572872 | tf_op jit(solution)/shard_map/ppermute | solution.py:337
  25.1 4.3 %features.2 = (bf16[128,2048]{1,0:T(8,128)(2,1)}, bf16[128,2048]{1,0:T(8,128)(2,1)}, bf16[128,2048]{1,0:T(8,128)(2,1)S(1)}, bf16[128,2048]{1,0:T(8,128)(2,1)S(1)}, bf16[128,2048]{1,0:T(8,128)(2,1)S(1)}) custom-call(bf16[128,4096]{1,0:T(8,128)(2,1)S(1)} %bitcast.41, bf16[128,4096]{1,0:T(8,128)(2,1)S(1)} %bitcast.46, bf16[128,4096]{1,0:T(8,128)(2,1)S(1)} %bitcast.51, ...), custom_call_target="tpu_custom_call" | custom-call | flops 13107200 | bytes 4718592 | tf_op jit(solution)/shard_map/features/pallas_call | solution.py:325
  29.4 0.0 copy-start.10
  29.4 0.8 copy-done.10
  30.2 0.8 copy-done.12
  31.1 0.8 copy-done.14
  31.9 3.6 %collective-permute-start.1 = (bf16[128,2048]{1,0:T(8,128)(2,1)}, bf16[128,2048]{1,0:T(8,128)(2,1)}, u32[]{:S(2)}, u32[]{:S(2)}) collective-permute-start(bf16[128,2048]{1,0:T(8,128)(2,1)} %get-tuple-element.32.mix_hbm), channel_id=1, source_target_pairs={{0,1},{1,2},{2,3},{3,4},{4,5},{5,6},{6,7},{8,9},{9,10},{10,11},{11... | collective-permute-start | bytes 1572872 | tf_op jit(solution)/shard_map/ppermute | solution.py:337
  35.5 1.9 %collective-permute-start.2 = (bf16[128,2048]{1,0:T(8,128)(2,1)}, bf16[128,2048]{1,0:T(8,128)(2,1)}, u32[]{:S(2)}, u32[]{:S(2)}) collective-permute-start(bf16[128,2048]{1,0:T(8,128)(2,1)} %get-tuple-element.33.gf_hbm), channel_id=1, source_target_pairs={{1,0},{2,1},{3,2},{4,3},{5,4},{6,5},{7,6},{9,8},{10,9},{11,10},{12... | collective-permute-start | bytes 1572872 | tf_op jit(solution)/shard_map/ppermute | solution.py:337
  37.5 0.0 copy-start.22
  37.5 0.0 collective-permute-done.3.prev_hbm
  37.5 0.0 collective-permute-done.4.next_hbm
  37.5 0.6 copy-done.22
  38.2 1.2 %copy-done.7 = bf16[1,128,4096]{2,1,0:T(8,128)(2,1)S(1)} copy-done((bf16[1,128,4096]{2,1,0:T(8,128)(2,1)S(1)}, bf16[1,128,4096]{2,1,0:T(8,128)(2,1)}, u32[]{:S(2)}) %copy-start.7) | copy-done | bytes 1048600
  39.4 1.0 copy-done.17
  40.4 1.0 copy-done.19
  41.5 1.0 copy-done.21
  42.5 11.6 %filters.2 = (bf16[128,4096]{1,0:T(8,128)(2,1)}, bf16[128,2048]{1,0:T(8,128)(2,1)S(1)}, bf16[128,2048]{1,0:T(8,128)(2,1)S(1)}, bf16[128,2048]{1,0:T(8,128)(2,1)S...) custom-call(s32[16]{0:T(128)S(1)} %fusion.4.place_ref, bf16[128,4096]{1,0:T(8,128)(2,1)S(1)} %bitcast.42, ...), custom_call_target="tpu_custom_call" | custom-call | flops 524288000 | bytes 7864320 | tf_op jit(solution)/shard_map/filters/pallas_call | solution.py:342
  54.2 0.0 collective-permute-done.1.prev_hbm
  54.2 11.6 %filters.3 = (bf16[128,4096]{1,0:T(8,128)(2,1)}, bf16[128,2048]{1,0:T(8,128)(2,1)S(1)}, bf16[128,2048]{1,0:T(8,128)(2,1)S(1)}, bf16[128,2048]{1,0:T(8,128)(2,1)S...) custom-call(s32[16]{0:T(128)S(1)} %fusion.4.place_ref, ...), custom_call_target="tpu_custom_call", output_to_operand_aliasing={{0}: (15, {})} | custom-call | flops 524288000 | bytes 7864320 | tf_op jit(solution)/shard_map/filters/pallas_call | solution.py:342
  65.9 0.1 collective-permute-start.7
  65.9 1.3 %collective-permute-done.7 = bf16[4,4,32,128]{3,2,1,0:T(8,128)(2,1)S(1)} collective-permute-done((bf16[4,4,32,128]{3,2,1,0:T(8,128)(2,1)S(1)}, bf16[4,4,32,128]{3,2,1,0:T(8,128)(2,1)S(1)}, u32[]{:S(2)}, u32[]{:S(2)}) %collective-permute-start.7) | collective-permute-done | bytes 131104 | tf_op jit(solution)/shard_map/ppermute | solution.py:259
  67.4 2.2 %collective-permute-start.10 = (bf16[4,32,128]{2,1,0:T(8,128)(2,1)S(1)}, bf16[4,32,128]{2,1,0:T(8,128)(2,1)S(1)}, u32[]{:S(2)}, u32[]{:S(2)}) collective-permute-start(bf16[4,32,128]{2,1,0:T(8,128)(2,1)S(1)} %get-tuple-element.62), channel_id=1, source_target_pairs={{0,24},{8,16},{16,8},{24,0},{1,25},{9,17},{17,9},{25,1},{2,26},{10... | collective-permute-start | bytes 98312 | tf_op jit(solution)/shard_map/ppermute | solution.py:263
  69.6 0.3 collective-permute-start.8
  69.8 0.2 collective-permute-start.9
  70.1 1.0 collective-permute-done.10
  71.1 1.3 %collective-permute-done.8 = bf16[4,32,128]{2,1,0:T(8,128)(2,1)S(1)} collective-permute-done((bf16[4,32,128]{2,1,0:T(8,128)(2,1)S(1)}, bf16[4,32,128]{2,1,0:T(8,128)(2,1)S(1)}, u32[]{:S(2)}, u32[]{:S(2)}) %collective-permute-start.8) | collective-permute-done | bytes 32800 | tf_op jit(solution)/shard_map/ppermute | solution.py:263
  72.3 0.3 collective-permute-done.9
  72.6 1.6 %collective-permute-start.11 = (bf16[4,32,128]{2,1,0:T(8,128)(2,1)S(1)}, bf16[4,32,128]{2,1,0:T(8,128)(2,1)S(1)}, u32[]{:S(2)}, u32[]{:S(2)}) collective-permute-start(bf16[4,32,128]{2,1,0:T(8,128)(2,1)S(1)} %fusion.3), channel_id=1, source_target_pairs={{0,2},{1,3},{2,0},{3,1},{4,6},{5,7},{6,4},{7,5},{8,10},{9,11},{10,... | collective-permute-start | bytes 98312 | tf_op jit(solution)/shard_map/ppermute | solution.py:270
  74.2 2.3 %collective-permute-start.12 = (bf16[4,32,128]{2,1,0:T(8,128)(2,1)S(1)}, bf16[4,32,128]{2,1,0:T(8,128)(2,1)S(1)}, u32[]{:S(2)}, u32[]{:S(2)}) collective-permute-start(bf16[4,32,128]{2,1,0:T(8,128)(2,1)S(1)} %fusion.3), channel_id=1, source_target_pairs={{0,4},{1,5},{2,6},{3,7},{4,0},{5,1},{6,2},{7,3},{8,12},{9,13},{10,... | collective-permute-start | bytes 98312 | tf_op jit(solution)/shard_map/ppermute | solution.py:270
  76.5 1.7 %collective-permute-done.12 = bf16[4,32,128]{2,1,0:T(8,128)(2,1)S(1)} collective-permute-done((bf16[4,32,128]{2,1,0:T(8,128)(2,1)S(1)}, bf16[4,32,128]{2,1,0:T(8,128)(2,1)S(1)}, u32[]{:S(2)}, u32[]{:S(2)}) %collective-permute-start.12) | collective-permute-done | bytes 32800 | tf_op jit(solution)/shard_map/ppermute | solution.py:270
  78.2 2.9 %collective-permute-done.13 = bf16[4,32,128]{2,1,0:T(8,128)(2,1)S(1)} collective-permute-done((bf16[4,32,128]{2,1,0:T(8,128)(2,1)S(1)}, bf16[4,32,128]{2,1,0:T(8,128)(2,1)S(1)}, u32[]{:S(2)}, u32[]{:S(2)}) %collective-permute-start.13) | collective-permute-done | bytes 32800 | tf_op jit(solution)/shard_map/ppermute | solution.py:270
  81.1 1.5 %collective-permute-start.14 = (bf16[4,32,128]{2,1,0:T(8,128)(2,1)S(1)}, bf16[4,32,128]{2,1,0:T(8,128)(2,1)S(1)}, u32[]{:S(2)}, u32[]{:S(2)}) collective-permute-start(bf16[4,32,128]{2,1,0:T(8,128)(2,1)S(1)} %add_convert_fusion), channel_id=1, source_target_pairs={{0,8},{8,0},{16,24},{24,16},{1,9},{9,1},{17,25},{25,17},{2,10},{10... | collective-permute-start | bytes 98312 | tf_op jit(solution)/shard_map/ppermute | solution.py:274
  82.6 0.3 collective-permute-start.15
  82.9 0.9 collective-permute-start.16
  83.8 0.4 collective-permute-done.14
  84.2 1.1 collective-permute-done.15
  85.3 1.2 %collective-permute-done.16 = bf16[4,32,128]{2,1,0:T(8,128)(2,1)S(1)} collective-permute-done((bf16[4,32,128]{2,1,0:T(8,128)(2,1)S(1)}, bf16[4,32,128]{2,1,0:T(8,128)(2,1)S(1)}, u32[]{:S(2)}, u32[]{:S(2)}) %collective-permute-start.16) | collective-permute-done | bytes 32800 | tf_op jit(solution)/shard_map/ppermute | solution.py:274
  86.6 5.3 %collective-permute-start.17 = (bf16[4,4,32,128]{3,2,1,0:T(8,128)(2,1)S(1)}, bf16[4,4,32,128]{3,2,1,0:T(8,128)(2,1)S(1)}, u32[]{:S(2)}, u32[]{:S(2)}) collective-permute-start(bf16[4,4,32,128]{3,2,1,0:T(8,128)(2,1)S(1)} %pad_maximum_fusion), channel_id=1, source_target_pairs={{0,1},{1,0},{2,3},{3,2},{4,5},{5,4},{6,7},{7,6},{8,9},{9,8},{10,11... | collective-permute-start | bytes 393224 | tf_op jit(solution)/shard_map/ppermute | solution.py:276
  91.8 1.9 %collective-permute-start.6 = (bf16[24,2048]{1,0:T(8,128)(2,1)S(1)}, bf16[24,2048]{1,0:T(8,128)(2,1)S(1)}, u32[]{:S(2)}, u32[]{:S(2)}) collective-permute-start(bf16[24,2048]{1,0:T(8,128)(2,1)S(1)} %get-tuple-element.47), channel_id=1, source_target_pairs={{1,0},{2,1},{3,2},{4,3},{5,4},{6,5},{7,6},{9,8},{10,9},{11,10},{12... | collective-permute-start | bytes 294920 | tf_op jit(solution)/shard_map/ppermute | solution.py:361
  93.8 1.9 %collective-permute-start.5 = (bf16[24,2048]{1,0:T(8,128)(2,1)S(1)}, bf16[24,2048]{1,0:T(8,128)(2,1)S(1)}, u32[]{:S(2)}, u32[]{:S(2)}) collective-permute-start(bf16[24,2048]{1,0:T(8,128)(2,1)S(1)} %get-tuple-element.46), channel_id=1, source_target_pairs={{1,0},{2,1},{3,2},{4,3},{5,4},{6,5},{7,6},{9,8},{10,9},{11,10},{12... | collective-permute-start | bytes 294920 | tf_op jit(solution)/shard_map/ppermute | solution.py:361
  95.7 2.1 %collective-permute-done.6.refs_3_ = bf16[24,2048]{1,0:T(8,128)(2,1)S(1)} collective-permute-done((bf16[24,2048]{1,0:T(8,128)(2,1)S(1)}, bf16[24,2048]{1,0:T(8,128)(2,1)S(1)}, u32[]{:S(2)}, u32[]{:S(2)}) %collective-permute-start.6) | collective-permute-done | bytes 98336 | tf_op jit(solution)/shard_map/ppermute | solution.py:361
  97.8 1.9 %collective-permute-done.5.refs_2_ = bf16[24,2048]{1,0:T(8,128)(2,1)S(1)} collective-permute-done((bf16[24,2048]{1,0:T(8,128)(2,1)S(1)}, bf16[24,2048]{1,0:T(8,128)(2,1)S(1)}, u32[]{:S(2)}, u32[]{:S(2)}) %collective-permute-start.5) | collective-permute-done | bytes 98336 | tf_op jit(solution)/shard_map/ppermute | solution.py:361
  99.7 3.2 %features_back.5 = bf16[128,4096]{1,0:T(8,128)(2,1)} custom-call(bf16[128,2048]{1,0:T(8,128)(2,1)S(1)} %get-tuple-element.50.refs_0_, bf16[128,2048]{1,0:T(8,128)(2,1)S(1)} %get-tuple-element.51.refs_1_, bf16[24,2048]{1,0:T(8,128)(2,1)S(1)} %collective-permute-done.5.refs_2_, bf16[24,2048]{1,0:T(8,128)(2,1)S(1)} %collective-permute-done.6.refs_3_, ...), custom_call_target="tpu_custom_call" | custom-call | flops 8388608 | bytes 2097152 | tf_op jit(solution)/shard_map/features_back/pallas_call | solution.py:368
  102.9 3.2 %features_back.4 = bf16[128,4096]{1,0:T(8,128)(2,1)} custom-call(bf16[128,2048]{1,0:T(8,128)(2,1)S(1)} %get-tuple-element.48.refs_0_, bf16[128,2048]{1,0:T(8,128)(2,1)S(1)} %get-tuple-element.49.refs_1_, bf16[24,2048]{1,0:T(8,128)(2,1)S(1)} %collective-permute-done.5.refs_2_, bf16[24,2048]{1,0:T(8,128)(2,1)S(1)} %collective-permute-done.6.refs_3_, ...), custom_call_target="tpu_custom_call" | custom-call | flops 8388608 | bytes 2097152 | tf_op jit(solution)/shard_map/features_back/pallas_call | solution.py:368
  106.1 3.2 %features_back.3 = bf16[128,4096]{1,0:T(8,128)(2,1)} custom-call(bf16[128,2048]{1,0:T(8,128)(2,1)S(1)} %get-tuple-element.44.refs_0_, bf16[128,2048]{1,0:T(8,128)(2,1)S(1)} %get-tuple-element.45.refs_1_, bf16[24,2048]{1,0:T(8,128)(2,1)S(1)} %collective-permute-done.5.refs_2_, bf16[24,2048]{1,0:T(8,128)(2,1)S(1)} %collective-permute-done.6.refs_3_, ...), custom_call_target="tpu_custom_call" | custom-call | flops 8388608 | bytes 2097152 | tf_op jit(solution)/shard_map/features_back/pallas_call | solution.py:368
  109.3 0.0 collective-permute-done.17
  109.3 1.5 %unpack.1 = (f32[3,7,4096]{2,1,0:T(8,128)}, f32[256,128]{1,0:T(8,128)}, f32[1,4096]{1,0:T(1,128)}) custom-call(s32[16]{0:T(128)S(1)} %fusion.4.place_ref, s32[1]{0:T(128)} %bitcast.9.core_ref, bf16[16,32,128]{2,1,0:T(8,128)(2,1)S(1)} %bitcast.58, bf16[16,32,128]{2,1,0:T(8,128)(2,1)S(1)} %bitcast.59), custom_call_target="tpu_custom_call" | custom-call | tf_op jit(solution)/shard_map/unpack/pallas_call | solution.py:380
  (40 shorter events, 0.2 us)
Async XLA Ops:
  0.6 1.2 %copy-start = (bf16[1,128,4096]{2,1,0:T(8,128)(2,1)S(1)}, bf16[1,128,4096]{2,1,0:T(8,128)(2,1)}, u32[]{:S(2)}) copy-start(bf16[1,128,4096]{2,1,0:T(8,128)(2,1)} %param.7) | copy-start | bytes 3145732
  1.9 1.2 %copy-start.2 = (bf16[1,128,4096]{2,1,0:T(8,128)(2,1)S(1)}, bf16[1,128,4096]{2,1,0:T(8,128)(2,1)}, u32[]{:S(2)}) copy-start(bf16[1,128,4096]{2,1,0:T(8,128)(2,1)} %param.8) | copy-start | bytes 3145732
  3.1 1.2 %copy-start.4 = (bf16[1,128,4096]{2,1,0:T(8,128)(2,1)S(1)}, bf16[1,128,4096]{2,1,0:T(8,128)(2,1)}, u32[]{:S(2)}) copy-start(bf16[1,128,4096]{2,1,0:T(8,128)(2,1)} %param.9) | copy-start | bytes 3145732
  4.3 4.8 %copy-start.23 = (f32[7,3,4096]{2,0,1:T(8,128)S(1)}, f32[7,3,4096]{2,0,1:T(8,128)}, u32[]{:S(2)}) copy-start(f32[7,3,4096]{2,0,1:T(8,128)} %param.11) | copy-start | bytes 1032196
  4.3 7.3 %copy-start.6 = (bf16[1,128,4096]{2,1,0:T(8,128)(2,1)S(1)}, bf16[1,128,4096]{2,1,0:T(8,128)(2,1)}, u32[]{:S(2)}) copy-start(bf16[1,128,4096]{2,1,0:T(8,128)(2,1)} %param.10) | copy-start | bytes 3145732
  4.3 7.3 %collective-permute-start = (bf16[24,4096]{1,0:T(8,128)(2,1)S(1)}, bf16[24,4096]{1,0:T(8,128)(2,1)S(1)}, u32[]{:S(2)}, u32[]{:S(2)}) collective-permute-start(bf16[24,4096]{1,0:T(8,128)(2,1)S(1)} %tails.1), channel_id=1, source_target_pairs={{0,1},{1,2},{2,3},{3,4},{4,5},{5,6},{6,7},{8,9},{9,10},{10,11},{11... | collective-permute-start | bytes 589832 | tf_op jit(solution)/shard_map/ppermute | solution.py:321
  9.3 15.8 %copy-start.8 = (f32[7,3,4096]{2,1,0:T(4,128)}, f32[7,3,4096]{2,1,0:T(4,128)S(1)}, u32[]{:S(2)}) copy-start(f32[7,3,4096]{2,1,0:T(4,128)S(1)} %copy.15.taps_ref.refs_4_) | copy-start | bytes 1032196
  16.0 0.8 copy-start.16
  16.8 0.8 copy-start.18
  17.6 0.8 copy-start.20
  18.5 19.0 %collective-permute-start.3 = (bf16[128,2048]{1,0:T(8,128)(2,1)}, bf16[128,2048]{1,0:T(8,128)(2,1)}, u32[]{:S(2)}, u32[]{:S(2)}) collective-permute-start(bf16[128,2048]{1,0:T(8,128)(2,1)} %get-tuple-element.37.mix_hbm), channel_id=1, source_target_pairs={{0,1},{1,2},{2,3},{3,4},{4,5},{5,6},{6,7},{8,9},{9,10},{10,11},{11... | collective-permute-start | bytes 1572872 | tf_op jit(solution)/shard_map/ppermute | solution.py:337
  22.8 14.6 %copy-start.24 = (f32[256,128]{1,0:T(8,128)S(1)}, f32[256,128]{1,0:T(8,128)}, u32[]{:S(2)}) copy-start(f32[256,128]{1,0:T(8,128)} %param.12) | copy-start | bytes 393220
  22.9 14.7 %copy-start.1 = (bf16[1,128,4096]{2,1,0:T(8,128)(2,1)S(1)}, bf16[1,128,4096]{2,1,0:T(8,128)(2,1)}, u32[]{:S(2)}) copy-start(bf16[1,128,4096]{2,1,0:T(8,128)(2,1)} %param.7) | copy-start | bytes 3145732
  22.9 14.7 %copy-start.3 = (bf16[1,128,4096]{2,1,0:T(8,128)(2,1)S(1)}, bf16[1,128,4096]{2,1,0:T(8,128)(2,1)}, u32[]{:S(2)}) copy-start(bf16[1,128,4096]{2,1,0:T(8,128)(2,1)} %param.8) | copy-start | bytes 3145732
  22.9 14.7 %copy-start.5 = (bf16[1,128,4096]{2,1,0:T(8,128)(2,1)S(1)}, bf16[1,128,4096]{2,1,0:T(8,128)(2,1)}, u32[]{:S(2)}) copy-start(bf16[1,128,4096]{2,1,0:T(8,128)(2,1)} %param.9) | copy-start | bytes 3145732
  22.9 14.6 %collective-permute-start.4 = (bf16[128,2048]{1,0:T(8,128)(2,1)}, bf16[128,2048]{1,0:T(8,128)(2,1)}, u32[]{:S(2)}, u32[]{:S(2)}) collective-permute-start(bf16[128,2048]{1,0:T(8,128)(2,1)} %get-tuple-element.38.gf_hbm), channel_id=1, source_target_pairs={{1,0},{2,1},{3,2},{4,3},{5,4},{6,5},{7,6},{9,8},{10,9},{11,10},{12... | collective-permute-start | bytes 1572872 | tf_op jit(solution)/shard_map/ppermute | solution.py:337
  29.4 0.8 copy-start.10
  30.2 0.8 copy-start.12
  31.1 0.8 copy-start.14
  31.9 22.3 %collective-permute-start.1 = (bf16[128,2048]{1,0:T(8,128)(2,1)}, bf16[128,2048]{1,0:T(8,128)(2,1)}, u32[]{:S(2)}, u32[]{:S(2)}) collective-permute-start(bf16[128,2048]{1,0:T(8,128)(2,1)} %get-tuple-element.32.mix_hbm), channel_id=1, source_target_pairs={{0,1},{1,2},{2,3},{3,4},{4,5},{5,6},{6,7},{8,9},{9,10},{10,11},{11... | collective-permute-start | bytes 1572872 | tf_op jit(solution)/shard_map/ppermute | solution.py:337
  35.5 18.7 %collective-permute-start.2 = (bf16[128,2048]{1,0:T(8,128)(2,1)}, bf16[128,2048]{1,0:T(8,128)(2,1)}, u32[]{:S(2)}, u32[]{:S(2)}) collective-permute-start(bf16[128,2048]{1,0:T(8,128)(2,1)} %get-tuple-element.33.gf_hbm), channel_id=1, source_target_pairs={{1,0},{2,1},{3,2},{4,3},{5,4},{6,5},{7,6},{9,8},{10,9},{11,10},{12... | collective-permute-start | bytes 1572872 | tf_op jit(solution)/shard_map/ppermute | solution.py:337
  37.5 0.7 copy-start.22
  38.2 1.2 %copy-start.7 = (bf16[1,128,4096]{2,1,0:T(8,128)(2,1)S(1)}, bf16[1,128,4096]{2,1,0:T(8,128)(2,1)}, u32[]{:S(2)}) copy-start(bf16[1,128,4096]{2,1,0:T(8,128)(2,1)} %param.10) | copy-start | bytes 3145732
  39.4 1.0 copy-start.17
  40.4 1.0 copy-start.19
  41.5 1.0 copy-start.21
  42.5 11.7 %copy-start.11 = (bf16[128,2048]{1,0:T(8,128)(2,1)S(1)}, bf16[128,2048]{1,0:T(8,128)(2,1)}, u32[]{:S(2)}) copy-start(bf16[128,2048]{1,0:T(8,128)(2,1)} %copy-done.10) | copy-start | bytes 1572868
  42.5 11.7 %copy-start.13 = (bf16[128,2048]{1,0:T(8,128)(2,1)S(1)}, bf16[128,2048]{1,0:T(8,128)(2,1)}, u32[]{:S(2)}) copy-start(bf16[128,2048]{1,0:T(8,128)(2,1)} %copy-done.12) | copy-start | bytes 1572868
  42.5 11.7 %copy-start.15 = (bf16[128,2048]{1,0:T(8,128)(2,1)S(1)}, bf16[128,2048]{1,0:T(8,128)(2,1)}, u32[]{:S(2)}) copy-start(bf16[128,2048]{1,0:T(8,128)(2,1)} %copy-done.14) | copy-start | bytes 1572868
  65.9 1.4 %collective-permute-start.7 = (bf16[4,4,32,128]{3,2,1,0:T(8,128)(2,1)S(1)}, bf16[4,4,32,128]{3,2,1,0:T(8,128)(2,1)S(1)}, u32[]{:S(2)}, u32[]{:S(2)}) collective-permute-start(bf16[4,4,32,128]{3,2,1,0:T(8,128)(2,1)S(1)} %bitcast.67), channel_id=1, source_target_pairs={{0,1},{1,0},{2,3},{3,2},{4,5},{5,4},{6,7},{7,6},{8,9},{9,8},{10,11... | collective-permute-start | bytes 393224 | tf_op jit(solution)/shard_map/ppermute | solution.py:259
  67.3 32.4 %copy-start.9 = (f32[7,3,4096]{2,1,0:T(4,128)S(1)}, f32[7,3,4096]{2,1,0:T(4,128)}, u32[]{:S(2)}) copy-start(f32[7,3,4096]{2,1,0:T(4,128)} %copy-done.8) | copy-start | bytes 1032196
  67.4 3.7 %collective-permute-start.10 = (bf16[4,32,128]{2,1,0:T(8,128)(2,1)S(1)}, bf16[4,32,128]{2,1,0:T(8,128)(2,1)S(1)}, u32[]{:S(2)}, u32[]{:S(2)}) collective-permute-start(bf16[4,32,128]{2,1,0:T(8,128)(2,1)S(1)} %get-tuple-element.62), channel_id=1, source_target_pairs={{0,24},{8,16},{16,8},{24,0},{1,25},{9,17},{17,9},{25,1},{2,26},{10... | collective-permute-start | bytes 98312 | tf_op jit(solution)/shard_map/ppermute | solution.py:263
  69.6 2.8 %collective-permute-start.8 = (bf16[4,32,128]{2,1,0:T(8,128)(2,1)S(1)}, bf16[4,32,128]{2,1,0:T(8,128)(2,1)S(1)}, u32[]{:S(2)}, u32[]{:S(2)}) collective-permute-start(bf16[4,32,128]{2,1,0:T(8,128)(2,1)S(1)} %get-tuple-element.61), channel_id=1, source_target_pairs={{0,8},{8,0},{16,24},{24,16},{1,9},{9,1},{17,25},{25,17},{2,10},{10... | collective-permute-start | bytes 98312 | tf_op jit(solution)/shard_map/ppermute | solution.py:263
  69.8 2.8 %collective-permute-start.9 = (bf16[4,32,128]{2,1,0:T(8,128)(2,1)S(1)}, bf16[4,32,128]{2,1,0:T(8,128)(2,1)S(1)}, u32[]{:S(2)}, u32[]{:S(2)}) collective-permute-start(bf16[4,32,128]{2,1,0:T(8,128)(2,1)S(1)} %get-tuple-element.63), channel_id=1, source_target_pairs={{0,16},{8,24},{16,0},{24,8},{1,17},{9,25},{17,1},{25,9},{2,18},{10... | collective-permute-start | bytes 98312 | tf_op jit(solution)/shard_map/ppermute | solution.py:263
  72.6 3.9 %collective-permute-start.11 = (bf16[4,32,128]{2,1,0:T(8,128)(2,1)S(1)}, bf16[4,32,128]{2,1,0:T(8,128)(2,1)S(1)}, u32[]{:S(2)}, u32[]{:S(2)}) collective-permute-start(bf16[4,32,128]{2,1,0:T(8,128)(2,1)S(1)} %fusion.3), channel_id=1, source_target_pairs={{0,2},{1,3},{2,0},{3,1},{4,6},{5,7},{6,4},{7,5},{8,10},{9,11},{10,... | collective-permute-start | bytes 98312 | tf_op jit(solution)/shard_map/ppermute | solution.py:270
  74.2 4.0 %collective-permute-start.12 = (bf16[4,32,128]{2,1,0:T(8,128)(2,1)S(1)}, bf16[4,32,128]{2,1,0:T(8,128)(2,1)S(1)}, u32[]{:S(2)}, u32[]{:S(2)}) collective-permute-start(bf16[4,32,128]{2,1,0:T(8,128)(2,1)S(1)} %fusion.3), channel_id=1, source_target_pairs={{0,4},{1,5},{2,6},{3,7},{4,0},{5,1},{6,2},{7,3},{8,12},{9,13},{10,... | collective-permute-start | bytes 98312 | tf_op jit(solution)/shard_map/ppermute | solution.py:270
  76.5 4.6 %collective-permute-start.13 = (bf16[4,32,128]{2,1,0:T(8,128)(2,1)S(1)}, bf16[4,32,128]{2,1,0:T(8,128)(2,1)S(1)}, u32[]{:S(2)}, u32[]{:S(2)}) collective-permute-start(bf16[4,32,128]{2,1,0:T(8,128)(2,1)S(1)} %fusion.3), channel_id=1, source_target_pairs={{0,6},{1,7},{2,4},{3,5},{4,2},{5,3},{6,0},{7,1},{8,14},{9,15},{10,... | collective-permute-start | bytes 98312 | tf_op jit(solution)/shard_map/ppermute | solution.py:270
  81.1 3.1 %collective-permute-start.14 = (bf16[4,32,128]{2,1,0:T(8,128)(2,1)S(1)}, bf16[4,32,128]{2,1,0:T(8,128)(2,1)S(1)}, u32[]{:S(2)}, u32[]{:S(2)}) collective-permute-start(bf16[4,32,128]{2,1,0:T(8,128)(2,1)S(1)} %add_convert_fusion), channel_id=1, source_target_pairs={{0,8},{8,0},{16,24},{24,16},{1,9},{9,1},{17,25},{25,17},{2,10},{10... | collective-permute-start | bytes 98312 | tf_op jit(solution)/shard_map/ppermute | solution.py:274
  82.6 2.8 %collective-permute-start.15 = (bf16[4,32,128]{2,1,0:T(8,128)(2,1)S(1)}, bf16[4,32,128]{2,1,0:T(8,128)(2,1)S(1)}, u32[]{:S(2)}, u32[]{:S(2)}) collective-permute-start(bf16[4,32,128]{2,1,0:T(8,128)(2,1)S(1)} %add_convert_fusion), channel_id=1, source_target_pairs={{0,16},{8,24},{16,0},{24,8},{1,17},{9,25},{17,1},{25,9},{2,18},{10... | collective-permute-start | bytes 98312 | tf_op jit(solution)/shard_map/ppermute | solution.py:274
  82.9 3.7 %collective-permute-start.16 = (bf16[4,32,128]{2,1,0:T(8,128)(2,1)S(1)}, bf16[4,32,128]{2,1,0:T(8,128)(2,1)S(1)}, u32[]{:S(2)}, u32[]{:S(2)}) collective-permute-start(bf16[4,32,128]{2,1,0:T(8,128)(2,1)S(1)} %add_convert_fusion), channel_id=1, source_target_pairs={{0,24},{8,16},{16,8},{24,0},{1,25},{9,17},{17,9},{25,1},{2,26},{10... | collective-permute-start | bytes 98312 | tf_op jit(solution)/shard_map/ppermute | solution.py:274
  86.6 22.7 %collective-permute-start.17 = (bf16[4,4,32,128]{3,2,1,0:T(8,128)(2,1)S(1)}, bf16[4,4,32,128]{3,2,1,0:T(8,128)(2,1)S(1)}, u32[]{:S(2)}, u32[]{:S(2)}) collective-permute-start(bf16[4,4,32,128]{3,2,1,0:T(8,128)(2,1)S(1)} %pad_maximum_fusion), channel_id=1, source_target_pairs={{0,1},{1,0},{2,3},{3,2},{4,5},{5,4},{6,7},{7,6},{8,9},{9,8},{10,11... | collective-permute-start | bytes 393224 | tf_op jit(solution)/shard_map/ppermute | solution.py:276
  91.8 5.9 %collective-permute-start.6 = (bf16[24,2048]{1,0:T(8,128)(2,1)S(1)}, bf16[24,2048]{1,0:T(8,128)(2,1)S(1)}, u32[]{:S(2)}, u32[]{:S(2)}) collective-permute-start(bf16[24,2048]{1,0:T(8,128)(2,1)S(1)} %get-tuple-element.47), channel_id=1, source_target_pairs={{1,0},{2,1},{3,2},{4,3},{5,4},{6,5},{7,6},{9,8},{10,9},{11,10},{12... | collective-permute-start | bytes 294920 | tf_op jit(solution)/shard_map/ppermute | solution.py:361
  93.8 5.9 %collective-permute-start.5 = (bf16[24,2048]{1,0:T(8,128)(2,1)S(1)}, bf16[24,2048]{1,0:T(8,128)(2,1)S(1)}, u32[]{:S(2)}, u32[]{:S(2)}) collective-permute-start(bf16[24,2048]{1,0:T(8,128)(2,1)S(1)} %get-tuple-element.46), channel_id=1, source_target_pairs={{1,0},{2,1},{3,2},{4,3},{5,4},{6,5},{7,6},{9,8},{10,9},{11,10},{12... | collective-permute-start | bytes 294920 | tf_op jit(solution)/shard_map/ppermute | solution.py:361

commit v3 on v2

v3 whole, which is shorter than its diff:
```python
import functools

import jax
import jax.numpy as jnp
from jax import lax
from jax.experimental import pallas as pl
from jax.experimental.pallas import tpu as pltpu
from jax.sharding import PartitionSpec as P

LANES = 128
HALO = 8
TILES = 4
WIDE = TILES * LANES
SHARE = 32
VMEM = 44 * 1024 * 1024
MEDIUM = 24 * 1024 * 1024
AHEAD = 4
SMALL = 4 * 1024 * 1024
F32, BF16 = jnp.float32, jnp.bfloat16
HBM = pl.BlockSpec(memory_space=pltpu.HBM)
WHOLE = pl.BlockSpec(memory_space=pltpu.VMEM)


def odd_core():
    return lax.rem(lax.axis_index("ctx"), 2)


def dp_position():
    return lax.axis_index("dp")


def lanes_at(first, width=LANES):
    if isinstance(first, int):
        return pl.ds(first, width)
    return pl.ds(pl.multiple_of(first, LANES), width)


def stream(pieces, ahead, sources, stores, in_sem, out_sem, work):
    def launch(ref, copy):
        if isinstance(ref, tuple):
            for odd in range(2):
                @pl.when(odd_core() == odd)
                def _():
                    copy(ref[odd]).start()
        else:
            copy(ref).start()

    def one_of(ref):
        return ref[0] if isinstance(ref, tuple) else ref

    def fetch(index, piece, ref):
        _, first, buffer = sources[index]
        return pltpu.make_async_copy(
            ref.at[:, lanes_at(first + piece * WIDE, WIDE)],
            buffer.at[:, lanes_at(piece * WIDE, WIDE)], in_sem.at[index, piece])

    def store(index, piece, ref):
        buffer, _, first = stores[index]
        return pltpu.make_async_copy(
            buffer.at[:, lanes_at(piece * WIDE, WIDE)],
            ref.at[:, lanes_at(first + piece * WIDE, WIDE)], out_sem.at[index, piece])

    def begin(piece):
        for index, (ref, _, _) in enumerate(sources):
            launch(ref, functools.partial(fetch, index, piece))

    def step(piece, carry):
        if ahead < pieces:
            @pl.when(piece + ahead < pieces)
            def _():
                begin(piece + ahead)

        for index, (ref, _, _) in enumerate(sources):
            fetch(index, piece, one_of(ref)).wait()
        work(piece)
        for index, (_, ref, _) in enumerate(stores):
            launch(ref, functools.partial(store, index, piece))
        return carry

    def end(piece, carry):
        for index, (_, ref, _) in enumerate(stores):
            store(index, piece, one_of(ref)).wait()
        return carry

    for piece in range(min(ahead, pieces)):
        begin(piece)
    lax.fori_loop(0, pieces, step, 0)
    lax.fori_loop(0, pieces, end, 0)


def per_tile(piece, unroll, one):
    def run(index, carry):
        one(piece * TILES + index)
        return carry

    lax.fori_loop(0, TILES, run, 0, unroll=unroll)


def tails_kernel(rows, q_hbm, k_hbm, v_hbm, out_ref, buffer, sem):
    copies = [pltpu.make_async_copy(ref.at[pl.ds(rows - 2 * HALO, 2 * HALO), :], buffer.at[index], sem.at[index])
              for index, ref in enumerate((q_hbm, k_hbm, v_hbm))]
    for copy in copies:
        copy.start()
    for copy in copies:
        copy.wait()
    out_ref[...] = jnp.concatenate([buffer[index].astype(F32)[HALO:] for index in range(3)], axis=0).astype(BF16)


def feat_kernel(first, rows, taps_count, pieces, q_hbm, k_hbm, v_hbm, cot_hbm, tail_ref, taps_ref, near_hbm, far_hbm,
                qf_hbm, kf_hbm, vf_hbm, *scratch):
    q_ref, k_ref, v_ref, cot_ref, mix_ref, gf_ref, qf_ref, kf_ref, vf_ref, ext, in_sem, out_sem = scratch

    def one(tile):
        lanes = lanes_at(tile * LANES)
        far = lanes_at(first + tile * LANES)
        tails = tail_ref[:, far].astype(F32)
        feats = []
        for which, src in enumerate((q_ref, k_ref, v_ref)):
            ext[which, pl.ds(0, HALO), :] = tails[which * HALO:(which + 1) * HALO]
            ext[which, pl.ds(HALO, rows), :] = src[:, lanes].astype(F32)
            total = None
            for lag in range(taps_count):
                term = taps_ref[lag, which:which + 1, far] * ext[which, pl.ds(HALO - lag, rows), :]
                total = term if total is None else total + term
            feats.append(total)
        qf_ref[:, lanes] = feats[0].astype(BF16)
        kf_ref[:, lanes] = feats[1].astype(BF16)
        vf_ref[:, lanes] = feats[2].astype(BF16)
        mix_ref[:, lanes] = (feats[1] * feats[2]).astype(BF16)
        gf_ref[:, lanes] = (cot_ref[:, lanes].astype(F32) * feats[0]).astype(BF16)

    stream(pieces, pieces,
           [(q_hbm, first, q_ref), (k_hbm, first, k_ref), (v_hbm, first, v_ref), (cot_hbm, first, cot_ref)],
           [(mix_ref, (near_hbm, far_hbm), 0), (gf_ref, (far_hbm, near_hbm), 0), (qf_ref, qf_hbm, 0),
            (kf_ref, kf_hbm, 0), (vf_ref, vf_hbm, 0)],
           in_sem, out_sem, lambda piece: per_tile(piece, 1, one))


def in_hbm(*arrays):
    return [pltpu.with_memory_space_constraint(array, pltpu.HBM) for array in arrays]


def turned(size):
    row = lax.broadcasted_iota(jnp.int32, (size, size), 0)
    col = lax.broadcasted_iota(jnp.int32, (size, size), 1)
    return jnp.where(lax.rem(row + col, size) == 0, 1.0, 0.0).astype(BF16)


def mix_kernel(first, rows, taps_count, pieces, ahead, per_group, dp_count, q_hbm, k_hbm, v_hbm, cot_hbm, tail_ref,
                near_hbm, far_hbm, qf_hbm, kf_hbm, vf_hbm, got_near_hbm, got_far_hbm, filt_ref, gain_ref,
               *rest):
    if first:
        rest = rest[2:]
    out_hbm, head_ref, gq_hbm, gk_hbm, gv_hbm, grad_ref = rest[:6]
    (q_ref, k_ref, v_ref, cot_ref, mix_ref, gf_ref, qf_ref, kf_ref, vf_ref, prev_ref, next_ref,
     out_ref, gq_ref, gk_ref, gv_ref, rev_ref, ext, part, in_sem, out_sem) = rest[6:]
    half = rows // 2
    groups = LANES // per_group
    row_id = lax.broadcasted_iota(jnp.int32, (half, LANES), 0)
    lane_id = lax.broadcasted_iota(jnp.int32, (half, LANES), 1)
    wide_group = lax.broadcasted_iota(jnp.int32, (half, 2 * LANES), 1) % LANES // per_group
    later = lane_id > row_id
    early = lane_id < row_id
    zero = jnp.zeros((half, LANES), F32)
    tiles = pieces * TILES
    base = first // per_group
    in_quarter = tiles // dp_count
    rev_ref[...] = jnp.dot(filt_ref[pl.ds(base, rev_ref.shape[0]), :].astype(BF16), turned(filt_ref.shape[1]),
                           preferred_element_type=F32)

    def one(tile):
        lanes = lanes_at(tile * LANES)
        far = lanes_at(first + tile * LANES)
        mix = mix_ref[:, lanes]
        prev = prev_ref[:, lanes]
        gf = gf_ref[:, lanes]
        nxt = next_ref[:, lanes]
        before = jnp.concatenate([
            jnp.concatenate([prev, mix], axis=0),
            jnp.concatenate([prev[half:], mix, mix[:half]], axis=0)], axis=1)
        after = jnp.concatenate([
            jnp.concatenate([gf, nxt], axis=0),
            jnp.concatenate([gf[half:], nxt, nxt[:half]], axis=0)], axis=1)
        gf_wide = jnp.concatenate([gf[:half], gf[half:]], axis=1)
        rev = rev_ref[pl.ds(pl.multiple_of(tile * groups, groups), groups), :]
        fwd = filt_ref[pl.ds(pl.multiple_of(base + tile * groups, groups), groups), :].astype(BF16).astype(F32)
        firsts, seconds, masked = [], [], []
        for group in range(groups):
            circ = pltpu.roll(jnp.broadcast_to(rev[group:group + 1], (half, LANES)), 0, 1,
                              stride=1, stride_axis=0)
            firsts.append(jnp.concatenate(
                [jnp.where(later, circ, zero), jnp.where(later, zero, circ)], axis=1).astype(BF16))
            circ = pltpu.roll(jnp.broadcast_to(fwd[group:group + 1], (half, LANES)), 0, 1,
                              stride=1, stride_axis=0)
            seconds.append(jnp.concatenate(
                [jnp.where(early, zero, circ), jnp.where(early, circ, zero)], axis=1).astype(BF16))
            masked.append(jnp.where(wide_group == group, gf_wide, jnp.zeros_like(gf_wide)))

        def filtered_by(matrices, window):
            found = jnp.dot(jnp.concatenate(matrices, axis=0), window, preferred_element_type=F32)
            picked = found[:half]
            for group in range(1, groups):
                picked = jnp.where(wide_group == group, found[group * half:(group + 1) * half], picked)
            return jnp.concatenate([picked[:, :LANES], picked[:, LANES:]], axis=0)

        conv = filtered_by(firsts, before)
        back = filtered_by(seconds, after)
        prod = lax.dot_general(jnp.concatenate(masked, axis=0), before, (((1,), (1,)), ((), ())),
                               preferred_element_type=F32)
        sums = []
        for group in range(groups):
            own = prod[group * half:(group + 1) * half]
            square = jnp.where(later, own[:, :LANES], own[:, LANES:])
            total = square[:8]
            for start in range(8, half, 8):
                total = total + pltpu.roll(square[start:start + 8], LANES - start, 1)
            sums.append(total)
        sums = jnp.concatenate(sums, axis=0)
        turn = lax.broadcasted_iota(jnp.int32, sums.shape, 0)
        for bit in (1, 2, 4):
            sums = jnp.where((turn & bit) > 0, pltpu.roll(sums, LANES - bit, 1), sums)
        part[pl.ds(SHARE - groups, groups), :] = jnp.sum(sums.reshape(groups, 8, LANES), axis=1)

        gain = gain_ref[:, far]
        mix_wide = mix.astype(F32)
        gf_f32 = gf.astype(F32)
        filtered = conv + gain * mix_wide
        grad_mix = back + gain * gf_f32
        part[pl.ds(3 * taps_count, 1), :] = jnp.sum(mix_wide * gf_f32, axis=0, keepdims=True)
        out_ref[:, lanes] = (qf_ref[:, lanes].astype(F32) * filtered).astype(BF16)
        grads = (cot_ref[:, lanes].astype(F32) * filtered, grad_mix * vf_ref[:, lanes].astype(F32),
                 grad_mix * kf_ref[:, lanes].astype(F32))
        tails = tail_ref[:, far].astype(F32)
        for which, (src, grad, dest) in enumerate(zip((q_ref, k_ref, v_ref), grads, (gq_ref, gk_ref, gv_ref))):
            dest[:, lanes] = grad.astype(BF16)
            ext[which, pl.ds(0, HALO), :] = tails[which * HALO:(which + 1) * HALO]
            ext[which, pl.ds(HALO, rows), :] = src[:, lanes].astype(F32)
            for lag in range(taps_count):
                part[pl.ds(lag * 3 + which, 1), :] = jnp.sum(
                    grad * ext[which, pl.ds(HALO - lag, rows), :], axis=0, keepdims=True)
        head_ref[:, far] = jnp.concatenate([grad[:HALO] for grad in grads], axis=0).astype(BF16)
        quarter = tile // in_quarter
        slot = (quarter ^ dp_position()) * in_quarter + lax.rem(tile, in_quarter)
        grad_ref[slot] = part[...].astype(BF16)

    part[...] = jnp.zeros(part.shape, F32)
    stream(pieces, ahead,
           [(q_hbm, first, q_ref), (k_hbm, first, k_ref), (v_hbm, first, v_ref), (cot_hbm, first, cot_ref),
            ((near_hbm, far_hbm), 0, mix_ref), ((far_hbm, near_hbm), 0, gf_ref),
            (qf_hbm, 0, qf_ref), (kf_hbm, 0, kf_ref), (vf_hbm, 0, vf_ref),
            ((got_far_hbm, got_near_hbm), 0, prev_ref), ((got_near_hbm, got_far_hbm), 0, next_ref)],
           [(out_ref, out_hbm, first), (gq_ref, gq_hbm, 0), (gk_ref, gk_hbm, 0), (gv_ref, gv_hbm, 0)],
           in_sem, out_sem, lambda piece: per_tile(piece, TILES, one))


def back_kernel(which, rows, taps_count, pieces, parts, *refs):
    grads, head_ref, taps_ref, out_hbm = refs[:parts], refs[parts], refs[parts + 1], refs[parts + 3]
    done_ref, grad_ref, out_ref, ext, in_sem, out_sem = refs[parts + 4:]
    each = pieces // parts
    done_ref[...] = jnp.zeros(done_ref.shape, F32)

    def fetch(piece):
        return pltpu.make_async_copy(grads[piece // each].at[:, pl.ds(piece % each * WIDE, WIDE)],
                                     grad_ref.at[:, pl.ds(piece * WIDE, WIDE)], in_sem.at[piece])

    def store(piece):
        lanes = pl.ds(piece * WIDE, WIDE)
        return pltpu.make_async_copy(out_ref.at[:, lanes], out_hbm.at[:, lanes], out_sem.at[piece])

    for piece in range(pieces):
        fetch(piece).start()
    for piece in range(pieces):
        def one(tile, piece=piece):
            lanes = lanes_at(tile * LANES)
            ext[pl.ds(0, rows), :] = grad_ref[:, lanes].astype(F32)
            head = head_ref[:, lanes].astype(F32)
            ext[pl.ds(rows, HALO), :] = head[which * HALO:(which + 1) * HALO]
            total = None
            for lag in range(taps_count):
                term = taps_ref[lag, which:which + 1, lanes] * ext[pl.ds(lag, rows), :]
                total = term if total is None else total + term
            out_ref[:, lanes] = total.astype(BF16)

        fetch(piece).wait()
        per_tile(piece, 1, one)
        store(piece).start()
    for piece in range(pieces):
        store(piece).wait()


def add_kernel(count, keep_ref, *refs):
    total = keep_ref[...]
    for ref in refs[:count]:
        total = total + ref[...].astype(F32)
    refs[count + 1][...] = total
    refs[count + 2][...] = total.astype(BF16)


def join_kernel(count, *refs):
    for index in range(count):
        refs[count + 1][index] = refs[index][...]


def unpack_kernel(taps_count, scale, dp_count, mine_ref, other_ref, taps_ref, filt_ref, skip_ref):
    in_half = mine_ref.shape[0]
    in_quarter = in_half // dp_count
    count = 2 * in_half
    groups = filt_ref.shape[0] // count
    flip = turned(filt_ref.shape[1])
    for tile in range(count):
        local = tile % in_half
        slot = (local // in_quarter ^ dp_position()) * in_quarter + local % in_quarter
        block = jnp.where(odd_core() == tile // in_half, mine_ref[slot].astype(F32), other_ref[slot].astype(F32))
        lanes = pl.ds(tile * LANES, LANES)
        for which in range(3):
            for lag in range(taps_count):
                row = lag * 3 + which
                taps_ref[which, lag:lag + 1, lanes] = block[row:row + 1] * scale
        skip_ref[:, lanes] = block[3 * taps_count:3 * taps_count + 1] * scale
        filt_ref[pl.ds(tile * groups, groups), :] = block[SHARE - groups:]
    filt_ref[...] = jnp.dot(filt_ref[...].astype(BF16), flip, preferred_element_type=F32) * scale


def swaps(size, mask):
    return [(i, i ^ mask) for i in range(size)]


def add(keep, arrived, after):
    return pl.pallas_call(
        functools.partial(add_kernel, len(arrived)),
        in_specs=[WHOLE] * (len(arrived) + 2),
        out_specs=[WHOLE] * 2,
        out_shape=[jax.ShapeDtypeStruct(keep.shape, F32), jax.ShapeDtypeStruct(keep.shape, BF16)],
        compiler_params=pltpu.CompilerParams(vmem_limit_bytes=SMALL),
        name="add",
    )(keep, *arrived, after)


def reduce_all(mine, theirs, ctx_count, dp_count, beside):
    half = mine.astype(F32) + lax.ppermute(theirs, "ctx", swaps(ctx_count, 1)).astype(F32)
    sent = half.astype(BF16)
    arrived = [lax.ppermute(sent[mask], "dp", swaps(dp_count, mask)) for mask in range(1, dp_count)]
    total, low = add(half[0], arrived, beside[0](sent))
    work = beside[1](low)
    mask = 2
    while mask < ctx_count:
        picks = (mask, 2 * mask, 3 * mask) if mask * 2 < ctx_count else (mask,)
        mask *= 4
        total, low = add(total, [lax.ppermute(low, "ctx", swaps(ctx_count, pick)) for pick in picks], work)
    quarters = [low] + [lax.ppermute(low, "dp", swaps(dp_count, mask)) for mask in range(1, dp_count)]
    whole = pl.pallas_call(
        functools.partial(join_kernel, dp_count),
        in_specs=[WHOLE] * (dp_count + 1),
        out_specs=WHOLE,
        out_shape=jax.ShapeDtypeStruct((dp_count,) + low.shape, BF16),
        compiler_params=pltpu.CompilerParams(vmem_limit_bytes=SMALL),
        name="join",
    )(*quarters, beside[2](low))
    return whole, lax.ppermute(whole, "ctx", swaps(ctx_count, 1))


def body(query_rows, key_rows, value_rows, cotangent, feature_taps, filter_taps, skip_gain):
    rows, channels = query_rows.shape[1:]
    taps_count = feature_taps.shape[0]
    group_count, taps_len = filter_taps.shape
    per_group = channels // group_count
    ctx_count, dp_count = lax.axis_size("ctx"), lax.axis_size("dp")
    assert rows == taps_len == LANES and taps_count <= HALO
    scale = float(dp_count * ctx_count * rows) ** (-0.5)
    parts = 2
    width = channels // parts
    pieces = width // WIDE
    in_half = width // LANES
    in_quarter = in_half // dp_count
    query, key, value, cot = query_rows[0], key_rows[0], value_rows[0], cotangent[0]
    onward = [(i, i + 1) for i in range(ctx_count - 1)]
    backward = [(i + 1, i) for i in range(ctx_count - 1)]
    gains = skip_gain.reshape(1, channels)
    def shape(height, kind, across=width):
        return jax.ShapeDtypeStruct((height, across), kind)

    def buffers(count):
        return [pltpu.VMEM((rows, width), BF16)] * count

    def sems(ins, outs):
        return [pltpu.SemaphoreType.DMA((ins, pieces)), pltpu.SemaphoreType.DMA((outs, pieces))]

    compiler_params = pltpu.CompilerParams(vmem_limit_bytes=VMEM)
    small_params = pltpu.CompilerParams(vmem_limit_bytes=MEDIUM)
    tails = pl.pallas_call(
        functools.partial(tails_kernel, rows),
        in_specs=[HBM] * 3,
        out_specs=WHOLE,
        out_shape=shape(3 * HALO, BF16, channels),
        scratch_shapes=[pltpu.VMEM((3, 2 * HALO, channels), BF16), pltpu.SemaphoreType.DMA((3,))],
        compiler_params=compiler_params,
        name="tails",
    )(*in_hbm(query, key, value))
    tails = lax.ppermute(tails, "ctx", onward)

    cores = swaps(ctx_count, 1)
    chips = [(i, i + 1) for i in range(1, ctx_count - 1, 2)] + [(i + 1, i) for i in range(1, ctx_count - 1, 2)]
    made, halos = [], []
    for part in range(parts):
        feats = pl.pallas_call(
            functools.partial(feat_kernel, part * width, rows, taps_count, pieces),
            in_specs=[HBM] * 4 + [WHOLE] * 2,
            out_specs=[HBM] * 5,
            out_shape=[pltpu.HBM((rows, width), BF16)] * 5,
            scratch_shapes=buffers(9) + [pltpu.VMEM((3, rows + HALO, LANES), F32)] + sems(4, 5),
            compiler_params=compiler_params,
            cost_estimate=pl.CostEstimate(flops=50 * rows * width, bytes_accessed=18 * rows * width, transcendentals=0),
            name="features",
        )(*in_hbm(query, key, value, cot), tails, feature_taps)
        made.append(feats)
        far = lax.ppermute(feats[1], "ctx", chips)
        halos.append((lax.ppermute(feats[0], "ctx", cores), far))

    shared = ()
    results = []
    for part in range(parts):
        found = pl.pallas_call(
            functools.partial(mix_kernel, part * width, rows, taps_count, pieces, AHEAD, per_group, dp_count),
            in_specs=[HBM] * 4 + [WHOLE] + [HBM] * 7 + [WHOLE] * 2 + ([HBM, WHOLE] if part else []),
            out_specs=[HBM, WHOLE] + [HBM] * 3 + [WHOLE],
            out_shape=[pltpu.HBM((rows, channels), BF16), shape(3 * HALO, BF16, channels)]
            + [shape(rows, BF16)] * 3
            + [jax.ShapeDtypeStruct((in_half, SHARE, LANES), BF16)],
            input_output_aliases={14: 0, 15: 1} if part else {},
            scratch_shapes=buffers(15)
            + [pltpu.VMEM((group_count // parts, taps_len), F32), pltpu.VMEM((3, rows + HALO, LANES), F32),
               pltpu.VMEM((SHARE, LANES), F32)] + sems(11, 4),
            compiler_params=compiler_params,
            cost_estimate=pl.CostEstimate(flops=2000 * rows * width, bytes_accessed=30 * rows * width,
                                          transcendentals=0),
            name="filters",
        )(*in_hbm(query, key, value, cot), tails, *in_hbm(*made[part]), *halos[part], filter_taps, gains, *shared)
        shared = found[:2]
        results.append(found[2:])

    out = shared[0]
    next_heads = lax.ppermute(shared[1], "ctx", backward)
    shares = [found[3].reshape(dp_count, in_quarter, SHARE, LANES) for found in results]
    grads = []

    def beside(which, after):
        grads.append(pl.pallas_call(
            functools.partial(back_kernel, which, rows, taps_count, parts * pieces, parts),
            in_specs=[HBM] * parts + [WHOLE] * 3,
            out_specs=[HBM, WHOLE],
            out_shape=[pltpu.HBM((rows, channels), BF16), jax.ShapeDtypeStruct((8, LANES), F32)],
            scratch_shapes=[pltpu.VMEM((rows, channels), BF16)] * 2 + [pltpu.VMEM((rows + HALO, LANES), F32)]
            + [pltpu.SemaphoreType.DMA((parts * pieces,))] * 2,
            compiler_params=small_params,
            cost_estimate=pl.CostEstimate(flops=16 * rows * channels, bytes_accessed=4 * rows * channels,
                                          transcendentals=0),
            name="features_back",
        )(*[found[which] for found in results], next_heads, feature_taps, after))
        return grads[-1][1]

    mine, other = reduce_all(
        jnp.where(odd_core() == 0, shares[0], shares[1]), jnp.where(odd_core() == 0, shares[1], shares[0]),
        ctx_count, dp_count, [functools.partial(beside, which) for which in range(3)])

    grad_taps, grad_filter, grad_skip = pl.pallas_call(
        functools.partial(unpack_kernel, taps_count, scale, dp_count),
        in_specs=[WHOLE, WHOLE],
        out_specs=[WHOLE] * 3,
        out_shape=[jax.ShapeDtypeStruct((3, taps_count, channels), F32), jax.ShapeDtypeStruct(filter_taps.shape, F32),
                   jax.ShapeDtypeStruct((1, channels), F32)],
        compiler_params=compiler_params,
        name="unpack",
    )(mine.reshape(in_half, SHARE, LANES), other.reshape(in_half, SHARE, LANES))
    return (out[None], grads[0][0][None], grads[1][0][None], grads[2][0][None], jnp.transpose(grad_taps, (1, 0, 2)),
            grad_filter, grad_skip.reshape(channels))


def solution(mesh):
    rows = P("dp", "ctx", None)
    return jax.shard_map(
        body,
        mesh=mesh,
        in_specs=(rows, rows, rows, rows, P(), P(), P()),
        out_specs=(rows, rows, rows, rows, P(), P(), P()),
        check_vma=False,
    )
```

time: 112 us -> 78.3 us (0.70)
  local copies, waits for them, and re-layouts: 13.8 us -> 0.27 us
  waiting for transfers between devices: 17.5 us -> 6.4 us
  starting transfers between devices: 35.3 us -> 27.5 us
    unnamed x51 -> x7, local copies, waits for them, and re-layouts: 13.8 us -> 0.26 us
    ppermute x15 -> x14, waiting for transfers between devices: 13.9 us -> 3.08 us  [the longest x1 1.97 us: body(): next_heads = lax.ppermute(shared[1], 'ctx', backward)]
    ppermute x15 -> x14, starting transfers between devices: 25.3 us -> 19.6 us  [the longest x2 8.11 us: body(): far = lax.ppermute(feats[1], 'ctx', chips)]
    ppermute x1, starting transfers between devices: 5.25 us -> 3.19 us  [reduce_all(): return (whole, lax.ppermute(whole, 'ctx', swaps(ctx_count, 1)))]
    ppermute x1, waiting for transfers between devices: 1.33 us -> 0.01 us  [reduce_all(): lax.ppermute(theirs, 'ctx', swaps(ctx_count, 1)).astype(F32)]
    pallas_call x2, Pallas kernels: 8.69 us -> 9.9 us  [body(): pl.pallas_call(functools.partial(feat_kernel, part * width, rows, taps_co...]
    pallas_call x5 -> x8, Pallas kernels: 11.1 us -> 10.4 us  [the longest x3 7.64 us: beside(): pl.pallas_call(functools.partial(back_kernel, which, rows, taps_count, pa...]
  transfers between devices with their start and end apart: 18 -> 17, of which waited for: 12 -> 5; matrix products, arithmetic and copies ran while one was open for 0% -> 0% of each run, Pallas kernels for 23% -> 30%
where the time goes in v3:
time: 78.3 us; the launch traced here: 77.7 us
  Pallas kernels  42.5 us (54%)
  starting transfers between devices  27.5 us (35%)
  waiting for transfers between devices  6.4 us (8%)
  between operations  0.95 us (1%)
    pallas_call x2, Pallas kernels, body(): pl.pallas_call(functools.partial(mix_kernel, part * width, rows, taps_cou...  22.1 us
    pallas_call x2, Pallas kernels, body(): pl.pallas_call(functools.partial(feat_kernel, part * width, rows, taps_co...  9.9 us
    ppermute x2, starting transfers between devices, body(): far = lax.ppermute(feats[1], 'ctx', chips)  8.11 us
    pallas_call x3, Pallas kernels, beside(): pl.pallas_call(functools.partial(back_kernel, which, rows, taps_count, pa...  7.64 us
    ppermute x1, starting transfers between devices, body(): tails = lax.ppermute(tails, 'ctx', onward)  4.59 us
    ppermute x3, starting transfers between devices, reduce_all(): lax.ppermute(low, 'ctx', swaps(ctx_count, pick))  3.64 us
    ppermute x1, starting transfers between devices, reduce_all(): return (whole, lax.ppermute(whole, 'ctx', swaps(ctx_count, 1)))  3.19 us
    ppermute x3, starting transfers between devices, reduce_all(): lax.ppermute(sent[mask], 'dp', swaps(dp_count, mask))  2.71 us
  transfers between devices with their start and end apart: 17, of which 5 were waited for; matrix products, arithmetic and copies ran while one was open for 0% of the time, Pallas kernels for 30%

profile of v3, /device:TPU:1, one launch (start us, length us, event | category | flops | bytes accessed | tf_op | source)
XLA Modules:
  0.0 77.7 jit_solution(561009517920665051)
XLA Ops:
  0.6 0.0 copy-start.2
  0.6 1.1 %tails.1 = bf16[24,4096]{1,0:T(8,128)(2,1)S(1)} custom-call(bf16[128,4096]{1,0:T(8,128)(2,1)} %bitcast.28, bf16[128,4096]{1,0:T(8,128)(2,1)} %bitcast.33, bf16[128,4096]{1,0:T(8,128)(2,1)} %bitcast.38), custom_call_target="tpu_custom_call" | custom-call | tf_op jit(solution)/shard_map/tails/pallas_call | solution.py:390
  1.8 4.6 %collective-permute-start = (bf16[24,4096]{1,0:T(8,128)(2,1)S(1)}, bf16[24,4096]{1,0:T(8,128)(2,1)S(1)}, u32[]{:S(2)}, u32[]{:S(2)}) collective-permute-start(bf16[24,4096]{1,0:T(8,128)(2,1)S(1)} %tails.1), channel_id=1, source_target_pairs={{0,1},{1,2},{2,3},{3,4},{4,5},{5,6},{6,7},{8,9},{9,10},{10,11},{11... | collective-permute-start | bytes 589832 | tf_op jit(solution)/shard_map/ppermute | solution.py:399
  6.4 0.0 copy-done.2
  6.4 0.2 copy.16.taps_ref.refs_3_
  6.6 2.3 %collective-permute-done.tail_ref = bf16[24,4096]{1,0:T(8,128)(2,1)S(1)} collective-permute-done((bf16[24,4096]{1,0:T(8,128)(2,1)S(1)}, bf16[24,4096]{1,0:T(8,128)(2,1)S(1)}, u32[]{:S(2)}, u32[]{:S(2)}) %collective-permute-start) | collective-permute-done | bytes 196640 | tf_op jit(solution)/shard_map/ppermute | solution.py:399
  9.0 5.0 %features.3 = (bf16[128,2048]{1,0:T(8,128)(2,1)}, bf16[128,2048]{1,0:T(8,128)(2,1)}, bf16[128,2048]{1,0:T(8,128)(2,1)}, bf16[128,2048]{1,0:T(8,128)(2,1)}, bf16[128,2048]{1,0:T(8,128)(2,1)}) custom-call(bf16[128,4096]{1,0:T(8,128)(2,1)} %bitcast.29, bf16[128,4096]{1,0:T(8,128)(2,1)} %bitcast.34, bf16[128,4096]{1,0:T(8,128)(2,1)} %bitcast.39, ...), custom_call_target="tpu_custom_call" | custom-call | flops 13107200 | bytes 4718592 | tf_op jit(solution)/shard_map/features/pallas_call | solution.py:405
  13.9 0.1 collective-permute-start.3
  14.0 0.0 copy-start
  14.0 4.5 %collective-permute-start.4 = (bf16[128,2048]{1,0:T(8,128)(2,1)}, bf16[128,2048]{1,0:T(8,128)(2,1)S(1)}, u32[]{:S(2)}, u32[]{:S(2)}) collective-permute-start(bf16[128,2048]{1,0:T(8,128)(2,1)} %get-tuple-element.47.far_hbm), channel_id=1, source_target_pairs={{1,2},{3,4},{5,6},{2,1},{4,3},{6,5},{9,10},{11,12},{13,14},{10,9},... | collective-permute-start | bytes 1572872 | tf_op jit(solution)/shard_map/ppermute | solution.py:416
  18.6 5.0 %features.2 = (bf16[128,2048]{1,0:T(8,128)(2,1)}, bf16[128,2048]{1,0:T(8,128)(2,1)}, bf16[128,2048]{1,0:T(8,128)(2,1)}, bf16[128,2048]{1,0:T(8,128)(2,1)}, bf16[128,2048]{1,0:T(8,128)(2,1)}) custom-call(bf16[128,4096]{1,0:T(8,128)(2,1)} %bitcast.30, bf16[128,4096]{1,0:T(8,128)(2,1)} %bitcast.35, bf16[128,4096]{1,0:T(8,128)(2,1)} %bitcast.40, ...), custom_call_target="tpu_custom_call" | custom-call | flops 13107200 | bytes 4718592 | tf_op jit(solution)/shard_map/features/pallas_call | solution.py:405
  23.5 0.0 copy-start.1
  23.5 0.1 collective-permute-start.1
  23.6 3.6 %collective-permute-start.2 = (bf16[128,2048]{1,0:T(8,128)(2,1)}, bf16[128,2048]{1,0:T(8,128)(2,1)S(1)}, u32[]{:S(2)}, u32[]{:S(2)}) collective-permute-start(bf16[128,2048]{1,0:T(8,128)(2,1)} %get-tuple-element.42.far_hbm), channel_id=1, source_target_pairs={{1,2},{3,4},{5,6},{2,1},{4,3},{6,5},{9,10},{11,12},{13,14},{10,9},... | collective-permute-start | bytes 1572872 | tf_op jit(solution)/shard_map/ppermute | solution.py:416
  27.2 0.0 collective-permute-done.3.got_near_hbm
  27.2 0.0 collective-permute-done.4.got_far_hbm
  27.2 0.0 copy-done
  27.2 0.0 copy-done.1
  27.2 11.1 %filters.2 = (bf16[128,4096]{1,0:T(8,128)(2,1)}, bf16[24,4096]{1,0:T(8,128)(2,1)S(1)}, bf16[128,2048]{1,0:T(8,128)(2,1)S(1)}, bf16[128,2048]{1,0:T(8,128)(2,1)S(...) custom-call(bf16[128,4096]{1,0:T(8,128)(2,1)} %bitcast.31, bf16[128,4096]{1,0:T(8,128)(2,1)} %bitcast.36, ...), custom_call_target="tpu_custom_call" | custom-call | flops 524288000 | bytes 7864320 | tf_op jit(solution)/shard_map/filters/pallas_call | solution.py:422
  38.3 0.0 collective-permute-done.1.got_near_hbm
  38.3 0.0 collective-permute-done.2.got_far_hbm
  38.3 11.1 %filters.3 = (bf16[128,4096]{1,0:T(8,128)(2,1)}, bf16[24,4096]{1,0:T(8,128)(2,1)S(1)}, bf16[128,2048]{1,0:T(8,128)(2,1)S(1)}, bf16[128,2048]{1,0:T(8,128)(2,1)S(...) custom-call(bf16[128,4096]{1,0:T(8,128)(2,1)} %bitcast.32, ...), custom_call_target="tpu_custom_call", output_to_operand_aliasing={{0}: (14, {}), {1}: (15, {})} | custom-call | flops 524288000 | bytes 7864320 | tf_op jit(solution)/shard_map/filters/pallas_call | solution.py:422
  49.4 0.1 collective-permute-start.6
  49.5 2.4 %collective-permute-start.5 = (bf16[24,4096]{1,0:T(8,128)(2,1)S(1)}, bf16[24,4096]{1,0:T(8,128)(2,1)S(1)}, u32[]{:S(2)}, u32[]{:S(2)}) collective-permute-start(bf16[24,4096]{1,0:T(8,128)(2,1)S(1)} %get-tuple-element.56), channel_id=1, source_target_pairs={{1,0},{2,1},{3,2},{4,3},{5,4},{6,5},{7,6},{9,8},{10,9},{11,10},{12... | collective-permute-start | bytes 589832 | tf_op jit(solution)/shard_map/ppermute | solution.py:442
  51.9 0.0 collective-permute-done.6
  52.0 1.3 %collective-permute-start.7 = (bf16[4,32,128]{2,1,0:T(8,128)(2,1)S(1)}, bf16[4,32,128]{2,1,0:T(8,128)(2,1)S(1)}, u32[]{:S(2)}, u32[]{:S(2)}) collective-permute-start(bf16[4,32,128]{2,1,0:T(8,128)(2,1)S(1)} %get-tuple-element.81), channel_id=1, source_target_pairs={{0,8},{8,0},{16,24},{24,16},{1,9},{9,1},{17,25},{25,17},{2,10},{10... | collective-permute-start | bytes 98312 | tf_op jit(solution)/shard_map/ppermute | solution.py:342
  53.3 1.3 %collective-permute-start.8 = (bf16[4,32,128]{2,1,0:T(8,128)(2,1)S(1)}, bf16[4,32,128]{2,1,0:T(8,128)(2,1)S(1)}, u32[]{:S(2)}, u32[]{:S(2)}) collective-permute-start(bf16[4,32,128]{2,1,0:T(8,128)(2,1)S(1)} %get-tuple-element.80), channel_id=1, source_target_pairs={{0,16},{8,24},{16,0},{24,8},{1,17},{9,25},{17,1},{25,9},{2,18},{10... | collective-permute-start | bytes 98312 | tf_op jit(solution)/shard_map/ppermute | solution.py:342
  54.5 0.2 collective-permute-start.9
  54.7 2.0 %collective-permute-done.5.refs_2_ = bf16[24,4096]{1,0:T(8,128)(2,1)S(1)} collective-permute-done((bf16[24,4096]{1,0:T(8,128)(2,1)S(1)}, bf16[24,4096]{1,0:T(8,128)(2,1)S(1)}, u32[]{:S(2)}, u32[]{:S(2)}) %collective-permute-start.5) | collective-permute-done | bytes 196640 | tf_op jit(solution)/shard_map/ppermute | solution.py:442
  56.7 2.5 %features_back.3 = (bf16[128,4096]{1,0:T(8,128)(2,1)}, f32[8,128]{1,0:T(8,128)S(1)}) custom-call(bf16[128,2048]{1,0:T(8,128)(2,1)S(1)} %get-tuple-element.54.refs_0_, bf16[128,2048]{1,0:T(8,128)(2,1)S(1)} %get-tuple-element.55.refs_1_, bf16[24,4096]{1,0:T(8,128)(2,1)S(1)} %collective-permute-done.5.refs_2_, f32[7,3,4096]{2,1,0:T(4,128)S(1)} %copy.16.taps_ref.refs_3_, ...), custom_call_target="tpu_custom_call" | custom-call | flops 8388608 | bytes 2097152 | tf_op jit(solution)/shard_map/features_back/pallas_call | solution.py:447
  59.2 0.0 collective-permute-done.7.refs_0_
  59.2 0.0 collective-permute-done.8.refs_1_
  59.3 0.0 collective-permute-done.9.refs_2_
  59.3 1.5 %collective-permute-start.10 = (bf16[4,32,128]{2,1,0:T(8,128)(2,1)S(1)}, bf16[4,32,128]{2,1,0:T(8,128)(2,1)S(1)}, u32[]{:S(2)}, u32[]{:S(2)}) collective-permute-start(bf16[4,32,128]{2,1,0:T(8,128)(2,1)S(1)} %get-tuple-element.63.refs_4_), channel_id=1, source_target_pairs={{0,2},{1,3},{2,0},{3,1},{4,6},{5,7},{6,4},{7,5},{8,10},{9,11},{10,... | collective-permute-start | bytes 98312 | tf_op jit(solution)/shard_map/ppermute | solution.py:349
  60.8 0.0 collective-permute-start.11
  60.8 2.2 %collective-permute-start.12 = (bf16[4,32,128]{2,1,0:T(8,128)(2,1)S(1)}, bf16[4,32,128]{2,1,0:T(8,128)(2,1)S(1)}, u32[]{:S(2)}, u32[]{:S(2)}) collective-permute-start(bf16[4,32,128]{2,1,0:T(8,128)(2,1)S(1)} %get-tuple-element.63.refs_4_), channel_id=1, source_target_pairs={{0,6},{1,7},{2,4},{3,5},{4,2},{5,3},{6,0},{7,1},{8,14},{9,15},{10,... | collective-permute-start | bytes 98312 | tf_op jit(solution)/shard_map/ppermute | solution.py:349
  62.9 2.6 %features_back.4 = (bf16[128,4096]{1,0:T(8,128)(2,1)}, f32[8,128]{1,0:T(8,128)S(1)}) custom-call(bf16[128,2048]{1,0:T(8,128)(2,1)S(1)} %get-tuple-element.60.refs_0_, bf16[128,2048]{1,0:T(8,128)(2,1)S(1)} %get-tuple-element.61.refs_1_, bf16[24,4096]{1,0:T(8,128)(2,1)S(1)} %collective-permute-done.5.refs_2_, f32[7,3,4096]{2,1,0:T(4,128)S(1)} %copy.16.taps_ref.refs_3_, ...), custom_call_target="tpu_custom_call" | custom-call | flops 8388608 | bytes 2097152 | tf_op jit(solution)/shard_map/features_back/pallas_call | solution.py:447
  65.5 0.0 collective-permute-done.10.refs_0_
  65.5 0.0 collective-permute-done.11.refs_1_
  65.5 0.3 collective-permute-done.12.refs_2_
  65.8 0.6 add.10
  66.4 0.8 %collective-permute-start.13 = (bf16[4,32,128]{2,1,0:T(8,128)(2,1)S(1)}, bf16[4,32,128]{2,1,0:T(8,128)(2,1)S(1)}, u32[]{:S(2)}, u32[]{:S(2)}) collective-permute-start(bf16[4,32,128]{2,1,0:T(8,128)(2,1)S(1)} %get-tuple-element.69.refs_4_.refs_0_), channel_id=1, source_target_pairs={{0,8},{8,0},{16,24},{24,16},{1,9},{9,1},{17,25},{25,17},{2,10},{10... | collective-permute-start | bytes 98312 | tf_op jit(solution)/shard_map/ppermute | solution.py:350
  67.2 1.5 %collective-permute-start.14 = (bf16[4,32,128]{2,1,0:T(8,128)(2,1)S(1)}, bf16[4,32,128]{2,1,0:T(8,128)(2,1)S(1)}, u32[]{:S(2)}, u32[]{:S(2)}) collective-permute-start(bf16[4,32,128]{2,1,0:T(8,128)(2,1)S(1)} %get-tuple-element.69.refs_4_.refs_0_), channel_id=1, source_target_pairs={{0,16},{8,24},{16,0},{24,8},{1,17},{9,25},{17,1},{25,9},{2,18},{10... | collective-permute-start | bytes 98312 | tf_op jit(solution)/shard_map/ppermute | solution.py:350
  68.7 0.4 collective-permute-start.15
  69.1 2.5 %features_back.5 = (bf16[128,4096]{1,0:T(8,128)(2,1)}, f32[8,128]{1,0:T(8,128)S(1)}) custom-call(bf16[128,2048]{1,0:T(8,128)(2,1)S(1)} %get-tuple-element.65.refs_0_, bf16[128,2048]{1,0:T(8,128)(2,1)S(1)} %get-tuple-element.66.refs_1_, bf16[24,4096]{1,0:T(8,128)(2,1)S(1)} %collective-permute-done.5.refs_2_, f32[7,3,4096]{2,1,0:T(4,128)S(1)} %copy.16.taps_ref.refs_3_, ...), custom_call_target="tpu_custom_call" | custom-call | flops 8388608 | bytes 2097152 | tf_op jit(solution)/shard_map/features_back/pallas_call | solution.py:447
  71.6 0.0 collective-permute-done.13.refs_1_
  71.7 0.0 collective-permute-done.14.refs_2_
  71.7 0.8 %collective-permute-done.15.refs_3_ = bf16[4,32,128]{2,1,0:T(8,128)(2,1)S(1)} collective-permute-done((bf16[4,32,128]{2,1,0:T(8,128)(2,1)S(1)}, bf16[4,32,128]{2,1,0:T(8,128)(2,1)S(1)}, u32[]{:S(2)}, u32[]{:S(2)}) %collective-permute-start.15) | collective-permute-done | bytes 32800 | tf_op jit(solution)/shard_map/ppermute | solution.py:350
  72.5 3.2 %collective-permute-start.16 = (bf16[4,4,32,128]{3,2,1,0:T(8,128)(2,1)S(1)}, bf16[4,4,32,128]{3,2,1,0:T(8,128)(2,1)S(1)}, u32[]{:S(2)}, u32[]{:S(2)}) collective-permute-start(bf16[4,4,32,128]{3,2,1,0:T(8,128)(2,1)S(1)} %join.1), channel_id=1, source_target_pairs={{0,1},{1,0},{2,3},{3,2},{4,5},{5,4},{6,7},{7,6},{8,9},{9,8},{10,11... | collective-permute-start | bytes 393224 | tf_op jit(solution)/shard_map/ppermute | solution.py:359
  75.7 1.0 %collective-permute-done.16 = bf16[4,4,32,128]{3,2,1,0:T(8,128)(2,1)S(1)} collective-permute-done((bf16[4,4,32,128]{3,2,1,0:T(8,128)(2,1)S(1)}, bf16[4,4,32,128]{3,2,1,0:T(8,128)(2,1)S(1)}, u32[]{:S(2)}, u32[]{:S(2)}) %collective-permute-start.16) | collective-permute-done | bytes 131104 | tf_op jit(solution)/shard_map/ppermute | solution.py:359
  76.7 1.0 %unpack.1 = (f32[3,7,4096]{2,1,0:T(8,128)}, f32[256,128]{1,0:T(8,128)}, f32[1,4096]{1,0:T(1,128)}) custom-call(bf16[16,32,128]{2,1,0:T(8,128)(2,1)S(1)} %bitcast.24, bf16[16,32,128]{2,1,0:T(8,128)(2,1)S(1)} %bitcast.25), custom_call_target="tpu_custom_call" | custom-call | tf_op jit(solution)/shard_map/unpack/pallas_call | solution.py:465
  (6 shorter events, 0.1 us)
Async XLA Ops:
  0.6 5.7 %copy-start.2 = (f32[7,3,4096]{2,0,1:T(8,128)S(1)}, f32[7,3,4096]{2,0,1:T(8,128)}, u32[]{:S(2)}) copy-start(f32[7,3,4096]{2,0,1:T(8,128)} %param.11) | copy-start | bytes 1032196
  1.8 7.2 %collective-permute-start = (bf16[24,4096]{1,0:T(8,128)(2,1)S(1)}, bf16[24,4096]{1,0:T(8,128)(2,1)S(1)}, u32[]{:S(2)}, u32[]{:S(2)}) collective-permute-start(bf16[24,4096]{1,0:T(8,128)(2,1)S(1)} %tails.1), channel_id=1, source_target_pairs={{0,1},{1,2},{2,3},{3,4},{4,5},{5,6},{6,7},{8,9},{9,10},{10,11},{11... | collective-permute-start | bytes 589832 | tf_op jit(solution)/shard_map/ppermute | solution.py:399
  13.9 13.3 %collective-permute-start.3 = (bf16[128,2048]{1,0:T(8,128)(2,1)}, bf16[128,2048]{1,0:T(8,128)(2,1)S(1)}, u32[]{:S(2)}, u32[]{:S(2)}) collective-permute-start(bf16[128,2048]{1,0:T(8,128)(2,1)} %get-tuple-element.46.near_hbm), channel_id=1, source_target_pairs={{0,1},{1,0},{2,3},{3,2},{4,5},{5,4},{6,7},{7,6},{8,9},{9,8},{10,11... | collective-permute-start | bytes 1572872 | tf_op jit(solution)/shard_map/ppermute | solution.py:417
  14.0 13.2 %copy-start = (f32[256,128]{1,0:T(8,128)S(1)}, f32[256,128]{1,0:T(8,128)}, u32[]{:S(2)}) copy-start(f32[256,128]{1,0:T(8,128)} %filt_ref.3) | copy-start | bytes 393220
  14.0 13.2 %collective-permute-start.4 = (bf16[128,2048]{1,0:T(8,128)(2,1)}, bf16[128,2048]{1,0:T(8,128)(2,1)S(1)}, u32[]{:S(2)}, u32[]{:S(2)}) collective-permute-start(bf16[128,2048]{1,0:T(8,128)(2,1)} %get-tuple-element.47.far_hbm), channel_id=1, source_target_pairs={{1,2},{3,4},{5,6},{2,1},{4,3},{6,5},{9,10},{11,12},{13,14},{10,9},... | collective-permute-start | bytes 1572872 | tf_op jit(solution)/shard_map/ppermute | solution.py:416
  23.5 3.7 %copy-start.1 = (f32[4096]{0:T(1024)S(1)}, f32[4096]{0:T(1024)}, u32[]{:S(2)}) copy-start(f32[4096]{0:T(1024)} %param.13) | copy-start | bytes 49156
  23.5 14.8 %collective-permute-start.1 = (bf16[128,2048]{1,0:T(8,128)(2,1)}, bf16[128,2048]{1,0:T(8,128)(2,1)S(1)}, u32[]{:S(2)}, u32[]{:S(2)}) collective-permute-start(bf16[128,2048]{1,0:T(8,128)(2,1)} %get-tuple-element.41.near_hbm), channel_id=1, source_target_pairs={{0,1},{1,0},{2,3},{3,2},{4,5},{5,4},{6,7},{7,6},{8,9},{9,8},{10,11... | collective-permute-start | bytes 1572872 | tf_op jit(solution)/shard_map/ppermute | solution.py:417
  23.6 14.7 %collective-permute-start.2 = (bf16[128,2048]{1,0:T(8,128)(2,1)}, bf16[128,2048]{1,0:T(8,128)(2,1)S(1)}, u32[]{:S(2)}, u32[]{:S(2)}) collective-permute-start(bf16[128,2048]{1,0:T(8,128)(2,1)} %get-tuple-element.42.far_hbm), channel_id=1, source_target_pairs={{1,2},{3,4},{5,6},{2,1},{4,3},{6,5},{9,10},{11,12},{13,14},{10,9},... | collective-permute-start | bytes 1572872 | tf_op jit(solution)/shard_map/ppermute | solution.py:416
  49.4 2.5 %collective-permute-start.6 = (bf16[4,4,32,128]{3,2,1,0:T(8,128)(2,1)S(1)}, bf16[4,4,32,128]{3,2,1,0:T(8,128)(2,1)S(1)}, u32[]{:S(2)}, u32[]{:S(2)}) collective-permute-start(bf16[4,4,32,128]{3,2,1,0:T(8,128)(2,1)S(1)} %bitcast.49), channel_id=1, source_target_pairs={{0,1},{1,0},{2,3},{3,2},{4,5},{5,4},{6,7},{7,6},{8,9},{9,8},{10,11... | collective-permute-start | bytes 393224 | tf_op jit(solution)/shard_map/ppermute | solution.py:340
  49.5 7.2 %collective-permute-start.5 = (bf16[24,4096]{1,0:T(8,128)(2,1)S(1)}, bf16[24,4096]{1,0:T(8,128)(2,1)S(1)}, u32[]{:S(2)}, u32[]{:S(2)}) collective-permute-start(bf16[24,4096]{1,0:T(8,128)(2,1)S(1)} %get-tuple-element.56), channel_id=1, source_target_pairs={{1,0},{2,1},{3,2},{4,3},{5,4},{6,5},{7,6},{9,8},{10,9},{11,10},{12... | collective-permute-start | bytes 589832 | tf_op jit(solution)/shard_map/ppermute | solution.py:442
  52.0 7.2 %collective-permute-start.7 = (bf16[4,32,128]{2,1,0:T(8,128)(2,1)S(1)}, bf16[4,32,128]{2,1,0:T(8,128)(2,1)S(1)}, u32[]{:S(2)}, u32[]{:S(2)}) collective-permute-start(bf16[4,32,128]{2,1,0:T(8,128)(2,1)S(1)} %get-tuple-element.81), channel_id=1, source_target_pairs={{0,8},{8,0},{16,24},{24,16},{1,9},{9,1},{17,25},{25,17},{2,10},{10... | collective-permute-start | bytes 98312 | tf_op jit(solution)/shard_map/ppermute | solution.py:342
  53.3 6.0 %collective-permute-start.8 = (bf16[4,32,128]{2,1,0:T(8,128)(2,1)S(1)}, bf16[4,32,128]{2,1,0:T(8,128)(2,1)S(1)}, u32[]{:S(2)}, u32[]{:S(2)}) collective-permute-start(bf16[4,32,128]{2,1,0:T(8,128)(2,1)S(1)} %get-tuple-element.80), channel_id=1, source_target_pairs={{0,16},{8,24},{16,0},{24,8},{1,17},{9,25},{17,1},{25,9},{2,18},{10... | collective-permute-start | bytes 98312 | tf_op jit(solution)/shard_map/ppermute | solution.py:342
  54.5 4.7 %collective-permute-start.9 = (bf16[4,32,128]{2,1,0:T(8,128)(2,1)S(1)}, bf16[4,32,128]{2,1,0:T(8,128)(2,1)S(1)}, u32[]{:S(2)}, u32[]{:S(2)}) collective-permute-start(bf16[4,32,128]{2,1,0:T(8,128)(2,1)S(1)} %get-tuple-element.79), channel_id=1, source_target_pairs={{0,24},{8,16},{16,8},{24,0},{1,25},{9,17},{17,9},{25,1},{2,26},{10... | collective-permute-start | bytes 98312 | tf_op jit(solution)/shard_map/ppermute | solution.py:342
  59.3 6.2 %collective-permute-start.10 = (bf16[4,32,128]{2,1,0:T(8,128)(2,1)S(1)}, bf16[4,32,128]{2,1,0:T(8,128)(2,1)S(1)}, u32[]{:S(2)}, u32[]{:S(2)}) collective-permute-start(bf16[4,32,128]{2,1,0:T(8,128)(2,1)S(1)} %get-tuple-element.63.refs_4_), channel_id=1, source_target_pairs={{0,2},{1,3},{2,0},{3,1},{4,6},{5,7},{6,4},{7,5},{8,10},{9,11},{10,... | collective-permute-start | bytes 98312 | tf_op jit(solution)/shard_map/ppermute | solution.py:349
  60.8 4.7 %collective-permute-start.11 = (bf16[4,32,128]{2,1,0:T(8,128)(2,1)S(1)}, bf16[4,32,128]{2,1,0:T(8,128)(2,1)S(1)}, u32[]{:S(2)}, u32[]{:S(2)}) collective-permute-start(bf16[4,32,128]{2,1,0:T(8,128)(2,1)S(1)} %get-tuple-element.63.refs_4_), channel_id=1, source_target_pairs={{0,4},{1,5},{2,6},{3,7},{4,0},{5,1},{6,2},{7,3},{8,12},{9,13},{10,... | collective-permute-start | bytes 98312 | tf_op jit(solution)/shard_map/ppermute | solution.py:349
  60.8 5.0 %collective-permute-start.12 = (bf16[4,32,128]{2,1,0:T(8,128)(2,1)S(1)}, bf16[4,32,128]{2,1,0:T(8,128)(2,1)S(1)}, u32[]{:S(2)}, u32[]{:S(2)}) collective-permute-start(bf16[4,32,128]{2,1,0:T(8,128)(2,1)S(1)} %get-tuple-element.63.refs_4_), channel_id=1, source_target_pairs={{0,6},{1,7},{2,4},{3,5},{4,2},{5,3},{6,0},{7,1},{8,14},{9,15},{10,... | collective-permute-start | bytes 98312 | tf_op jit(solution)/shard_map/ppermute | solution.py:349
  66.4 5.2 %collective-permute-start.13 = (bf16[4,32,128]{2,1,0:T(8,128)(2,1)S(1)}, bf16[4,32,128]{2,1,0:T(8,128)(2,1)S(1)}, u32[]{:S(2)}, u32[]{:S(2)}) collective-permute-start(bf16[4,32,128]{2,1,0:T(8,128)(2,1)S(1)} %get-tuple-element.69.refs_4_.refs_0_), channel_id=1, source_target_pairs={{0,8},{8,0},{16,24},{24,16},{1,9},{9,1},{17,25},{25,17},{2,10},{10... | collective-permute-start | bytes 98312 | tf_op jit(solution)/shard_map/ppermute | solution.py:350
  67.2 4.4 %collective-permute-start.14 = (bf16[4,32,128]{2,1,0:T(8,128)(2,1)S(1)}, bf16[4,32,128]{2,1,0:T(8,128)(2,1)S(1)}, u32[]{:S(2)}, u32[]{:S(2)}) collective-permute-start(bf16[4,32,128]{2,1,0:T(8,128)(2,1)S(1)} %get-tuple-element.69.refs_4_.refs_0_), channel_id=1, source_target_pairs={{0,16},{8,24},{16,0},{24,8},{1,17},{9,25},{17,1},{25,9},{2,18},{10... | collective-permute-start | bytes 98312 | tf_op jit(solution)/shard_map/ppermute | solution.py:350
  68.7 3.7 %collective-permute-start.15 = (bf16[4,32,128]{2,1,0:T(8,128)(2,1)S(1)}, bf16[4,32,128]{2,1,0:T(8,128)(2,1)S(1)}, u32[]{:S(2)}, u32[]{:S(2)}) collective-permute-start(bf16[4,32,128]{2,1,0:T(8,128)(2,1)S(1)} %get-tuple-element.69.refs_4_.refs_0_), channel_id=1, source_target_pairs={{0,24},{8,16},{16,8},{24,0},{1,25},{9,17},{17,9},{25,1},{2,26},{10... | collective-permute-start | bytes 98312 | tf_op jit(solution)/shard_map/ppermute | solution.py:350
  72.5 4.2 %collective-permute-start.16 = (bf16[4,4,32,128]{3,2,1,0:T(8,128)(2,1)S(1)}, bf16[4,4,32,128]{3,2,1,0:T(8,128)(2,1)S(1)}, u32[]{:S(2)}, u32[]{:S(2)}) collective-permute-start(bf16[4,4,32,128]{3,2,1,0:T(8,128)(2,1)S(1)} %join.1), channel_id=1, source_target_pairs={{0,1},{1,0},{2,3},{3,2},{4,5},{5,4},{6,7},{7,6},{8,9},{9,8},{10,11... | collective-permute-start | bytes 393224 | tf_op jit(solution)/shard_map/ppermute | solution.py:359

commit v4 on v3

--- a/solution.py
+++ b/solution.py
@@ -9,7 +9,8 @@
 
 LANES = 128
 HALO = 8
-TILES = 4
+TILES = 8
+STRIP = 16
 WIDE = TILES * LANES
 SHARE = 32
 VMEM = 44 * 1024 * 1024
@@ -94,6 +95,11 @@
         return carry
 
     lax.fori_loop(0, TILES, run, 0, unroll=unroll)
+
+
+def all_tiles(piece, one):
+    for index in range(TILES):
+        one(piece * TILES + index, index)
 
 
 def tails_kernel(rows, q_hbm, k_hbm, v_hbm, out_ref, buffer, sem):
@@ -140,6 +146,13 @@
     return [pltpu.with_memory_space_constraint(array, pltpu.HBM) for array in arrays]
 
 
+def by_eight(values):
+    total = values[:8]
+    for start in range(8, values.shape[0], 8):
+        total = total + values[start:start + 8]
+    return total
+
+
 def turned(size):
     row = lax.broadcasted_iota(jnp.int32, (size, size), 0)
     col = lax.broadcasted_iota(jnp.int32, (size, size), 1)
@@ -153,12 +166,14 @@
         rest = rest[2:]
     out_hbm, head_ref, gq_hbm, gk_hbm, gv_hbm, grad_ref = rest[:6]
     (q_ref, k_ref, v_ref, cot_ref, mix_ref, gf_ref, qf_ref, kf_ref, vf_ref, prev_ref, next_ref,
-     out_ref, gq_ref, gk_ref, gv_ref, rev_ref, ext, part, in_sem, out_sem) = rest[6:]
+     out_ref, gq_ref, gk_ref, gv_ref, rev_ref, exts, parts, in_sem, out_sem) = rest[6:]
     half = rows // 2
     groups = LANES // per_group
     row_id = lax.broadcasted_iota(jnp.int32, (half, LANES), 0)
     lane_id = lax.broadcasted_iota(jnp.int32, (half, LANES), 1)
     wide_group = lax.broadcasted_iota(jnp.int32, (half, 2 * LANES), 1) % LANES // per_group
+    wide_pair = wide_group // 2
+    odd_group = lax.broadcasted_iota(jnp.int32, (2 * rows, 2 * LANES), 1) // per_group % 2 == 1
     later = lane_id > row_id
     early = lane_id < row_id
     zero = jnp.zeros((half, LANES), F32)
@@ -168,7 +183,8 @@
     rev_ref[...] = jnp.dot(filt_ref[pl.ds(base, rev_ref.shape[0]), :].astype(BF16), turned(filt_ref.shape[1]),
                            preferred_element_type=F32)
 
-    def one(tile):
+    def one(tile, slot_index):
+        ext, part = exts.at[slot_index], parts.at[slot_index]
         lanes = lanes_at(tile * LANES)
         far = lanes_at(first + tile * LANES)
         mix = mix_ref[:, lanes]
@@ -197,10 +213,14 @@
             masked.append(jnp.where(wide_group == group, gf_wide, jnp.zeros_like(gf_wide)))
 
         def filtered_by(matrices, window):
-            found = jnp.dot(jnp.concatenate(matrices, axis=0), window, preferred_element_type=F32)
+            even = jnp.where(odd_group, jnp.zeros_like(window), window)
+            uneven = jnp.where(odd_group, window, jnp.zeros_like(window))
+            pairs = [jnp.concatenate(matrices[index:index + 2], axis=1) for index in range(0, groups, 2)]
+            found = jnp.dot(jnp.concatenate(pairs, axis=0), jnp.concatenate([even, uneven], axis=0),
+                            preferred_element_type=F32)
             picked = found[:half]
-            for group in range(1, groups):
-                picked = jnp.where(wide_group == group, found[group * half:(group + 1) * half], picked)
+            for pair in range(1, groups // 2):
+                picked = jnp.where(wide_pair == pair, found[pair * half:(pair + 1) * half], picked)
             return jnp.concatenate([picked[:, :LANES], picked[:, LANES:]], axis=0)
 
         conv = filtered_by(firsts, before)
@@ -222,35 +242,49 @@
         part[pl.ds(SHARE - groups, groups), :] = jnp.sum(sums.reshape(groups, 8, LANES), axis=1)
 
         gain = gain_ref[:, far]
-        mix_wide = mix.astype(F32)
-        gf_f32 = gf.astype(F32)
-        filtered = conv + gain * mix_wide
-        grad_mix = back + gain * gf_f32
-        part[pl.ds(3 * taps_count, 1), :] = jnp.sum(mix_wide * gf_f32, axis=0, keepdims=True)
-        out_ref[:, lanes] = (qf_ref[:, lanes].astype(F32) * filtered).astype(BF16)
-        grads = (cot_ref[:, lanes].astype(F32) * filtered, grad_mix * vf_ref[:, lanes].astype(F32),
-                 grad_mix * kf_ref[:, lanes].astype(F32))
         tails = tail_ref[:, far].astype(F32)
-        for which, (src, grad, dest) in enumerate(zip((q_ref, k_ref, v_ref), grads, (gq_ref, gk_ref, gv_ref))):
-            dest[:, lanes] = grad.astype(BF16)
+        sources, dests = (q_ref, k_ref, v_ref), (gq_ref, gk_ref, gv_ref)
+        for which in range(3):
             ext[which, pl.ds(0, HALO), :] = tails[which * HALO:(which + 1) * HALO]
-            ext[which, pl.ds(HALO, rows), :] = src[:, lanes].astype(F32)
+        skip = jnp.zeros((8, LANES), F32)
+        lags = [[jnp.zeros((8, LANES), F32)] * taps_count for _ in range(3)]
+        heads = []
+        for start in range(0, rows, STRIP):
+            strip = pl.ds(start, STRIP)
+            span = slice(start, start + STRIP)
+            mix_wide = mix[span].astype(F32)
+            gf_wide_rows = gf[span].astype(F32)
+            filtered = conv[span] + gain * mix_wide
+            grad_mix = back[span] + gain * gf_wide_rows
+            skip = skip + by_eight(mix_wide * gf_wide_rows)
+            out_ref[strip, lanes] = (qf_ref[strip, lanes].astype(F32) * filtered).astype(BF16)
+            grads = (cot_ref[strip, lanes].astype(F32) * filtered, grad_mix * vf_ref[strip, lanes].astype(F32),
+                     grad_mix * kf_ref[strip, lanes].astype(F32))
+            if start == 0:
+                heads = [grad[:HALO] for grad in grads]
+            for which in range(3):
+                dests[which][strip, lanes] = grads[which].astype(BF16)
+                ext[which, pl.ds(HALO + start, STRIP), :] = sources[which][strip, lanes].astype(F32)
+                for lag in range(taps_count):
+                    lags[which][lag] = lags[which][lag] + by_eight(
+                        grads[which] * ext[which, pl.ds(HALO + start - lag, STRIP), :])
+        part[pl.ds(3 * taps_count, 1), :] = jnp.sum(skip, axis=0, keepdims=True)
+        for which in range(3):
             for lag in range(taps_count):
-                part[pl.ds(lag * 3 + which, 1), :] = jnp.sum(
-                    grad * ext[which, pl.ds(HALO - lag, rows), :], axis=0, keepdims=True)
-        head_ref[:, far] = jnp.concatenate([grad[:HALO] for grad in grads], axis=0).astype(BF16)
+                part[pl.ds(lag * 3 + which, 1), :] = jnp.sum(lags[which][lag], axis=0, keepdims=True)
+        head_ref[:, far] = jnp.concatenate(heads, axis=0).astype(BF16)
         quarter = tile // in_quarter
         slot = (quarter ^ dp_position()) * in_quarter + lax.rem(tile, in_quarter)
         grad_ref[slot] = part[...].astype(BF16)
 
-    part[...] = jnp.zeros(part.shape, F32)
+    parts[...] = jnp.zeros(parts.shape, F32)
     stream(pieces, ahead,
            [(q_hbm, first, q_ref), (k_hbm, first, k_ref), (v_hbm, first, v_ref), (cot_hbm, first, cot_ref),
             ((near_hbm, far_hbm), 0, mix_ref), ((far_hbm, near_hbm), 0, gf_ref),
             (qf_hbm, 0, qf_ref), (kf_hbm, 0, kf_ref), (vf_hbm, 0, vf_ref),
             ((got_far_hbm, got_near_hbm), 0, prev_ref), ((got_near_hbm, got_far_hbm), 0, next_ref)],
            [(out_ref, out_hbm, first), (gq_ref, gq_hbm, 0), (gk_ref, gk_hbm, 0), (gv_ref, gv_hbm, 0)],
-           in_sem, out_sem, lambda piece: per_tile(piece, TILES, one))
+           in_sem, out_sem, lambda piece: all_tiles(piece, one))
 
 
 def back_kernel(which, rows, taps_count, pieces, parts, *refs):
@@ -292,8 +326,9 @@
     total = keep_ref[...]
     for ref in refs[:count]:
         total = total + ref[...].astype(F32)
-    refs[count + 1][...] = total
-    refs[count + 2][...] = total.astype(BF16)
+    refs[count + 1][...] = total.astype(BF16)
+    if len(refs) > count + 2:
+        refs[count + 2][...] = total
 
 
 def join_kernel(count, *refs):
@@ -325,28 +360,31 @@
     return [(i, i ^ mask) for i in range(size)]
 
 
-def add(keep, arrived, after):
-    return pl.pallas_call(
+def add(keep, arrived, after, last=False):
+    kinds = [BF16] if last else [BF16, F32]
+    found = pl.pallas_call(
         functools.partial(add_kernel, len(arrived)),
         in_specs=[WHOLE] * (len(arrived) + 2),
-        out_specs=[WHOLE] * 2,
-        out_shape=[jax.ShapeDtypeStruct(keep.shape, F32), jax.ShapeDtypeStruct(keep.shape, BF16)],
+        out_specs=[WHOLE] * len(kinds),
+        out_shape=[jax.ShapeDtypeStruct(keep.shape, kind) for kind in kinds],
         compiler_params=pltpu.CompilerParams(vmem_limit_bytes=SMALL),
         name="add",
     )(keep, *arrived, after)
+    return found[0], found[-1]
 
 
 def reduce_all(mine, theirs, ctx_count, dp_count, beside):
     half = mine.astype(F32) + lax.ppermute(theirs, "ctx", swaps(ctx_count, 1)).astype(F32)
     sent = half.astype(BF16)
     arrived = [lax.ppermute(sent[mask], "dp", swaps(dp_count, mask)) for mask in range(1, dp_count)]
-    total, low = add(half[0], arrived, beside[0](sent))
+    low, total = add(half[0], arrived, beside[0](sent))
     work = beside[1](low)
     mask = 2
     while mask < ctx_count:
         picks = (mask, 2 * mask, 3 * mask) if mask * 2 < ctx_count else (mask,)
         mask *= 4
-        total, low = add(total, [lax.ppermute(low, "ctx", swaps(ctx_count, pick)) for pick in picks], work)
+        low, total = add(total, [lax.ppermute(low, "ctx", swaps(ctx_count, pick)) for pick in picks], work,
+                         mask >= ctx_count)
     quarters = [low] + [lax.ppermute(low, "dp", swaps(dp_count, mask)) for mask in range(1, dp_count)]
     whole = pl.pallas_call(
         functools.partial(join_kernel, dp_count),
@@ -356,7 +394,8 @@
         compiler_params=pltpu.CompilerParams(vmem_limit_bytes=SMALL),
         name="join",
     )(*quarters, beside[2](low))
-    return whole, lax.ppermute(whole, "ctx", swaps(ctx_count, 1))
+    other = lax.ppermute(whole, "ctx", swaps(ctx_count, 1))
+    return whole, other
 
 
 def body(query_rows, key_rows, value_rows, cotangent, feature_taps, filter_taps, skip_gain):
@@ -428,8 +467,8 @@
             + [jax.ShapeDtypeStruct((in_half, SHARE, LANES), BF16)],
             input_output_aliases={14: 0, 15: 1} if part else {},
             scratch_shapes=buffers(15)
-            + [pltpu.VMEM((group_count // parts, taps_len), F32), pltpu.VMEM((3, rows + HALO, LANES), F32),
-               pltpu.VMEM((SHARE, LANES), F32)] + sems(11, 4),
+            + [pltpu.VMEM((group_count // parts, taps_len), F32), pltpu.VMEM((TILES, 3, rows + HALO, LANES), F32),
+               pltpu.VMEM((TILES, SHARE, LANES), F32)] + sems(11, 4),
             compiler_params=compiler_params,
             cost_estimate=pl.CostEstimate(flops=2000 * rows * width, bytes_accessed=30 * rows * width,
                                           transcendentals=0),
@@ -439,9 +478,9 @@
         results.append(found[2:])
 
     out = shared[0]
-    next_heads = lax.ppermute(shared[1], "ctx", backward)
     shares = [found[3].reshape(dp_count, in_quarter, SHARE, LANES) for found in results]
     grads = []
+    next_heads = lax.ppermute(shared[1], "ctx", backward)
 
     def beside(which, after):
         grads.append(pl.pallas_call(

time: 78.3 us -> 75.5 us (0.964)
  Pallas kernels: 42.5 us -> 39.5 us
    pallas_call x2, Pallas kernels: 22.1 us -> 19.8 us  [body(): pl.pallas_call(functools.partial(mix_kernel, part * width, rows, taps_cou...]
where the time goes in v4:
time: 75.5 us; the launch traced here: 74.9 us
  Pallas kernels  39.5 us (52%)
  starting transfers between devices  27.7 us (37%)
  waiting for transfers between devices  6.44 us (9%)
  between operations  0.95 us (1%)
    pallas_call x2, Pallas kernels, body(): pl.pallas_call(functools.partial(mix_kernel, part * width, rows, taps_cou...  19.8 us
    pallas_call x2, Pallas kernels, body(): pl.pallas_call(functools.partial(feat_kernel, part * width, rows, taps_co...  10.2 us
    ppermute x2, starting transfers between devices, body(): far = lax.ppermute(feats[1], 'ctx', chips)  8.08 us
    pallas_call x3, Pallas kernels, beside(): pl.pallas_call(functools.partial(back_kernel, which, rows, taps_count, pa...  7.31 us
    ppermute x1, starting transfers between devices, body(): tails = lax.ppermute(tails, 'ctx', onward)  4.59 us
    ppermute x3, starting transfers between devices, reduce_all(): lax.ppermute(low, 'ctx', swaps(ctx_count, pick))  3.64 us
    ppermute x1, starting transfers between devices, reduce_all(): other = lax.ppermute(whole, 'ctx', swaps(ctx_count, 1))  3.34 us
    ppermute x3, starting transfers between devices, reduce_all(): lax.ppermute(sent[mask], 'dp', swaps(dp_count, mask))  2.71 us
  transfers between devices with their start and end apart: 17, of which 5 were waited for; matrix products, arithmetic and copies ran while one was open for 0% of the time, Pallas kernels for 30%

profile of v4, /device:TPU:1, one launch (start us, length us, event | category | flops | bytes accessed | tf_op | source)
XLA Modules:
  0.0 74.9 jit_solution(4508009138504723065)
XLA Ops:
  0.6 0.0 copy-start.2
  0.6 1.1 %tails.1 = bf16[24,4096]{1,0:T(8,128)(2,1)S(1)} custom-call(bf16[128,4096]{1,0:T(8,128)(2,1)} %bitcast.28, bf16[128,4096]{1,0:T(8,128)(2,1)} %bitcast.33, bf16[128,4096]{1,0:T(8,128)(2,1)} %bitcast.38), custom_call_target="tpu_custom_call" | custom-call | tf_op jit(solution)/shard_map/tails/pallas_call | solution.py:429
  1.8 4.6 %collective-permute-start = (bf16[24,4096]{1,0:T(8,128)(2,1)S(1)}, bf16[24,4096]{1,0:T(8,128)(2,1)S(1)}, u32[]{:S(2)}, u32[]{:S(2)}) collective-permute-start(bf16[24,4096]{1,0:T(8,128)(2,1)S(1)} %tails.1), channel_id=1, source_target_pairs={{0,1},{1,2},{2,3},{3,4},{4,5},{5,6},{6,7},{8,9},{9,10},{10,11},{11... | collective-permute-start | bytes 589832 | tf_op jit(solution)/shard_map/ppermute | solution.py:438
  6.4 0.0 copy-done.2
  6.4 0.2 copy.16.taps_ref.refs_3_
  6.6 2.3 %collective-permute-done.tail_ref = bf16[24,4096]{1,0:T(8,128)(2,1)S(1)} collective-permute-done((bf16[24,4096]{1,0:T(8,128)(2,1)S(1)}, bf16[24,4096]{1,0:T(8,128)(2,1)S(1)}, u32[]{:S(2)}, u32[]{:S(2)}) %collective-permute-start) | collective-permute-done | bytes 196640 | tf_op jit(solution)/shard_map/ppermute | solution.py:438
  9.0 5.1 %features.3 = (bf16[128,2048]{1,0:T(8,128)(2,1)}, bf16[128,2048]{1,0:T(8,128)(2,1)}, bf16[128,2048]{1,0:T(8,128)(2,1)}, bf16[128,2048]{1,0:T(8,128)(2,1)}, bf16[128,2048]{1,0:T(8,128)(2,1)}) custom-call(bf16[128,4096]{1,0:T(8,128)(2,1)} %bitcast.29, bf16[128,4096]{1,0:T(8,128)(2,1)} %bitcast.34, bf16[128,4096]{1,0:T(8,128)(2,1)} %bitcast.39, ...), custom_call_target="tpu_custom_call" | custom-call | flops 13107200 | bytes 4718592 | tf_op jit(solution)/shard_map/features/pallas_call | solution.py:444
  14.1 0.1 collective-permute-start.3
  14.2 0.0 copy-start
  14.2 4.5 %collective-permute-start.4 = (bf16[128,2048]{1,0:T(8,128)(2,1)}, bf16[128,2048]{1,0:T(8,128)(2,1)S(1)}, u32[]{:S(2)}, u32[]{:S(2)}) collective-permute-start(bf16[128,2048]{1,0:T(8,128)(2,1)} %get-tuple-element.46.far_hbm), channel_id=1, source_target_pairs={{1,2},{3,4},{5,6},{2,1},{4,3},{6,5},{9,10},{11,12},{13,14},{10,9},... | collective-permute-start | bytes 1572872 | tf_op jit(solution)/shard_map/ppermute | solution.py:455
  18.7 5.1 %features.2 = (bf16[128,2048]{1,0:T(8,128)(2,1)}, bf16[128,2048]{1,0:T(8,128)(2,1)}, bf16[128,2048]{1,0:T(8,128)(2,1)}, bf16[128,2048]{1,0:T(8,128)(2,1)}, bf16[128,2048]{1,0:T(8,128)(2,1)}) custom-call(bf16[128,4096]{1,0:T(8,128)(2,1)} %bitcast.30, bf16[128,4096]{1,0:T(8,128)(2,1)} %bitcast.35, bf16[128,4096]{1,0:T(8,128)(2,1)} %bitcast.40, ...), custom_call_target="tpu_custom_call" | custom-call | flops 13107200 | bytes 4718592 | tf_op jit(solution)/shard_map/features/pallas_call | solution.py:444
  23.8 0.0 copy-start.1
  23.8 0.1 collective-permute-start.1
  23.9 3.6 %collective-permute-start.2 = (bf16[128,2048]{1,0:T(8,128)(2,1)}, bf16[128,2048]{1,0:T(8,128)(2,1)S(1)}, u32[]{:S(2)}, u32[]{:S(2)}) collective-permute-start(bf16[128,2048]{1,0:T(8,128)(2,1)} %get-tuple-element.41.far_hbm), channel_id=1, source_target_pairs={{1,2},{3,4},{5,6},{2,1},{4,3},{6,5},{9,10},{11,12},{13,14},{10,9},... | collective-permute-start | bytes 1572872 | tf_op jit(solution)/shard_map/ppermute | solution.py:455
  27.5 0.0 collective-permute-done.3.got_near_hbm
  27.5 0.0 collective-permute-done.4.got_far_hbm
  27.5 0.0 copy-done
  27.5 0.0 copy-done.1
  27.5 9.9 %filters.2 = (bf16[128,4096]{1,0:T(8,128)(2,1)}, bf16[24,4096]{1,0:T(8,128)(2,1)S(1)}, bf16[128,2048]{1,0:T(8,128)(2,1)S(1)}, bf16[128,2048]{1,0:T(8,128)(2,1)S(...) custom-call(bf16[128,4096]{1,0:T(8,128)(2,1)} %bitcast.31, bf16[128,4096]{1,0:T(8,128)(2,1)} %bitcast.36, ...), custom_call_target="tpu_custom_call" | custom-call | flops 524288000 | bytes 7864320 | tf_op jit(solution)/shard_map/filters/pallas_call | solution.py:461
  37.4 0.0 collective-permute-done.1.got_near_hbm
  37.4 0.0 collective-permute-done.2.got_far_hbm
  37.4 9.9 %filters.3 = (bf16[128,4096]{1,0:T(8,128)(2,1)}, bf16[24,4096]{1,0:T(8,128)(2,1)S(1)}, bf16[128,2048]{1,0:T(8,128)(2,1)S(1)}, bf16[128,2048]{1,0:T(8,128)(2,1)S(...) custom-call(bf16[128,4096]{1,0:T(8,128)(2,1)} %bitcast.32, ...), custom_call_target="tpu_custom_call", output_to_operand_aliasing={{0}: (14, {}), {1}: (15, {})} | custom-call | flops 524288000 | bytes 7864320 | tf_op jit(solution)/shard_map/filters/pallas_call | solution.py:461
  47.4 0.1 collective-permute-start.6
  47.4 2.4 %collective-permute-start.5 = (bf16[24,4096]{1,0:T(8,128)(2,1)S(1)}, bf16[24,4096]{1,0:T(8,128)(2,1)S(1)}, u32[]{:S(2)}, u32[]{:S(2)}) collective-permute-start(bf16[24,4096]{1,0:T(8,128)(2,1)S(1)} %get-tuple-element.55), channel_id=1, source_target_pairs={{1,0},{2,1},{3,2},{4,3},{5,4},{6,5},{7,6},{9,8},{10,9},{11,10},{12... | collective-permute-start | bytes 589832 | tf_op jit(solution)/shard_map/ppermute | solution.py:483
  49.8 0.0 collective-permute-done.6
  49.9 1.3 %collective-permute-start.7 = (bf16[4,32,128]{2,1,0:T(8,128)(2,1)S(1)}, bf16[4,32,128]{2,1,0:T(8,128)(2,1)S(1)}, u32[]{:S(2)}, u32[]{:S(2)}) collective-permute-start(bf16[4,32,128]{2,1,0:T(8,128)(2,1)S(1)} %get-tuple-element.79), channel_id=1, source_target_pairs={{0,8},{8,0},{16,24},{24,16},{1,9},{9,1},{17,25},{25,17},{2,10},{10... | collective-permute-start | bytes 98312 | tf_op jit(solution)/shard_map/ppermute | solution.py:379
  51.2 1.2 %collective-permute-start.8 = (bf16[4,32,128]{2,1,0:T(8,128)(2,1)S(1)}, bf16[4,32,128]{2,1,0:T(8,128)(2,1)S(1)}, u32[]{:S(2)}, u32[]{:S(2)}) collective-permute-start(bf16[4,32,128]{2,1,0:T(8,128)(2,1)S(1)} %get-tuple-element.78), channel_id=1, source_target_pairs={{0,16},{8,24},{16,0},{24,8},{1,17},{9,25},{17,1},{25,9},{2,18},{10... | collective-permute-start | bytes 98312 | tf_op jit(solution)/shard_map/ppermute | solution.py:379
  52.4 0.2 collective-permute-start.9
  52.6 2.0 %collective-permute-done.5.refs_2_ = bf16[24,4096]{1,0:T(8,128)(2,1)S(1)} collective-permute-done((bf16[24,4096]{1,0:T(8,128)(2,1)S(1)}, bf16[24,4096]{1,0:T(8,128)(2,1)S(1)}, u32[]{:S(2)}, u32[]{:S(2)}) %collective-permute-start.5) | collective-permute-done | bytes 196640 | tf_op jit(solution)/shard_map/ppermute | solution.py:483
  54.6 2.4 %features_back.3 = (bf16[128,4096]{1,0:T(8,128)(2,1)}, f32[8,128]{1,0:T(8,128)S(1)}) custom-call(bf16[128,2048]{1,0:T(8,128)(2,1)S(1)} %get-tuple-element.53.refs_0_, bf16[128,2048]{1,0:T(8,128)(2,1)S(1)} %get-tuple-element.54.refs_1_, bf16[24,4096]{1,0:T(8,128)(2,1)S(1)} %collective-permute-done.5.refs_2_, f32[7,3,4096]{2,1,0:T(4,128)S(1)} %copy.16.taps_ref.refs_3_, ...), custom_call_target="tpu_custom_call" | custom-call | flops 8388608 | bytes 2097152 | tf_op jit(solution)/shard_map/features_back/pallas_call | solution.py:486
  57.1 0.0 collective-permute-done.7.refs_0_
  57.1 0.0 collective-permute-done.8.refs_1_
  57.1 0.0 collective-permute-done.9.refs_2_
  57.1 1.2 %collective-permute-start.10 = (bf16[4,32,128]{2,1,0:T(8,128)(2,1)S(1)}, bf16[4,32,128]{2,1,0:T(8,128)(2,1)S(1)}, u32[]{:S(2)}, u32[]{:S(2)}) collective-permute-start(bf16[4,32,128]{2,1,0:T(8,128)(2,1)S(1)} %get-tuple-element.62.refs_4_), channel_id=1, source_target_pairs={{0,2},{1,3},{2,0},{3,1},{4,6},{5,7},{6,4},{7,5},{8,10},{9,11},{10,... | collective-permute-start | bytes 98312 | tf_op jit(solution)/shard_map/ppermute | solution.py:386
  58.3 0.2 collective-permute-start.11
  58.5 2.2 %collective-permute-start.12 = (bf16[4,32,128]{2,1,0:T(8,128)(2,1)S(1)}, bf16[4,32,128]{2,1,0:T(8,128)(2,1)S(1)}, u32[]{:S(2)}, u32[]{:S(2)}) collective-permute-start(bf16[4,32,128]{2,1,0:T(8,128)(2,1)S(1)} %get-tuple-element.62.refs_4_), channel_id=1, source_target_pairs={{0,6},{1,7},{2,4},{3,5},{4,2},{5,3},{6,0},{7,1},{8,14},{9,15},{10,... | collective-permute-start | bytes 98312 | tf_op jit(solution)/shard_map/ppermute | solution.py:386
  60.8 2.4 %features_back.4 = (bf16[128,4096]{1,0:T(8,128)(2,1)}, f32[8,128]{1,0:T(8,128)S(1)}) custom-call(bf16[128,2048]{1,0:T(8,128)(2,1)S(1)} %get-tuple-element.59.refs_0_, bf16[128,2048]{1,0:T(8,128)(2,1)S(1)} %get-tuple-element.60.refs_1_, bf16[24,4096]{1,0:T(8,128)(2,1)S(1)} %collective-permute-done.5.refs_2_, f32[7,3,4096]{2,1,0:T(4,128)S(1)} %copy.16.taps_ref.refs_3_, ...), custom_call_target="tpu_custom_call" | custom-call | flops 8388608 | bytes 2097152 | tf_op jit(solution)/shard_map/features_back/pallas_call | solution.py:486
  63.2 0.0 collective-permute-done.10.refs_0_
  63.2 0.0 collective-permute-done.11.refs_1_
  63.2 0.1 collective-permute-done.12.refs_2_
  63.4 1.1 %collective-permute-start.13 = (bf16[4,32,128]{2,1,0:T(8,128)(2,1)S(1)}, bf16[4,32,128]{2,1,0:T(8,128)(2,1)S(1)}, u32[]{:S(2)}, u32[]{:S(2)}) collective-permute-start(bf16[4,32,128]{2,1,0:T(8,128)(2,1)S(1)} %add.10.refs_4_.refs_0_), channel_id=1, source_target_pairs={{0,8},{8,0},{16,24},{24,16},{1,9},{9,1},{17,25},{25,17},{2,10},{10... | collective-permute-start | bytes 98312 | tf_op jit(solution)/shard_map/ppermute | solution.py:388
  64.4 1.5 %collective-permute-start.14 = (bf16[4,32,128]{2,1,0:T(8,128)(2,1)S(1)}, bf16[4,32,128]{2,1,0:T(8,128)(2,1)S(1)}, u32[]{:S(2)}, u32[]{:S(2)}) collective-permute-start(bf16[4,32,128]{2,1,0:T(8,128)(2,1)S(1)} %add.10.refs_4_.refs_0_), channel_id=1, source_target_pairs={{0,16},{8,24},{16,0},{24,8},{1,17},{9,25},{17,1},{25,9},{2,18},{10... | collective-permute-start | bytes 98312 | tf_op jit(solution)/shard_map/ppermute | solution.py:388
  65.9 0.2 collective-permute-start.15
  66.1 2.4 %features_back.5 = (bf16[128,4096]{1,0:T(8,128)(2,1)}, f32[8,128]{1,0:T(8,128)S(1)}) custom-call(bf16[128,2048]{1,0:T(8,128)(2,1)S(1)} %get-tuple-element.64.refs_0_, bf16[128,2048]{1,0:T(8,128)(2,1)S(1)} %get-tuple-element.65.refs_1_, bf16[24,4096]{1,0:T(8,128)(2,1)S(1)} %collective-permute-done.5.refs_2_, f32[7,3,4096]{2,1,0:T(4,128)S(1)} %copy.16.taps_ref.refs_3_, ...), custom_call_target="tpu_custom_call" | custom-call | flops 8388608 | bytes 2097152 | tf_op jit(solution)/shard_map/features_back/pallas_call | solution.py:486
  68.5 0.0 collective-permute-done.13.refs_1_
  68.5 0.0 collective-permute-done.14.refs_2_
  68.5 1.0 %collective-permute-done.15.refs_3_ = bf16[4,32,128]{2,1,0:T(8,128)(2,1)S(1)} collective-permute-done((bf16[4,32,128]{2,1,0:T(8,128)(2,1)S(1)}, bf16[4,32,128]{2,1,0:T(8,128)(2,1)S(1)}, u32[]{:S(2)}, u32[]{:S(2)}) %collective-permute-start.15) | collective-permute-done | bytes 32800 | tf_op jit(solution)/shard_map/ppermute | solution.py:388
  69.6 3.3 %collective-permute-start.16 = (bf16[4,4,32,128]{3,2,1,0:T(8,128)(2,1)S(1)}, bf16[4,4,32,128]{3,2,1,0:T(8,128)(2,1)S(1)}, u32[]{:S(2)}, u32[]{:S(2)}) collective-permute-start(bf16[4,4,32,128]{3,2,1,0:T(8,128)(2,1)S(1)} %join.1), channel_id=1, source_target_pairs={{0,1},{1,0},{2,3},{3,2},{4,5},{5,4},{6,7},{7,6},{8,9},{9,8},{10,11... | collective-permute-start | bytes 393224 | tf_op jit(solution)/shard_map/ppermute | solution.py:397
  72.9 1.0 %collective-permute-done.16 = bf16[4,4,32,128]{3,2,1,0:T(8,128)(2,1)S(1)} collective-permute-done((bf16[4,4,32,128]{3,2,1,0:T(8,128)(2,1)S(1)}, bf16[4,4,32,128]{3,2,1,0:T(8,128)(2,1)S(1)}, u32[]{:S(2)}, u32[]{:S(2)}) %collective-permute-start.16) | collective-permute-done | bytes 131104 | tf_op jit(solution)/shard_map/ppermute | solution.py:397
  73.9 1.0 %unpack.1 = (f32[3,7,4096]{2,1,0:T(8,128)}, f32[256,128]{1,0:T(8,128)}, f32[1,4096]{1,0:T(1,128)}) custom-call(bf16[16,32,128]{2,1,0:T(8,128)(2,1)S(1)} %bitcast.24, bf16[16,32,128]{2,1,0:T(8,128)(2,1)S(1)} %bitcast.25), custom_call_target="tpu_custom_call" | custom-call | tf_op jit(solution)/shard_map/unpack/pallas_call | solution.py:504
  (7 shorter events, 0.1 us)
Async XLA Ops:
  0.6 5.7 %copy-start.2 = (f32[7,3,4096]{2,0,1:T(8,128)S(1)}, f32[7,3,4096]{2,0,1:T(8,128)}, u32[]{:S(2)}) copy-start(f32[7,3,4096]{2,0,1:T(8,128)} %param.11) | copy-start | bytes 1032196
  1.8 7.2 %collective-permute-start = (bf16[24,4096]{1,0:T(8,128)(2,1)S(1)}, bf16[24,4096]{1,0:T(8,128)(2,1)S(1)}, u32[]{:S(2)}, u32[]{:S(2)}) collective-permute-start(bf16[24,4096]{1,0:T(8,128)(2,1)S(1)} %tails.1), channel_id=1, source_target_pairs={{0,1},{1,2},{2,3},{3,4},{4,5},{5,6},{6,7},{8,9},{9,10},{10,11},{11... | collective-permute-start | bytes 589832 | tf_op jit(solution)/shard_map/ppermute | solution.py:438
  14.1 13.4 %collective-permute-start.3 = (bf16[128,2048]{1,0:T(8,128)(2,1)}, bf16[128,2048]{1,0:T(8,128)(2,1)S(1)}, u32[]{:S(2)}, u32[]{:S(2)}) collective-permute-start(bf16[128,2048]{1,0:T(8,128)(2,1)} %get-tuple-element.45.near_hbm), channel_id=1, source_target_pairs={{0,1},{1,0},{2,3},{3,2},{4,5},{5,4},{6,7},{7,6},{8,9},{9,8},{10,11... | collective-permute-start | bytes 1572872 | tf_op jit(solution)/shard_map/ppermute | solution.py:456
  14.2 13.3 %copy-start = (f32[256,128]{1,0:T(8,128)S(1)}, f32[256,128]{1,0:T(8,128)}, u32[]{:S(2)}) copy-start(f32[256,128]{1,0:T(8,128)} %filt_ref.3) | copy-start | bytes 393220
  14.2 13.3 %collective-permute-start.4 = (bf16[128,2048]{1,0:T(8,128)(2,1)}, bf16[128,2048]{1,0:T(8,128)(2,1)S(1)}, u32[]{:S(2)}, u32[]{:S(2)}) collective-permute-start(bf16[128,2048]{1,0:T(8,128)(2,1)} %get-tuple-element.46.far_hbm), channel_id=1, source_target_pairs={{1,2},{3,4},{5,6},{2,1},{4,3},{6,5},{9,10},{11,12},{13,14},{10,9},... | collective-permute-start | bytes 1572872 | tf_op jit(solution)/shard_map/ppermute | solution.py:455
  23.8 3.7 %copy-start.1 = (f32[4096]{0:T(1024)S(1)}, f32[4096]{0:T(1024)}, u32[]{:S(2)}) copy-start(f32[4096]{0:T(1024)} %param.13) | copy-start | bytes 49156
  23.8 13.6 %collective-permute-start.1 = (bf16[128,2048]{1,0:T(8,128)(2,1)}, bf16[128,2048]{1,0:T(8,128)(2,1)S(1)}, u32[]{:S(2)}, u32[]{:S(2)}) collective-permute-start(bf16[128,2048]{1,0:T(8,128)(2,1)} %get-tuple-element.40.near_hbm), channel_id=1, source_target_pairs={{0,1},{1,0},{2,3},{3,2},{4,5},{5,4},{6,7},{7,6},{8,9},{9,8},{10,11... | collective-permute-start | bytes 1572872 | tf_op jit(solution)/shard_map/ppermute | solution.py:456
  23.9 13.5 %collective-permute-start.2 = (bf16[128,2048]{1,0:T(8,128)(2,1)}, bf16[128,2048]{1,0:T(8,128)(2,1)S(1)}, u32[]{:S(2)}, u32[]{:S(2)}) collective-permute-start(bf16[128,2048]{1,0:T(8,128)(2,1)} %get-tuple-element.41.far_hbm), channel_id=1, source_target_pairs={{1,2},{3,4},{5,6},{2,1},{4,3},{6,5},{9,10},{11,12},{13,14},{10,9},... | collective-permute-start | bytes 1572872 | tf_op jit(solution)/shard_map/ppermute | solution.py:455
  47.4 2.5 %collective-permute-start.6 = (bf16[4,4,32,128]{3,2,1,0:T(8,128)(2,1)S(1)}, bf16[4,4,32,128]{3,2,1,0:T(8,128)(2,1)S(1)}, u32[]{:S(2)}, u32[]{:S(2)}) collective-permute-start(bf16[4,4,32,128]{3,2,1,0:T(8,128)(2,1)S(1)} %bitcast.49), channel_id=1, source_target_pairs={{0,1},{1,0},{2,3},{3,2},{4,5},{5,4},{6,7},{7,6},{8,9},{9,8},{10,11... | collective-permute-start | bytes 393224 | tf_op jit(solution)/shard_map/ppermute | solution.py:377
  47.4 7.2 %collective-permute-start.5 = (bf16[24,4096]{1,0:T(8,128)(2,1)S(1)}, bf16[24,4096]{1,0:T(8,128)(2,1)S(1)}, u32[]{:S(2)}, u32[]{:S(2)}) collective-permute-start(bf16[24,4096]{1,0:T(8,128)(2,1)S(1)} %get-tuple-element.55), channel_id=1, source_target_pairs={{1,0},{2,1},{3,2},{4,3},{5,4},{6,5},{7,6},{9,8},{10,9},{11,10},{12... | collective-permute-start | bytes 589832 | tf_op jit(solution)/shard_map/ppermute | solution.py:483
  49.9 7.1 %collective-permute-start.7 = (bf16[4,32,128]{2,1,0:T(8,128)(2,1)S(1)}, bf16[4,32,128]{2,1,0:T(8,128)(2,1)S(1)}, u32[]{:S(2)}, u32[]{:S(2)}) collective-permute-start(bf16[4,32,128]{2,1,0:T(8,128)(2,1)S(1)} %get-tuple-element.79), channel_id=1, source_target_pairs={{0,8},{8,0},{16,24},{24,16},{1,9},{9,1},{17,25},{25,17},{2,10},{10... | collective-permute-start | bytes 98312 | tf_op jit(solution)/shard_map/ppermute | solution.py:379
  51.2 5.9 %collective-permute-start.8 = (bf16[4,32,128]{2,1,0:T(8,128)(2,1)S(1)}, bf16[4,32,128]{2,1,0:T(8,128)(2,1)S(1)}, u32[]{:S(2)}, u32[]{:S(2)}) collective-permute-start(bf16[4,32,128]{2,1,0:T(8,128)(2,1)S(1)} %get-tuple-element.78), channel_id=1, source_target_pairs={{0,16},{8,24},{16,0},{24,8},{1,17},{9,25},{17,1},{25,9},{2,18},{10... | collective-permute-start | bytes 98312 | tf_op jit(solution)/shard_map/ppermute | solution.py:379
  52.4 4.6 %collective-permute-start.9 = (bf16[4,32,128]{2,1,0:T(8,128)(2,1)S(1)}, bf16[4,32,128]{2,1,0:T(8,128)(2,1)S(1)}, u32[]{:S(2)}, u32[]{:S(2)}) collective-permute-start(bf16[4,32,128]{2,1,0:T(8,128)(2,1)S(1)} %get-tuple-element.77), channel_id=1, source_target_pairs={{0,24},{8,16},{16,8},{24,0},{1,25},{9,17},{17,9},{25,1},{2,26},{10... | collective-permute-start | bytes 98312 | tf_op jit(solution)/shard_map/ppermute | solution.py:379
  57.1 6.1 %collective-permute-start.10 = (bf16[4,32,128]{2,1,0:T(8,128)(2,1)S(1)}, bf16[4,32,128]{2,1,0:T(8,128)(2,1)S(1)}, u32[]{:S(2)}, u32[]{:S(2)}) collective-permute-start(bf16[4,32,128]{2,1,0:T(8,128)(2,1)S(1)} %get-tuple-element.62.refs_4_), channel_id=1, source_target_pairs={{0,2},{1,3},{2,0},{3,1},{4,6},{5,7},{6,4},{7,5},{8,10},{9,11},{10,... | collective-permute-start | bytes 98312 | tf_op jit(solution)/shard_map/ppermute | solution.py:386
  58.3 4.9 %collective-permute-start.11 = (bf16[4,32,128]{2,1,0:T(8,128)(2,1)S(1)}, bf16[4,32,128]{2,1,0:T(8,128)(2,1)S(1)}, u32[]{:S(2)}, u32[]{:S(2)}) collective-permute-start(bf16[4,32,128]{2,1,0:T(8,128)(2,1)S(1)} %get-tuple-element.62.refs_4_), channel_id=1, source_target_pairs={{0,4},{1,5},{2,6},{3,7},{4,0},{5,1},{6,2},{7,3},{8,12},{9,13},{10,... | collective-permute-start | bytes 98312 | tf_op jit(solution)/shard_map/ppermute | solution.py:386
  58.5 4.8 %collective-permute-start.12 = (bf16[4,32,128]{2,1,0:T(8,128)(2,1)S(1)}, bf16[4,32,128]{2,1,0:T(8,128)(2,1)S(1)}, u32[]{:S(2)}, u32[]{:S(2)}) collective-permute-start(bf16[4,32,128]{2,1,0:T(8,128)(2,1)S(1)} %get-tuple-element.62.refs_4_), channel_id=1, source_target_pairs={{0,6},{1,7},{2,4},{3,5},{4,2},{5,3},{6,0},{7,1},{8,14},{9,15},{10,... | collective-permute-start | bytes 98312 | tf_op jit(solution)/shard_map/ppermute | solution.py:386
  63.4 5.2 %collective-permute-start.13 = (bf16[4,32,128]{2,1,0:T(8,128)(2,1)S(1)}, bf16[4,32,128]{2,1,0:T(8,128)(2,1)S(1)}, u32[]{:S(2)}, u32[]{:S(2)}) collective-permute-start(bf16[4,32,128]{2,1,0:T(8,128)(2,1)S(1)} %add.10.refs_4_.refs_0_), channel_id=1, source_target_pairs={{0,8},{8,0},{16,24},{24,16},{1,9},{9,1},{17,25},{25,17},{2,10},{10... | collective-permute-start | bytes 98312 | tf_op jit(solution)/shard_map/ppermute | solution.py:388
  64.4 4.1 %collective-permute-start.14 = (bf16[4,32,128]{2,1,0:T(8,128)(2,1)S(1)}, bf16[4,32,128]{2,1,0:T(8,128)(2,1)S(1)}, u32[]{:S(2)}, u32[]{:S(2)}) collective-permute-start(bf16[4,32,128]{2,1,0:T(8,128)(2,1)S(1)} %add.10.refs_4_.refs_0_), channel_id=1, source_target_pairs={{0,16},{8,24},{16,0},{24,8},{1,17},{9,25},{17,1},{25,9},{2,18},{10... | collective-permute-start | bytes 98312 | tf_op jit(solution)/shard_map/ppermute | solution.py:388
  65.9 3.7 %collective-permute-start.15 = (bf16[4,32,128]{2,1,0:T(8,128)(2,1)S(1)}, bf16[4,32,128]{2,1,0:T(8,128)(2,1)S(1)}, u32[]{:S(2)}, u32[]{:S(2)}) collective-permute-start(bf16[4,32,128]{2,1,0:T(8,128)(2,1)S(1)} %add.10.refs_4_.refs_0_), channel_id=1, source_target_pairs={{0,24},{8,16},{16,8},{24,0},{1,25},{9,17},{17,9},{25,1},{2,26},{10... | collective-permute-start | bytes 98312 | tf_op jit(solution)/shard_map/ppermute | solution.py:388
  69.6 4.3 %collective-permute-start.16 = (bf16[4,4,32,128]{3,2,1,0:T(8,128)(2,1)S(1)}, bf16[4,4,32,128]{3,2,1,0:T(8,128)(2,1)S(1)}, u32[]{:S(2)}, u32[]{:S(2)}) collective-permute-start(bf16[4,4,32,128]{3,2,1,0:T(8,128)(2,1)S(1)} %join.1), channel_id=1, source_target_pairs={{0,1},{1,0},{2,3},{3,2},{4,5},{5,4},{6,7},{7,6},{8,9},{9,8},{10,11... | collective-permute-start | bytes 393224 | tf_op jit(solution)/shard_map/ppermute | solution.py:397

commit v5 on v4

--- a/solution.py
+++ b/solution.py
@@ -112,9 +112,9 @@
     out_ref[...] = jnp.concatenate([buffer[index].astype(F32)[HALO:] for index in range(3)], axis=0).astype(BF16)
 
 
-def feat_kernel(first, rows, taps_count, pieces, q_hbm, k_hbm, v_hbm, cot_hbm, tail_ref, taps_ref, near_hbm, far_hbm,
+def feat_kernel(first, rows, taps_count, pieces, tiles, q_ref, k_ref, v_ref, cot_ref, tail_ref, taps_ref, near_hbm, far_hbm,
                 qf_hbm, kf_hbm, vf_hbm, *scratch):
-    q_ref, k_ref, v_ref, cot_ref, mix_ref, gf_ref, qf_ref, kf_ref, vf_ref, ext, in_sem, out_sem = scratch
+    mix_ref, gf_ref, qf_ref, kf_ref, vf_ref, ext, out_sem = scratch
 
     def one(tile):
         lanes = lanes_at(tile * LANES)
@@ -123,7 +123,7 @@
         feats = []
         for which, src in enumerate((q_ref, k_ref, v_ref)):
             ext[which, pl.ds(0, HALO), :] = tails[which * HALO:(which + 1) * HALO]
-            ext[which, pl.ds(HALO, rows), :] = src[:, lanes].astype(F32)
+            ext[which, pl.ds(HALO, rows), :] = src[:, far].astype(F32)
             total = None
             for lag in range(taps_count):
                 term = taps_ref[lag, which:which + 1, far] * ext[which, pl.ds(HALO - lag, rows), :]
@@ -133,13 +133,36 @@
         kf_ref[:, lanes] = feats[1].astype(BF16)
         vf_ref[:, lanes] = feats[2].astype(BF16)
         mix_ref[:, lanes] = (feats[1] * feats[2]).astype(BF16)
-        gf_ref[:, lanes] = (cot_ref[:, lanes].astype(F32) * feats[0]).astype(BF16)
-
-    stream(pieces, pieces,
-           [(q_hbm, first, q_ref), (k_hbm, first, k_ref), (v_hbm, first, v_ref), (cot_hbm, first, cot_ref)],
-           [(mix_ref, (near_hbm, far_hbm), 0), (gf_ref, (far_hbm, near_hbm), 0), (qf_ref, qf_hbm, 0),
-            (kf_ref, kf_hbm, 0), (vf_ref, vf_hbm, 0)],
-           in_sem, out_sem, lambda piece: per_tile(piece, 1, one))
+        gf_ref[:, lanes] = (cot_ref[:, far].astype(F32) * feats[0]).astype(BF16)
+
+    stores = ((mix_ref, (near_hbm, far_hbm)), (gf_ref, (far_hbm, near_hbm)), (qf_ref, (qf_hbm, qf_hbm)),
+              (kf_ref, (kf_hbm, kf_hbm)), (vf_ref, (vf_hbm, vf_hbm)))
+
+    def store(index, piece, odd):
+        buffer, refs = stores[index]
+        lanes = lanes_at(piece * tiles * LANES, tiles * LANES)
+        return pltpu.make_async_copy(buffer.at[:, lanes], refs[odd].at[:, lanes], out_sem.at[index, piece])
+
+    def step(piece, carry):
+        def run(index, inner):
+            one(piece * tiles + index)
+            return inner
+
+        lax.fori_loop(0, tiles, run, 0)
+        for odd in range(2):
+            @pl.when(odd_core() == odd)
+            def _():
+                for index in range(len(stores)):
+                    store(index, piece, odd).start()
+        return carry
+
+    def end(piece, carry):
+        for index in range(len(stores)):
+            store(index, piece, 0).wait()
+        return carry
+
+    lax.fori_loop(0, pieces, step, 0)
+    lax.fori_loop(0, pieces, end, 0)
 
 
 def in_hbm(*arrays):
@@ -442,15 +465,15 @@
     made, halos = [], []
     for part in range(parts):
         feats = pl.pallas_call(
-            functools.partial(feat_kernel, part * width, rows, taps_count, pieces),
-            in_specs=[HBM] * 4 + [WHOLE] * 2,
+            functools.partial(feat_kernel, part * width, rows, taps_count, 4, in_half // 4),
+            in_specs=[WHOLE] * 6,
             out_specs=[HBM] * 5,
             out_shape=[pltpu.HBM((rows, width), BF16)] * 5,
-            scratch_shapes=buffers(9) + [pltpu.VMEM((3, rows + HALO, LANES), F32)] + sems(4, 5),
+            scratch_shapes=buffers(5) + [pltpu.VMEM((3, rows + HALO, LANES), F32), pltpu.SemaphoreType.DMA((5, 4))],
             compiler_params=compiler_params,
             cost_estimate=pl.CostEstimate(flops=50 * rows * width, bytes_accessed=18 * rows * width, transcendentals=0),
             name="features",
-        )(*in_hbm(query, key, value, cot), tails, feature_taps)
+        )(query, key, value, cot, tails, feature_taps)
         made.append(feats)
         far = lax.ppermute(feats[1], "ctx", chips)
         halos.append((lax.ppermute(feats[0], "ctx", cores), far))

time: 75.5 us -> 74.6 us (0.988)
  Pallas kernels: 39.5 us -> 37 us
  local copies, waits for them, and re-layouts: 0.27 us -> 1.3 us
  starting transfers between devices: 27.7 us -> 28.6 us
    pallas_call x2, Pallas kernels: 10.2 us -> 7.43 us  [body(): pl.pallas_call(functools.partial(feat_kernel, part * width, rows, taps_co...]
    unnamed x7 -> x17, local copies, waits for them, and re-layouts: 0.26 us -> 1.28 us
    ppermute x1, waiting for transfers between devices: 2.34 us -> 1.34 us  [body(): tails = lax.ppermute(tails, 'ctx', onward)]
  transfers between devices with their start and end apart: 17 -> 17, of which waited for: 5 -> 5; matrix products, arithmetic and copies ran while one was open for 0% -> 2% of each run, Pallas kernels for 30% -> 28%
where the time goes in v5:
time: 74.6 us; the launch traced here: 74 us
  Pallas kernels  37 us (50%)
  starting transfers between devices  28.6 us (38%)
  waiting for transfers between devices  6.06 us (8%)
  local copies, waits for them, and re-layouts  1.3 us (2%)
  between operations  0.99 us (1%)
    pallas_call x2, Pallas kernels, body(): pl.pallas_call(functools.partial(mix_kernel, part * width, rows, taps_cou...  20 us
    ppermute x2, starting transfers between devices, body(): far = lax.ppermute(feats[1], 'ctx', chips)  8.1 us
    pallas_call x2, Pallas kernels, body(): pl.pallas_call(functools.partial(feat_kernel, part * width, rows, taps_co...  7.43 us
    pallas_call x3, Pallas kernels, beside(): pl.pallas_call(functools.partial(back_kernel, which, rows, taps_count, pa...  7.32 us
    ppermute x1, starting transfers between devices, body(): tails = lax.ppermute(tails, 'ctx', onward)  4.73 us
    ppermute x3, starting transfers between devices, reduce_all(): lax.ppermute(low, 'ctx', swaps(ctx_count, pick))  3.89 us
    ppermute x1, starting transfers between devices, reduce_all(): other = lax.ppermute(whole, 'ctx', swaps(ctx_count, 1))  3.85 us
    ppermute x3, starting transfers between devices, reduce_all(): lax.ppermute(sent[mask], 'dp', swaps(dp_count, mask))  2.71 us
  transfers between devices with their start and end apart: 17, of which 5 were waited for; matrix products, arithmetic and copies ran while one was open for 2% of the time, Pallas kernels for 28%

profile of v5, /device:TPU:1, one launch (start us, length us, event | category | flops | bytes accessed | tf_op | source)
XLA Modules:
  0.0 74.0 jit_solution(18045254363319430018)
XLA Ops:
  0.6 0.0 copy-start
  0.6 0.0 copy-start.1
  0.7 0.0 copy-start.2
  0.7 0.0 copy-start.3
  0.7 1.2 %tails.1 = bf16[24,4096]{1,0:T(8,128)(2,1)S(1)} custom-call(bf16[128,4096]{1,0:T(8,128)(2,1)} %bitcast.24, bf16[128,4096]{1,0:T(8,128)(2,1)} %bitcast.29, bf16[128,4096]{1,0:T(8,128)(2,1)} %bitcast.34), custom_call_target="tpu_custom_call" | custom-call | tf_op jit(solution)/shard_map/tails/pallas_call | solution.py:452
  1.9 4.7 %collective-permute-start = (bf16[24,4096]{1,0:T(8,128)(2,1)S(1)}, bf16[24,4096]{1,0:T(8,128)(2,1)S(1)}, u32[]{:S(2)}, u32[]{:S(2)}) collective-permute-start(bf16[24,4096]{1,0:T(8,128)(2,1)S(1)} %tails.1), channel_id=1, source_target_pairs={{0,1},{1,2},{2,3},{3,4},{4,5},{5,6},{6,7},{8,9},{9,10},{10,11},{11... | collective-permute-start | bytes 589832 | tf_op jit(solution)/shard_map/ppermute | solution.py:461
  6.6 1.2 %copy.16.taps_ref.refs_3_ = f32[7,3,4096]{2,1,0:T(4,128)S(1)} copy(f32[7,3,4096]{2,0,1:T(8,128)} %param.11) | data formatting | bytes 688128 | tf_op args[4]
  7.9 0.0 copy-start.4
  7.9 1.3 %collective-permute-done.tail_ref = bf16[24,4096]{1,0:T(8,128)(2,1)S(1)} collective-permute-done((bf16[24,4096]{1,0:T(8,128)(2,1)S(1)}, bf16[24,4096]{1,0:T(8,128)(2,1)S(1)}, u32[]{:S(2)}, u32[]{:S(2)}) %collective-permute-start) | collective-permute-done | bytes 196640 | tf_op jit(solution)/shard_map/ppermute | solution.py:461
  9.2 0.0 copy-done
  9.2 0.0 copy-done.1
  9.2 0.0 copy-done.2
  9.2 0.0 copy-done.3
  9.2 3.7 %features.3 = (bf16[128,2048]{1,0:T(8,128)(2,1)}, bf16[128,2048]{1,0:T(8,128)(2,1)}, bf16[128,2048]{1,0:T(8,128)(2,1)}, bf16[128,2048]{1,0:T(8,128)(2,1)}, bf16[128,2048]{1,0:T(8,128)(2,1)}) custom-call(bf16[128,4096]{1,0:T(8,128)(2,1)S(1)} %bitcast.27, bf16[128,4096]{1,0:T(8,128)(2,1)S(1)} %bitcast.32, bf16[128,4096]{1,0:T(8,128)(2,1)S(1)} %bitcast.37, ...), custom_call_target="tpu_custom_call" | custom-call | flops 13107200 | bytes 4718592 | tf_op jit(solution)/shard_map/features/pallas_call | solution.py:467
  13.0 0.1 collective-permute-start.3
  13.1 0.0 copy-start.6
  13.1 4.5 %collective-permute-start.4 = (bf16[128,2048]{1,0:T(8,128)(2,1)}, bf16[128,2048]{1,0:T(8,128)(2,1)}, u32[]{:S(2)}, u32[]{:S(2)}) collective-permute-start(bf16[128,2048]{1,0:T(8,128)(2,1)} %get-tuple-element.46.far_hbm), channel_id=1, source_target_pairs={{1,2},{3,4},{5,6},{2,1},{4,3},{6,5},{9,10},{11,12},{13,14},{10,9},... | collective-permute-start | bytes 1572872 | tf_op jit(solution)/shard_map/ppermute | solution.py:478
  17.6 0.0 copy-done.4
  17.6 3.7 %features.2 = (bf16[128,2048]{1,0:T(8,128)(2,1)}, bf16[128,2048]{1,0:T(8,128)(2,1)}, bf16[128,2048]{1,0:T(8,128)(2,1)}, bf16[128,2048]{1,0:T(8,128)(2,1)}, bf16[128,2048]{1,0:T(8,128)(2,1)}) custom-call(bf16[128,4096]{1,0:T(8,128)(2,1)S(1)} %bitcast.28, bf16[128,4096]{1,0:T(8,128)(2,1)S(1)} %bitcast.33, bf16[128,4096]{1,0:T(8,128)(2,1)S(1)} %bitcast.38, ...), custom_call_target="tpu_custom_call" | custom-call | flops 13107200 | bytes 4718592 | tf_op jit(solution)/shard_map/features/pallas_call | solution.py:467
  21.3 0.0 copy-start.7
  21.3 0.1 collective-permute-start.1
  21.4 3.6 %collective-permute-start.2 = (bf16[128,2048]{1,0:T(8,128)(2,1)}, bf16[128,2048]{1,0:T(8,128)(2,1)S(1)}, u32[]{:S(2)}, u32[]{:S(2)}) collective-permute-start(bf16[128,2048]{1,0:T(8,128)(2,1)} %get-tuple-element.41.far_hbm), channel_id=1, source_target_pairs={{1,2},{3,4},{5,6},{2,1},{4,3},{6,5},{9,10},{11,12},{13,14},{10,9},... | collective-permute-start | bytes 1572872 | tf_op jit(solution)/shard_map/ppermute | solution.py:478
  25.0 0.0 collective-permute-done.3.got_near_hbm
  25.0 0.0 collective-permute-done.4.got_far_hbm
  25.0 0.0 copy-done.6
  25.0 0.0 copy-done.7
  25.1 10.0 %filters.2 = (bf16[128,4096]{1,0:T(8,128)(2,1)}, bf16[24,4096]{1,0:T(8,128)(2,1)S(1)}, bf16[128,2048]{1,0:T(8,128)(2,1)S(1)}, bf16[128,2048]{1,0:T(8,128)(2,1)S(...) custom-call(bf16[128,4096]{1,0:T(8,128)(2,1)} %bitcast.25, bf16[128,4096]{1,0:T(8,128)(2,1)} %bitcast.30, ...), custom_call_target="tpu_custom_call" | custom-call | flops 524288000 | bytes 7864320 | tf_op jit(solution)/shard_map/filters/pallas_call | solution.py:484
  35.1 0.0 collective-permute-done.1.got_near_hbm
  35.1 0.0 collective-permute-done.2.got_far_hbm
  35.1 9.9 %filters.3 = (bf16[128,4096]{1,0:T(8,128)(2,1)}, bf16[24,4096]{1,0:T(8,128)(2,1)S(1)}, bf16[128,2048]{1,0:T(8,128)(2,1)S(1)}, bf16[128,2048]{1,0:T(8,128)(2,1)S(...) custom-call(bf16[128,4096]{1,0:T(8,128)(2,1)} %bitcast.26, ...), custom_call_target="tpu_custom_call", output_to_operand_aliasing={{0}: (14, {}), {1}: (15, {})} | custom-call | flops 524288000 | bytes 7864320 | tf_op jit(solution)/shard_map/filters/pallas_call | solution.py:484
  45.1 0.1 collective-permute-start.6
  45.2 2.4 %collective-permute-start.5 = (bf16[24,4096]{1,0:T(8,128)(2,1)S(1)}, bf16[24,4096]{1,0:T(8,128)(2,1)S(1)}, u32[]{:S(2)}, u32[]{:S(2)}) collective-permute-start(bf16[24,4096]{1,0:T(8,128)(2,1)S(1)} %get-tuple-element.55), channel_id=1, source_target_pairs={{1,0},{2,1},{3,2},{4,3},{5,4},{6,5},{7,6},{9,8},{10,9},{11,10},{12... | collective-permute-start | bytes 589832 | tf_op jit(solution)/shard_map/ppermute | solution.py:506
  47.6 0.0 collective-permute-done.6
  47.6 0.0 copy-start.5
  47.7 1.3 %collective-permute-start.7 = (bf16[4,32,128]{2,1,0:T(8,128)(2,1)S(1)}, bf16[4,32,128]{2,1,0:T(8,128)(2,1)S(1)}, u32[]{:S(2)}, u32[]{:S(2)}) collective-permute-start(bf16[4,32,128]{2,1,0:T(8,128)(2,1)S(1)} %get-tuple-element.79), channel_id=1, source_target_pairs={{0,8},{8,0},{16,24},{24,16},{1,9},{9,1},{17,25},{25,17},{2,10},{10... | collective-permute-start | bytes 98312 | tf_op jit(solution)/shard_map/ppermute | solution.py:402
  48.9 1.2 %collective-permute-start.8 = (bf16[4,32,128]{2,1,0:T(8,128)(2,1)S(1)}, bf16[4,32,128]{2,1,0:T(8,128)(2,1)S(1)}, u32[]{:S(2)}, u32[]{:S(2)}) collective-permute-start(bf16[4,32,128]{2,1,0:T(8,128)(2,1)S(1)} %get-tuple-element.78), channel_id=1, source_target_pairs={{0,16},{8,24},{16,0},{24,8},{1,17},{9,25},{17,1},{25,9},{2,18},{10... | collective-permute-start | bytes 98312 | tf_op jit(solution)/shard_map/ppermute | solution.py:402
  50.2 0.2 collective-permute-start.9
  50.4 2.0 %collective-permute-done.5.refs_2_ = bf16[24,4096]{1,0:T(8,128)(2,1)S(1)} collective-permute-done((bf16[24,4096]{1,0:T(8,128)(2,1)S(1)}, bf16[24,4096]{1,0:T(8,128)(2,1)S(1)}, u32[]{:S(2)}, u32[]{:S(2)}) %collective-permute-start.5) | collective-permute-done | bytes 196640 | tf_op jit(solution)/shard_map/ppermute | solution.py:506
  52.3 0.0 copy-done.5
  52.3 2.4 %features_back.3 = (bf16[128,4096]{1,0:T(8,128)(2,1)}, f32[8,128]{1,0:T(8,128)S(1)}) custom-call(bf16[128,2048]{1,0:T(8,128)(2,1)S(1)} %get-tuple-element.53.refs_0_, bf16[128,2048]{1,0:T(8,128)(2,1)S(1)} %get-tuple-element.54.refs_1_, bf16[24,4096]{1,0:T(8,128)(2,1)S(1)} %collective-permute-done.5.refs_2_, f32[7,3,4096]{2,1,0:T(4,128)S(1)} %copy-done.5, ...), custom_call_target="tpu_custom_call" | custom-call | flops 8388608 | bytes 2097152 | tf_op jit(solution)/shard_map/features_back/pallas_call | solution.py:509
  54.8 0.0 collective-permute-done.7.refs_0_
  54.8 0.0 collective-permute-done.8.refs_1_
  54.8 0.0 collective-permute-done.9.refs_2_
  54.8 1.7 %collective-permute-start.10 = (bf16[4,32,128]{2,1,0:T(8,128)(2,1)S(1)}, bf16[4,32,128]{2,1,0:T(8,128)(2,1)S(1)}, u32[]{:S(2)}, u32[]{:S(2)}) collective-permute-start(bf16[4,32,128]{2,1,0:T(8,128)(2,1)S(1)} %get-tuple-element.62.refs_4_), channel_id=1, source_target_pairs={{0,2},{1,3},{2,0},{3,1},{4,6},{5,7},{6,4},{7,5},{8,10},{9,11},{10,... | collective-permute-start | bytes 98312 | tf_op jit(solution)/shard_map/ppermute | solution.py:409
  56.6 0.8 %collective-permute-start.11 = (bf16[4,32,128]{2,1,0:T(8,128)(2,1)S(1)}, bf16[4,32,128]{2,1,0:T(8,128)(2,1)S(1)}, u32[]{:S(2)}, u32[]{:S(2)}) collective-permute-start(bf16[4,32,128]{2,1,0:T(8,128)(2,1)S(1)} %get-tuple-element.62.refs_4_), channel_id=1, source_target_pairs={{0,4},{1,5},{2,6},{3,7},{4,0},{5,1},{6,2},{7,3},{8,12},{9,13},{10,... | collective-permute-start | bytes 98312 | tf_op jit(solution)/shard_map/ppermute | solution.py:409
  57.4 1.4 %collective-permute-start.12 = (bf16[4,32,128]{2,1,0:T(8,128)(2,1)S(1)}, bf16[4,32,128]{2,1,0:T(8,128)(2,1)S(1)}, u32[]{:S(2)}, u32[]{:S(2)}) collective-permute-start(bf16[4,32,128]{2,1,0:T(8,128)(2,1)S(1)} %get-tuple-element.62.refs_4_), channel_id=1, source_target_pairs={{0,6},{1,7},{2,4},{3,5},{4,2},{5,3},{6,0},{7,1},{8,14},{9,15},{10,... | collective-permute-start | bytes 98312 | tf_op jit(solution)/shard_map/ppermute | solution.py:409
  58.7 2.4 %features_back.4 = (bf16[128,4096]{1,0:T(8,128)(2,1)}, f32[8,128]{1,0:T(8,128)S(1)}) custom-call(bf16[128,2048]{1,0:T(8,128)(2,1)S(1)} %get-tuple-element.59.refs_0_, bf16[128,2048]{1,0:T(8,128)(2,1)S(1)} %get-tuple-element.60.refs_1_, bf16[24,4096]{1,0:T(8,128)(2,1)S(1)} %collective-permute-done.5.refs_2_, f32[7,3,4096]{2,1,0:T(4,128)S(1)} %copy-done.5, ...), custom_call_target="tpu_custom_call" | custom-call | flops 8388608 | bytes 2097152 | tf_op jit(solution)/shard_map/features_back/pallas_call | solution.py:509
  61.2 0.0 collective-permute-done.10.refs_0_
  61.2 0.0 collective-permute-done.11.refs_1_
  61.2 0.8 %collective-permute-done.12.refs_2_ = bf16[4,32,128]{2,1,0:T(8,128)(2,1)S(1)} collective-permute-done((bf16[4,32,128]{2,1,0:T(8,128)(2,1)S(1)}, bf16[4,32,128]{2,1,0:T(8,128)(2,1)S(1)}, u32[]{:S(2)}, u32[]{:S(2)}) %collective-permute-start.12) | collective-permute-done | bytes 32800 | tf_op jit(solution)/shard_map/ppermute | solution.py:409
  62.0 1.2 %collective-permute-start.13 = (bf16[4,32,128]{2,1,0:T(8,128)(2,1)S(1)}, bf16[4,32,128]{2,1,0:T(8,128)(2,1)S(1)}, u32[]{:S(2)}, u32[]{:S(2)}) collective-permute-start(bf16[4,32,128]{2,1,0:T(8,128)(2,1)S(1)} %add.10.refs_4_.refs_0_), channel_id=1, source_target_pairs={{0,8},{8,0},{16,24},{24,16},{1,9},{9,1},{17,25},{25,17},{2,10},{10... | collective-permute-start | bytes 98312 | tf_op jit(solution)/shard_map/ppermute | solution.py:411
  63.2 1.2 %collective-permute-start.14 = (bf16[4,32,128]{2,1,0:T(8,128)(2,1)S(1)}, bf16[4,32,128]{2,1,0:T(8,128)(2,1)S(1)}, u32[]{:S(2)}, u32[]{:S(2)}) collective-permute-start(bf16[4,32,128]{2,1,0:T(8,128)(2,1)S(1)} %add.10.refs_4_.refs_0_), channel_id=1, source_target_pairs={{0,16},{8,24},{16,0},{24,8},{1,17},{9,25},{17,1},{25,9},{2,18},{10... | collective-permute-start | bytes 98312 | tf_op jit(solution)/shard_map/ppermute | solution.py:411
  64.5 0.3 collective-permute-start.15
  64.8 2.4 %features_back.5 = (bf16[128,4096]{1,0:T(8,128)(2,1)}, f32[8,128]{1,0:T(8,128)S(1)}) custom-call(bf16[128,2048]{1,0:T(8,128)(2,1)S(1)} %get-tuple-element.64.refs_0_, bf16[128,2048]{1,0:T(8,128)(2,1)S(1)} %get-tuple-element.65.refs_1_, bf16[24,4096]{1,0:T(8,128)(2,1)S(1)} %collective-permute-done.5.refs_2_, f32[7,3,4096]{2,1,0:T(4,128)S(1)} %copy-done.5, ...), custom_call_target="tpu_custom_call" | custom-call | flops 8388608 | bytes 2097152 | tf_op jit(solution)/shard_map/features_back/pallas_call | solution.py:509
  67.2 0.0 collective-permute-done.13.refs_1_
  67.2 0.0 collective-permute-done.14.refs_2_
  67.2 0.9 %collective-permute-done.15.refs_3_ = bf16[4,32,128]{2,1,0:T(8,128)(2,1)S(1)} collective-permute-done((bf16[4,32,128]{2,1,0:T(8,128)(2,1)S(1)}, bf16[4,32,128]{2,1,0:T(8,128)(2,1)S(1)}, u32[]{:S(2)}, u32[]{:S(2)}) %collective-permute-start.15) | collective-permute-done | bytes 32800 | tf_op jit(solution)/shard_map/ppermute | solution.py:411
  68.2 3.9 %collective-permute-start.16 = (bf16[4,4,32,128]{3,2,1,0:T(8,128)(2,1)S(1)}, bf16[4,4,32,128]{3,2,1,0:T(8,128)(2,1)S(1)}, u32[]{:S(2)}, u32[]{:S(2)}) collective-permute-start(bf16[4,4,32,128]{3,2,1,0:T(8,128)(2,1)S(1)} %join.1), channel_id=1, source_target_pairs={{0,1},{1,0},{2,3},{3,2},{4,5},{5,4},{6,7},{7,6},{8,9},{9,8},{10,11... | collective-permute-start | bytes 393224 | tf_op jit(solution)/shard_map/ppermute | solution.py:420
  72.0 1.0 %collective-permute-done.16 = bf16[4,4,32,128]{3,2,1,0:T(8,128)(2,1)S(1)} collective-permute-done((bf16[4,4,32,128]{3,2,1,0:T(8,128)(2,1)S(1)}, bf16[4,4,32,128]{3,2,1,0:T(8,128)(2,1)S(1)}, u32[]{:S(2)}, u32[]{:S(2)}) %collective-permute-start.16) | collective-permute-done | bytes 131104 | tf_op jit(solution)/shard_map/ppermute | solution.py:420
  73.0 1.0 %unpack.1 = (f32[3,7,4096]{2,1,0:T(8,128)}, f32[256,128]{1,0:T(8,128)}, f32[1,4096]{1,0:T(1,128)}) custom-call(bf16[16,32,128]{2,1,0:T(8,128)(2,1)S(1)} %bitcast.43, bf16[16,32,128]{2,1,0:T(8,128)(2,1)S(1)} %bitcast.44), custom_call_target="tpu_custom_call" | custom-call | tf_op jit(solution)/shard_map/unpack/pallas_call | solution.py:527
  (7 shorter events, 0.1 us)
Async XLA Ops:
  0.6 8.6 %copy-start = (bf16[1,128,4096]{2,1,0:T(8,128)(2,1)S(1)}, bf16[1,128,4096]{2,1,0:T(8,128)(2,1)}, u32[]{:S(2)}) copy-start(bf16[1,128,4096]{2,1,0:T(8,128)(2,1)} %param.7) | copy-start | bytes 3145732
  0.6 8.6 %copy-start.1 = (bf16[1,128,4096]{2,1,0:T(8,128)(2,1)S(1)}, bf16[1,128,4096]{2,1,0:T(8,128)(2,1)}, u32[]{:S(2)}) copy-start(bf16[1,128,4096]{2,1,0:T(8,128)(2,1)} %param.8) | copy-start | bytes 3145732
  0.7 8.6 %copy-start.2 = (bf16[1,128,4096]{2,1,0:T(8,128)(2,1)S(1)}, bf16[1,128,4096]{2,1,0:T(8,128)(2,1)}, u32[]{:S(2)}) copy-start(bf16[1,128,4096]{2,1,0:T(8,128)(2,1)} %param.9) | copy-start | bytes 3145732
  0.7 8.6 %copy-start.3 = (bf16[1,128,4096]{2,1,0:T(8,128)(2,1)S(1)}, bf16[1,128,4096]{2,1,0:T(8,128)(2,1)}, u32[]{:S(2)}) copy-start(bf16[1,128,4096]{2,1,0:T(8,128)(2,1)} %param.10) | copy-start | bytes 3145732
  1.9 7.3 %collective-permute-start = (bf16[24,4096]{1,0:T(8,128)(2,1)S(1)}, bf16[24,4096]{1,0:T(8,128)(2,1)S(1)}, u32[]{:S(2)}, u32[]{:S(2)}) collective-permute-start(bf16[24,4096]{1,0:T(8,128)(2,1)S(1)} %tails.1), channel_id=1, source_target_pairs={{0,1},{1,2},{2,3},{3,4},{4,5},{5,6},{6,7},{8,9},{9,10},{10,11},{11... | collective-permute-start | bytes 589832 | tf_op jit(solution)/shard_map/ppermute | solution.py:461
  7.9 9.7 %copy-start.4 = (f32[7,3,4096]{2,1,0:T(4,128)}, f32[7,3,4096]{2,1,0:T(4,128)S(1)}, u32[]{:S(2)}) copy-start(f32[7,3,4096]{2,1,0:T(4,128)S(1)} %copy.16.taps_ref.refs_3_) | copy-start | bytes 1032196
  13.0 12.0 %collective-permute-start.3 = (bf16[128,2048]{1,0:T(8,128)(2,1)}, bf16[128,2048]{1,0:T(8,128)(2,1)}, u32[]{:S(2)}, u32[]{:S(2)}) collective-permute-start(bf16[128,2048]{1,0:T(8,128)(2,1)} %get-tuple-element.45.near_hbm), channel_id=1, source_target_pairs={{0,1},{1,0},{2,3},{3,2},{4,5},{5,4},{6,7},{7,6},{8,9},{9,8},{10,11... | collective-permute-start | bytes 1572872 | tf_op jit(solution)/shard_map/ppermute | solution.py:479
  13.1 12.0 %copy-start.6 = (f32[256,128]{1,0:T(8,128)S(1)}, f32[256,128]{1,0:T(8,128)}, u32[]{:S(2)}) copy-start(f32[256,128]{1,0:T(8,128)} %filt_ref.3) | copy-start | bytes 393220
  13.1 11.9 %collective-permute-start.4 = (bf16[128,2048]{1,0:T(8,128)(2,1)}, bf16[128,2048]{1,0:T(8,128)(2,1)}, u32[]{:S(2)}, u32[]{:S(2)}) collective-permute-start(bf16[128,2048]{1,0:T(8,128)(2,1)} %get-tuple-element.46.far_hbm), channel_id=1, source_target_pairs={{1,2},{3,4},{5,6},{2,1},{4,3},{6,5},{9,10},{11,12},{13,14},{10,9},... | collective-permute-start | bytes 1572872 | tf_op jit(solution)/shard_map/ppermute | solution.py:478
  21.3 3.7 %copy-start.7 = (f32[4096]{0:T(1024)S(1)}, f32[4096]{0:T(1024)}, u32[]{:S(2)}) copy-start(f32[4096]{0:T(1024)} %param.13) | copy-start | bytes 49156
  21.3 13.8 %collective-permute-start.1 = (bf16[128,2048]{1,0:T(8,128)(2,1)}, bf16[128,2048]{1,0:T(8,128)(2,1)S(1)}, u32[]{:S(2)}, u32[]{:S(2)}) collective-permute-start(bf16[128,2048]{1,0:T(8,128)(2,1)} %get-tuple-element.40.near_hbm), channel_id=1, source_target_pairs={{0,1},{1,0},{2,3},{3,2},{4,5},{5,4},{6,7},{7,6},{8,9},{9,8},{10,11... | collective-permute-start | bytes 1572872 | tf_op jit(solution)/shard_map/ppermute | solution.py:479
  21.4 13.7 %collective-permute-start.2 = (bf16[128,2048]{1,0:T(8,128)(2,1)}, bf16[128,2048]{1,0:T(8,128)(2,1)S(1)}, u32[]{:S(2)}, u32[]{:S(2)}) collective-permute-start(bf16[128,2048]{1,0:T(8,128)(2,1)} %get-tuple-element.41.far_hbm), channel_id=1, source_target_pairs={{1,2},{3,4},{5,6},{2,1},{4,3},{6,5},{9,10},{11,12},{13,14},{10,9},... | collective-permute-start | bytes 1572872 | tf_op jit(solution)/shard_map/ppermute | solution.py:478
  45.1 2.5 %collective-permute-start.6 = (bf16[4,4,32,128]{3,2,1,0:T(8,128)(2,1)S(1)}, bf16[4,4,32,128]{3,2,1,0:T(8,128)(2,1)S(1)}, u32[]{:S(2)}, u32[]{:S(2)}) collective-permute-start(bf16[4,4,32,128]{3,2,1,0:T(8,128)(2,1)S(1)} %bitcast.49), channel_id=1, source_target_pairs={{0,1},{1,0},{2,3},{3,2},{4,5},{5,4},{6,7},{7,6},{8,9},{9,8},{10,11... | collective-permute-start | bytes 393224 | tf_op jit(solution)/shard_map/ppermute | solution.py:400
  45.2 7.2 %collective-permute-start.5 = (bf16[24,4096]{1,0:T(8,128)(2,1)S(1)}, bf16[24,4096]{1,0:T(8,128)(2,1)S(1)}, u32[]{:S(2)}, u32[]{:S(2)}) collective-permute-start(bf16[24,4096]{1,0:T(8,128)(2,1)S(1)} %get-tuple-element.55), channel_id=1, source_target_pairs={{1,0},{2,1},{3,2},{4,3},{5,4},{6,5},{7,6},{9,8},{10,9},{11,10},{12... | collective-permute-start | bytes 589832 | tf_op jit(solution)/shard_map/ppermute | solution.py:506
  47.6 4.8 %copy-start.5 = (f32[7,3,4096]{2,1,0:T(4,128)S(1)}, f32[7,3,4096]{2,1,0:T(4,128)}, u32[]{:S(2)}) copy-start(f32[7,3,4096]{2,1,0:T(4,128)} %copy-done.4) | copy-start | bytes 1032196
  47.7 7.1 %collective-permute-start.7 = (bf16[4,32,128]{2,1,0:T(8,128)(2,1)S(1)}, bf16[4,32,128]{2,1,0:T(8,128)(2,1)S(1)}, u32[]{:S(2)}, u32[]{:S(2)}) collective-permute-start(bf16[4,32,128]{2,1,0:T(8,128)(2,1)S(1)} %get-tuple-element.79), channel_id=1, source_target_pairs={{0,8},{8,0},{16,24},{24,16},{1,9},{9,1},{17,25},{25,17},{2,10},{10... | collective-permute-start | bytes 98312 | tf_op jit(solution)/shard_map/ppermute | solution.py:402
  48.9 5.9 %collective-permute-start.8 = (bf16[4,32,128]{2,1,0:T(8,128)(2,1)S(1)}, bf16[4,32,128]{2,1,0:T(8,128)(2,1)S(1)}, u32[]{:S(2)}, u32[]{:S(2)}) collective-permute-start(bf16[4,32,128]{2,1,0:T(8,128)(2,1)S(1)} %get-tuple-element.78), channel_id=1, source_target_pairs={{0,16},{8,24},{16,0},{24,8},{1,17},{9,25},{17,1},{25,9},{2,18},{10... | collective-permute-start | bytes 98312 | tf_op jit(solution)/shard_map/ppermute | solution.py:402
  50.2 4.6 %collective-permute-start.9 = (bf16[4,32,128]{2,1,0:T(8,128)(2,1)S(1)}, bf16[4,32,128]{2,1,0:T(8,128)(2,1)S(1)}, u32[]{:S(2)}, u32[]{:S(2)}) collective-permute-start(bf16[4,32,128]{2,1,0:T(8,128)(2,1)S(1)} %get-tuple-element.77), channel_id=1, source_target_pairs={{0,24},{8,16},{16,8},{24,0},{1,25},{9,17},{17,9},{25,1},{2,26},{10... | collective-permute-start | bytes 98312 | tf_op jit(solution)/shard_map/ppermute | solution.py:402
  54.8 6.3 %collective-permute-start.10 = (bf16[4,32,128]{2,1,0:T(8,128)(2,1)S(1)}, bf16[4,32,128]{2,1,0:T(8,128)(2,1)S(1)}, u32[]{:S(2)}, u32[]{:S(2)}) collective-permute-start(bf16[4,32,128]{2,1,0:T(8,128)(2,1)S(1)} %get-tuple-element.62.refs_4_), channel_id=1, source_target_pairs={{0,2},{1,3},{2,0},{3,1},{4,6},{5,7},{6,4},{7,5},{8,10},{9,11},{10,... | collective-permute-start | bytes 98312 | tf_op jit(solution)/shard_map/ppermute | solution.py:409
  56.6 4.6 %collective-permute-start.11 = (bf16[4,32,128]{2,1,0:T(8,128)(2,1)S(1)}, bf16[4,32,128]{2,1,0:T(8,128)(2,1)S(1)}, u32[]{:S(2)}, u32[]{:S(2)}) collective-permute-start(bf16[4,32,128]{2,1,0:T(8,128)(2,1)S(1)} %get-tuple-element.62.refs_4_), channel_id=1, source_target_pairs={{0,4},{1,5},{2,6},{3,7},{4,0},{5,1},{6,2},{7,3},{8,12},{9,13},{10,... | collective-permute-start | bytes 98312 | tf_op jit(solution)/shard_map/ppermute | solution.py:409
  57.4 4.6 %collective-permute-start.12 = (bf16[4,32,128]{2,1,0:T(8,128)(2,1)S(1)}, bf16[4,32,128]{2,1,0:T(8,128)(2,1)S(1)}, u32[]{:S(2)}, u32[]{:S(2)}) collective-permute-start(bf16[4,32,128]{2,1,0:T(8,128)(2,1)S(1)} %get-tuple-element.62.refs_4_), channel_id=1, source_target_pairs={{0,6},{1,7},{2,4},{3,5},{4,2},{5,3},{6,0},{7,1},{8,14},{9,15},{10,... | collective-permute-start | bytes 98312 | tf_op jit(solution)/shard_map/ppermute | solution.py:409
  62.0 5.2 %collective-permute-start.13 = (bf16[4,32,128]{2,1,0:T(8,128)(2,1)S(1)}, bf16[4,32,128]{2,1,0:T(8,128)(2,1)S(1)}, u32[]{:S(2)}, u32[]{:S(2)}) collective-permute-start(bf16[4,32,128]{2,1,0:T(8,128)(2,1)S(1)} %add.10.refs_4_.refs_0_), channel_id=1, source_target_pairs={{0,8},{8,0},{16,24},{24,16},{1,9},{9,1},{17,25},{25,17},{2,10},{10... | collective-permute-start | bytes 98312 | tf_op jit(solution)/shard_map/ppermute | solution.py:411
  63.2 4.0 %collective-permute-start.14 = (bf16[4,32,128]{2,1,0:T(8,128)(2,1)S(1)}, bf16[4,32,128]{2,1,0:T(8,128)(2,1)S(1)}, u32[]{:S(2)}, u32[]{:S(2)}) collective-permute-start(bf16[4,32,128]{2,1,0:T(8,128)(2,1)S(1)} %add.10.refs_4_.refs_0_), channel_id=1, source_target_pairs={{0,16},{8,24},{16,0},{24,8},{1,17},{9,25},{17,1},{25,9},{2,18},{10... | collective-permute-start | bytes 98312 | tf_op jit(solution)/shard_map/ppermute | solution.py:411
  64.5 3.7 %collective-permute-start.15 = (bf16[4,32,128]{2,1,0:T(8,128)(2,1)S(1)}, bf16[4,32,128]{2,1,0:T(8,128)(2,1)S(1)}, u32[]{:S(2)}, u32[]{:S(2)}) collective-permute-start(bf16[4,32,128]{2,1,0:T(8,128)(2,1)S(1)} %add.10.refs_4_.refs_0_), channel_id=1, source_target_pairs={{0,24},{8,16},{16,8},{24,0},{1,25},{9,17},{17,9},{25,1},{2,26},{10... | collective-permute-start | bytes 98312 | tf_op jit(solution)/shard_map/ppermute | solution.py:411
  68.2 4.8 %collective-permute-start.16 = (bf16[4,4,32,128]{3,2,1,0:T(8,128)(2,1)S(1)}, bf16[4,4,32,128]{3,2,1,0:T(8,128)(2,1)S(1)}, u32[]{:S(2)}, u32[]{:S(2)}) collective-permute-start(bf16[4,4,32,128]{3,2,1,0:T(8,128)(2,1)S(1)} %join.1), channel_id=1, source_target_pairs={{0,1},{1,0},{2,3},{3,2},{4,5},{5,4},{6,7},{7,6},{8,9},{9,8},{10,11... | collective-permute-start | bytes 393224 | tf_op jit(solution)/shard_map/ppermute | solution.py:420

commit v6 on v5

--- a/solution.py
+++ b/solution.py
@@ -400,14 +400,13 @@
     half = mine.astype(F32) + lax.ppermute(theirs, "ctx", swaps(ctx_count, 1)).astype(F32)
     sent = half.astype(BF16)
     arrived = [lax.ppermute(sent[mask], "dp", swaps(dp_count, mask)) for mask in range(1, dp_count)]
-    low, total = add(half[0], arrived, beside[0](sent))
-    work = beside[1](low)
+    low, total = add(half[0], arrived, beside.pop(0)(sent))
     mask = 2
     while mask < ctx_count:
-        picks = (mask, 2 * mask, 3 * mask) if mask * 2 < ctx_count else (mask,)
-        mask *= 4
-        low, total = add(total, [lax.ppermute(low, "ctx", swaps(ctx_count, pick)) for pick in picks], work,
-                         mask >= ctx_count)
+        arrived = lax.ppermute(low, "ctx", swaps(ctx_count, mask))
+        work = beside.pop(0)(low) if beside else low
+        low, total = add(total, [arrived], work, 2 * mask >= ctx_count)
+        mask *= 2
     quarters = [low] + [lax.ppermute(low, "dp", swaps(dp_count, mask)) for mask in range(1, dp_count)]
     whole = pl.pallas_call(
         functools.partial(join_kernel, dp_count),
@@ -416,8 +415,10 @@
         out_shape=jax.ShapeDtypeStruct((dp_count,) + low.shape, BF16),
         compiler_params=pltpu.CompilerParams(vmem_limit_bytes=SMALL),
         name="join",
-    )(*quarters, beside[2](low))
+    )(*quarters, beside.pop(0)(low) if beside else low)
     other = lax.ppermute(whole, "ctx", swaps(ctx_count, 1))
+    while beside:
+        beside.pop(0)(low)
     return whole, other
 
 

time: 74.6 us -> 74.1 us (level)
  starting transfers between devices: 28.6 us -> 25.6 us
  waiting for transfers between devices: 6.06 us -> 8.53 us
    ppermute x3, waiting for transfers between devices: 0.93 us -> 3.66 us  [reduce_all(): lax.ppermute(low, 'dp', swaps(dp_count, mask))]
    ppermute x1, starting transfers between devices: 3.85 us -> 1.93 us  [reduce_all(): other = lax.ppermute(whole, 'ctx', swaps(ctx_count, 1))]
    ppermute x3 -> x2, starting transfers between devices: 3.89 us -> 2.81 us  [reduce_all(): arrived = lax.ppermute(low, 'ctx', swaps(ctx_count, mask))]
  transfers between devices with their start and end apart: 17 -> 16, of which waited for: 5 -> 7; matrix products, arithmetic and copies ran while one was open for 2% -> 2% of each run, Pallas kernels for 28% -> 29%
where the time goes in v6:
time: 74.1 us; the launch traced here: 73.5 us
  Pallas kernels  37 us (50%)
  starting transfers between devices  25.6 us (35%)
  waiting for transfers between devices  8.53 us (12%)
  local copies, waits for them, and re-layouts  1.3 us (2%)
  between operations  0.98 us (1%)
    pallas_call x2, Pallas kernels, body(): pl.pallas_call(functools.partial(mix_kernel, part * width, rows, taps_cou...  20 us
    ppermute x2, starting transfers between devices, body(): far = lax.ppermute(feats[1], 'ctx', chips)  8.1 us
    pallas_call x2, Pallas kernels, body(): pl.pallas_call(functools.partial(feat_kernel, part * width, rows, taps_co...  7.43 us
    pallas_call x3, Pallas kernels, beside(): pl.pallas_call(functools.partial(back_kernel, which, rows, taps_count, pa...  7.32 us
    ppermute x1, starting transfers between devices, body(): tails = lax.ppermute(tails, 'ctx', onward)  4.73 us
    ppermute x3, waiting for transfers between devices, reduce_all(): lax.ppermute(low, 'dp', swaps(dp_count, mask))  3.66 us
    ppermute x2, starting transfers between devices, reduce_all(): arrived = lax.ppermute(low, 'ctx', swaps(ctx_count, mask))  2.81 us
    ppermute x3, starting transfers between devices, reduce_all(): lax.ppermute(low, 'dp', swaps(dp_count, mask))  2.74 us
  transfers between devices with their start and end apart: 16, of which 7 were waited for; matrix products, arithmetic and copies ran while one was open for 2% of the time, Pallas kernels for 29%

profile of v6, /device:TPU:1, one launch (start us, length us, event | category | flops | bytes accessed | tf_op | source)
XLA Modules:
  0.0 73.5 jit_solution(7226512242103602185)
XLA Ops:
  0.6 0.0 copy-start
  0.6 0.0 copy-start.1
  0.7 0.0 copy-start.2
  0.7 0.0 copy-start.3
  0.7 1.2 %tails.1 = bf16[24,4096]{1,0:T(8,128)(2,1)S(1)} custom-call(bf16[128,4096]{1,0:T(8,128)(2,1)} %bitcast.24, bf16[128,4096]{1,0:T(8,128)(2,1)} %bitcast.29, bf16[128,4096]{1,0:T(8,128)(2,1)} %bitcast.34), custom_call_target="tpu_custom_call" | custom-call | tf_op jit(solution)/shard_map/tails/pallas_call | solution.py:453
  1.9 4.7 %collective-permute-start = (bf16[24,4096]{1,0:T(8,128)(2,1)S(1)}, bf16[24,4096]{1,0:T(8,128)(2,1)S(1)}, u32[]{:S(2)}, u32[]{:S(2)}) collective-permute-start(bf16[24,4096]{1,0:T(8,128)(2,1)S(1)} %tails.1), channel_id=1, source_target_pairs={{0,1},{1,2},{2,3},{3,4},{4,5},{5,6},{6,7},{8,9},{9,10},{10,11},{11... | collective-permute-start | bytes 589832 | tf_op jit(solution)/shard_map/ppermute | solution.py:462
  6.6 1.2 %copy.16.taps_ref.refs_3_ = f32[7,3,4096]{2,1,0:T(4,128)S(1)} copy(f32[7,3,4096]{2,0,1:T(8,128)} %param.11) | data formatting | bytes 688128 | tf_op args[4]
  7.9 0.0 copy-start.4
  7.9 1.3 %collective-permute-done.tail_ref = bf16[24,4096]{1,0:T(8,128)(2,1)S(1)} collective-permute-done((bf16[24,4096]{1,0:T(8,128)(2,1)S(1)}, bf16[24,4096]{1,0:T(8,128)(2,1)S(1)}, u32[]{:S(2)}, u32[]{:S(2)}) %collective-permute-start) | collective-permute-done | bytes 196640 | tf_op jit(solution)/shard_map/ppermute | solution.py:462
  9.2 0.0 copy-done
  9.2 0.0 copy-done.1
  9.2 0.0 copy-done.2
  9.2 0.0 copy-done.3
  9.2 3.7 %features.3 = (bf16[128,2048]{1,0:T(8,128)(2,1)}, bf16[128,2048]{1,0:T(8,128)(2,1)}, bf16[128,2048]{1,0:T(8,128)(2,1)}, bf16[128,2048]{1,0:T(8,128)(2,1)}, bf16[128,2048]{1,0:T(8,128)(2,1)}) custom-call(bf16[128,4096]{1,0:T(8,128)(2,1)S(1)} %bitcast.27, bf16[128,4096]{1,0:T(8,128)(2,1)S(1)} %bitcast.32, bf16[128,4096]{1,0:T(8,128)(2,1)S(1)} %bitcast.37, ...), custom_call_target="tpu_custom_call" | custom-call | flops 13107200 | bytes 4718592 | tf_op jit(solution)/shard_map/features/pallas_call | solution.py:468
  13.0 0.1 collective-permute-start.3
  13.1 0.0 copy-start.6
  13.1 4.5 %collective-permute-start.4 = (bf16[128,2048]{1,0:T(8,128)(2,1)}, bf16[128,2048]{1,0:T(8,128)(2,1)}, u32[]{:S(2)}, u32[]{:S(2)}) collective-permute-start(bf16[128,2048]{1,0:T(8,128)(2,1)} %get-tuple-element.48.far_hbm), channel_id=1, source_target_pairs={{1,2},{3,4},{5,6},{2,1},{4,3},{6,5},{9,10},{11,12},{13,14},{10,9},... | collective-permute-start | bytes 1572872 | tf_op jit(solution)/shard_map/ppermute | solution.py:479
  17.6 0.0 copy-done.4
  17.6 3.7 %features.2 = (bf16[128,2048]{1,0:T(8,128)(2,1)}, bf16[128,2048]{1,0:T(8,128)(2,1)}, bf16[128,2048]{1,0:T(8,128)(2,1)}, bf16[128,2048]{1,0:T(8,128)(2,1)}, bf16[128,2048]{1,0:T(8,128)(2,1)}) custom-call(bf16[128,4096]{1,0:T(8,128)(2,1)S(1)} %bitcast.28, bf16[128,4096]{1,0:T(8,128)(2,1)S(1)} %bitcast.33, bf16[128,4096]{1,0:T(8,128)(2,1)S(1)} %bitcast.38, ...), custom_call_target="tpu_custom_call" | custom-call | flops 13107200 | bytes 4718592 | tf_op jit(solution)/shard_map/features/pallas_call | solution.py:468
  21.3 0.0 copy-start.7
  21.3 0.1 collective-permute-start.1
  21.4 3.6 %collective-permute-start.2 = (bf16[128,2048]{1,0:T(8,128)(2,1)}, bf16[128,2048]{1,0:T(8,128)(2,1)S(1)}, u32[]{:S(2)}, u32[]{:S(2)}) collective-permute-start(bf16[128,2048]{1,0:T(8,128)(2,1)} %get-tuple-element.43.far_hbm), channel_id=1, source_target_pairs={{1,2},{3,4},{5,6},{2,1},{4,3},{6,5},{9,10},{11,12},{13,14},{10,9},... | collective-permute-start | bytes 1572872 | tf_op jit(solution)/shard_map/ppermute | solution.py:479
  25.0 0.0 collective-permute-done.3.got_near_hbm
  25.0 0.0 collective-permute-done.4.got_far_hbm
  25.0 0.0 copy-done.6
  25.0 0.0 copy-done.7
  25.1 10.0 %filters.2 = (bf16[128,4096]{1,0:T(8,128)(2,1)}, bf16[24,4096]{1,0:T(8,128)(2,1)S(1)}, bf16[128,2048]{1,0:T(8,128)(2,1)S(1)}, bf16[128,2048]{1,0:T(8,128)(2,1)S(...) custom-call(bf16[128,4096]{1,0:T(8,128)(2,1)} %bitcast.25, bf16[128,4096]{1,0:T(8,128)(2,1)} %bitcast.30, ...), custom_call_target="tpu_custom_call" | custom-call | flops 524288000 | bytes 7864320 | tf_op jit(solution)/shard_map/filters/pallas_call | solution.py:485
  35.1 0.0 collective-permute-done.1.got_near_hbm
  35.1 0.0 collective-permute-done.2.got_far_hbm
  35.1 9.9 %filters.3 = (bf16[128,4096]{1,0:T(8,128)(2,1)}, bf16[24,4096]{1,0:T(8,128)(2,1)S(1)}, bf16[128,2048]{1,0:T(8,128)(2,1)S(1)}, bf16[128,2048]{1,0:T(8,128)(2,1)S(...) custom-call(bf16[128,4096]{1,0:T(8,128)(2,1)} %bitcast.26, ...), custom_call_target="tpu_custom_call", output_to_operand_aliasing={{0}: (14, {}), {1}: (15, {})} | custom-call | flops 524288000 | bytes 7864320 | tf_op jit(solution)/shard_map/filters/pallas_call | solution.py:485
  45.1 0.1 collective-permute-start.6
  45.2 2.4 %collective-permute-start.5 = (bf16[24,4096]{1,0:T(8,128)(2,1)S(1)}, bf16[24,4096]{1,0:T(8,128)(2,1)S(1)}, u32[]{:S(2)}, u32[]{:S(2)}) collective-permute-start(bf16[24,4096]{1,0:T(8,128)(2,1)S(1)} %get-tuple-element.57), channel_id=1, source_target_pairs={{1,0},{2,1},{3,2},{4,3},{5,4},{6,5},{7,6},{9,8},{10,9},{11,10},{12... | collective-permute-start | bytes 589832 | tf_op jit(solution)/shard_map/ppermute | solution.py:507
  47.6 0.0 collective-permute-done.6
  47.6 0.0 copy-start.5
  47.7 1.3 %collective-permute-start.7 = (bf16[4,32,128]{2,1,0:T(8,128)(2,1)S(1)}, bf16[4,32,128]{2,1,0:T(8,128)(2,1)S(1)}, u32[]{:S(2)}, u32[]{:S(2)}) collective-permute-start(bf16[4,32,128]{2,1,0:T(8,128)(2,1)S(1)} %get-tuple-element.83), channel_id=1, source_target_pairs={{0,8},{8,0},{16,24},{24,16},{1,9},{9,1},{17,25},{25,17},{2,10},{10... | collective-permute-start | bytes 98312 | tf_op jit(solution)/shard_map/ppermute | solution.py:402
  48.9 1.2 %collective-permute-start.8 = (bf16[4,32,128]{2,1,0:T(8,128)(2,1)S(1)}, bf16[4,32,128]{2,1,0:T(8,128)(2,1)S(1)}, u32[]{:S(2)}, u32[]{:S(2)}) collective-permute-start(bf16[4,32,128]{2,1,0:T(8,128)(2,1)S(1)} %get-tuple-element.82), channel_id=1, source_target_pairs={{0,16},{8,24},{16,0},{24,8},{1,17},{9,25},{17,1},{25,9},{2,18},{10... | collective-permute-start | bytes 98312 | tf_op jit(solution)/shard_map/ppermute | solution.py:402
  50.2 0.2 collective-permute-start.9
  50.4 2.0 %collective-permute-done.5.refs_2_ = bf16[24,4096]{1,0:T(8,128)(2,1)S(1)} collective-permute-done((bf16[24,4096]{1,0:T(8,128)(2,1)S(1)}, bf16[24,4096]{1,0:T(8,128)(2,1)S(1)}, u32[]{:S(2)}, u32[]{:S(2)}) %collective-permute-start.5) | collective-permute-done | bytes 196640 | tf_op jit(solution)/shard_map/ppermute | solution.py:507
  52.3 0.0 copy-done.5
  52.3 2.4 %features_back.3 = (bf16[128,4096]{1,0:T(8,128)(2,1)}, f32[8,128]{1,0:T(8,128)S(1)}) custom-call(bf16[128,2048]{1,0:T(8,128)(2,1)S(1)} %get-tuple-element.55.refs_0_, bf16[128,2048]{1,0:T(8,128)(2,1)S(1)} %get-tuple-element.56.refs_1_, bf16[24,4096]{1,0:T(8,128)(2,1)S(1)} %collective-permute-done.5.refs_2_, f32[7,3,4096]{2,1,0:T(4,128)S(1)} %copy-done.5, ...), custom_call_target="tpu_custom_call" | custom-call | flops 8388608 | bytes 2097152 | tf_op jit(solution)/shard_map/features_back/pallas_call | solution.py:510
  54.8 0.0 collective-permute-done.7.refs_0_
  54.8 0.0 collective-permute-done.8.refs_1_
  54.8 0.0 collective-permute-done.9.refs_2_
  54.8 1.7 %collective-permute-start.10 = (bf16[4,32,128]{2,1,0:T(8,128)(2,1)S(1)}, bf16[4,32,128]{2,1,0:T(8,128)(2,1)S(1)}, u32[]{:S(2)}, u32[]{:S(2)}) collective-permute-start(bf16[4,32,128]{2,1,0:T(8,128)(2,1)S(1)} %get-tuple-element.64.refs_4_), channel_id=1, source_target_pairs={{0,2},{1,3},{2,0},{3,1},{4,6},{5,7},{6,4},{7,5},{8,10},{9,11},{10,... | collective-permute-start | bytes 98312 | tf_op jit(solution)/shard_map/ppermute | solution.py:406
  56.6 2.4 %features_back.4 = (bf16[128,4096]{1,0:T(8,128)(2,1)}, f32[8,128]{1,0:T(8,128)S(1)}) custom-call(bf16[128,2048]{1,0:T(8,128)(2,1)S(1)} %get-tuple-element.61.refs_0_, bf16[128,2048]{1,0:T(8,128)(2,1)S(1)} %get-tuple-element.62.refs_1_, bf16[24,4096]{1,0:T(8,128)(2,1)S(1)} %collective-permute-done.5.refs_2_, f32[7,3,4096]{2,1,0:T(4,128)S(1)} %copy-done.5, ...), custom_call_target="tpu_custom_call" | custom-call | flops 8388608 | bytes 2097152 | tf_op jit(solution)/shard_map/features_back/pallas_call | solution.py:510
  59.0 0.0 collective-permute-done.10.refs_0_
  59.1 1.1 %collective-permute-start.11 = (bf16[4,32,128]{2,1,0:T(8,128)(2,1)S(1)}, bf16[4,32,128]{2,1,0:T(8,128)(2,1)S(1)}, u32[]{:S(2)}, u32[]{:S(2)}) collective-permute-start(bf16[4,32,128]{2,1,0:T(8,128)(2,1)S(1)} %get-tuple-element.70.refs_4_), channel_id=1, source_target_pairs={{0,4},{1,5},{2,6},{3,7},{4,0},{5,1},{6,2},{7,3},{8,12},{9,13},{10,... | collective-permute-start | bytes 98312 | tf_op jit(solution)/shard_map/ppermute | solution.py:406
  60.1 2.4 %features_back.5 = (bf16[128,4096]{1,0:T(8,128)(2,1)}, f32[8,128]{1,0:T(8,128)S(1)}) custom-call(bf16[128,2048]{1,0:T(8,128)(2,1)S(1)} %get-tuple-element.66.refs_0_, bf16[128,2048]{1,0:T(8,128)(2,1)S(1)} %get-tuple-element.67.refs_1_, bf16[24,4096]{1,0:T(8,128)(2,1)S(1)} %collective-permute-done.5.refs_2_, f32[7,3,4096]{2,1,0:T(4,128)S(1)} %copy-done.5, ...), custom_call_target="tpu_custom_call" | custom-call | flops 8388608 | bytes 2097152 | tf_op jit(solution)/shard_map/features_back/pallas_call | solution.py:510
  62.6 0.6 collective-permute-done.11.refs_0_
  63.1 1.3 %collective-permute-start.12 = (bf16[4,32,128]{2,1,0:T(8,128)(2,1)S(1)}, bf16[4,32,128]{2,1,0:T(8,128)(2,1)S(1)}, u32[]{:S(2)}, u32[]{:S(2)}) collective-permute-start(bf16[4,32,128]{2,1,0:T(8,128)(2,1)S(1)} %add.12.refs_0_.refs_4_), channel_id=1, source_target_pairs={{0,8},{8,0},{16,24},{24,16},{1,9},{9,1},{17,25},{25,17},{2,10},{10... | collective-permute-start | bytes 98312 | tf_op jit(solution)/shard_map/ppermute | solution.py:410
  64.4 1.5 %collective-permute-start.13 = (bf16[4,32,128]{2,1,0:T(8,128)(2,1)S(1)}, bf16[4,32,128]{2,1,0:T(8,128)(2,1)S(1)}, u32[]{:S(2)}, u32[]{:S(2)}) collective-permute-start(bf16[4,32,128]{2,1,0:T(8,128)(2,1)S(1)} %add.12.refs_0_.refs_4_), channel_id=1, source_target_pairs={{0,16},{8,24},{16,0},{24,8},{1,17},{9,25},{17,1},{25,9},{2,18},{10... | collective-permute-start | bytes 98312 | tf_op jit(solution)/shard_map/ppermute | solution.py:410
  65.9 0.0 collective-permute-start.14
  65.9 0.1 collective-permute-done.12.refs_1_
  66.0 1.2 %collective-permute-done.13.refs_2_ = bf16[4,32,128]{2,1,0:T(8,128)(2,1)S(1)} collective-permute-done((bf16[4,32,128]{2,1,0:T(8,128)(2,1)S(1)}, bf16[4,32,128]{2,1,0:T(8,128)(2,1)S(1)}, u32[]{:S(2)}, u32[]{:S(2)}) %collective-permute-start.13) | collective-permute-done | bytes 32800 | tf_op jit(solution)/shard_map/ppermute | solution.py:410
  67.2 2.4 %collective-permute-done.14.refs_3_ = bf16[4,32,128]{2,1,0:T(8,128)(2,1)S(1)} collective-permute-done((bf16[4,32,128]{2,1,0:T(8,128)(2,1)S(1)}, bf16[4,32,128]{2,1,0:T(8,128)(2,1)S(1)}, u32[]{:S(2)}, u32[]{:S(2)}) %collective-permute-start.14) | collective-permute-done | bytes 32800 | tf_op jit(solution)/shard_map/ppermute | solution.py:410
  69.6 1.9 %collective-permute-start.15 = (bf16[4,4,32,128]{3,2,1,0:T(8,128)(2,1)S(1)}, bf16[4,4,32,128]{3,2,1,0:T(8,128)(2,1)S(1)}, u32[]{:S(2)}, u32[]{:S(2)}) collective-permute-start(bf16[4,4,32,128]{3,2,1,0:T(8,128)(2,1)S(1)} %join.1), channel_id=1, source_target_pairs={{0,1},{1,0},{2,3},{3,2},{4,5},{5,4},{6,7},{7,6},{8,9},{9,8},{10,11... | collective-permute-start | bytes 393224 | tf_op jit(solution)/shard_map/ppermute | solution.py:419
  71.5 1.0 %collective-permute-done.15 = bf16[4,4,32,128]{3,2,1,0:T(8,128)(2,1)S(1)} collective-permute-done((bf16[4,4,32,128]{3,2,1,0:T(8,128)(2,1)S(1)}, bf16[4,4,32,128]{3,2,1,0:T(8,128)(2,1)S(1)}, u32[]{:S(2)}, u32[]{:S(2)}) %collective-permute-start.15) | collective-permute-done | bytes 131104 | tf_op jit(solution)/shard_map/ppermute | solution.py:419
  72.5 1.0 %unpack.1 = (f32[3,7,4096]{2,1,0:T(8,128)}, f32[256,128]{1,0:T(8,128)}, f32[1,4096]{1,0:T(1,128)}) custom-call(bf16[16,32,128]{2,1,0:T(8,128)(2,1)S(1)} %bitcast.43, bf16[16,32,128]{2,1,0:T(8,128)(2,1)S(1)} %bitcast.44), custom_call_target="tpu_custom_call" | custom-call | tf_op jit(solution)/shard_map/unpack/pallas_call | solution.py:528
  (8 shorter events, 0.1 us)
Async XLA Ops:
  0.6 8.6 %copy-start = (bf16[1,128,4096]{2,1,0:T(8,128)(2,1)S(1)}, bf16[1,128,4096]{2,1,0:T(8,128)(2,1)}, u32[]{:S(2)}) copy-start(bf16[1,128,4096]{2,1,0:T(8,128)(2,1)} %param.7) | copy-start | bytes 3145732
  0.6 8.6 %copy-start.1 = (bf16[1,128,4096]{2,1,0:T(8,128)(2,1)S(1)}, bf16[1,128,4096]{2,1,0:T(8,128)(2,1)}, u32[]{:S(2)}) copy-start(bf16[1,128,4096]{2,1,0:T(8,128)(2,1)} %param.8) | copy-start | bytes 3145732
  0.7 8.6 %copy-start.2 = (bf16[1,128,4096]{2,1,0:T(8,128)(2,1)S(1)}, bf16[1,128,4096]{2,1,0:T(8,128)(2,1)}, u32[]{:S(2)}) copy-start(bf16[1,128,4096]{2,1,0:T(8,128)(2,1)} %param.9) | copy-start | bytes 3145732
  0.7 8.6 %copy-start.3 = (bf16[1,128,4096]{2,1,0:T(8,128)(2,1)S(1)}, bf16[1,128,4096]{2,1,0:T(8,128)(2,1)}, u32[]{:S(2)}) copy-start(bf16[1,128,4096]{2,1,0:T(8,128)(2,1)} %param.10) | copy-start | bytes 3145732
  1.9 7.3 %collective-permute-start = (bf16[24,4096]{1,0:T(8,128)(2,1)S(1)}, bf16[24,4096]{1,0:T(8,128)(2,1)S(1)}, u32[]{:S(2)}, u32[]{:S(2)}) collective-permute-start(bf16[24,4096]{1,0:T(8,128)(2,1)S(1)} %tails.1), channel_id=1, source_target_pairs={{0,1},{1,2},{2,3},{3,4},{4,5},{5,6},{6,7},{8,9},{9,10},{10,11},{11... | collective-permute-start | bytes 589832 | tf_op jit(solution)/shard_map/ppermute | solution.py:462
  7.9 9.7 %copy-start.4 = (f32[7,3,4096]{2,1,0:T(4,128)}, f32[7,3,4096]{2,1,0:T(4,128)S(1)}, u32[]{:S(2)}) copy-start(f32[7,3,4096]{2,1,0:T(4,128)S(1)} %copy.16.taps_ref.refs_3_) | copy-start | bytes 1032196
  13.0 12.0 %collective-permute-start.3 = (bf16[128,2048]{1,0:T(8,128)(2,1)}, bf16[128,2048]{1,0:T(8,128)(2,1)}, u32[]{:S(2)}, u32[]{:S(2)}) collective-permute-start(bf16[128,2048]{1,0:T(8,128)(2,1)} %get-tuple-element.47.near_hbm), channel_id=1, source_target_pairs={{0,1},{1,0},{2,3},{3,2},{4,5},{5,4},{6,7},{7,6},{8,9},{9,8},{10,11... | collective-permute-start | bytes 1572872 | tf_op jit(solution)/shard_map/ppermute | solution.py:480
  13.1 12.0 %copy-start.6 = (f32[256,128]{1,0:T(8,128)S(1)}, f32[256,128]{1,0:T(8,128)}, u32[]{:S(2)}) copy-start(f32[256,128]{1,0:T(8,128)} %filt_ref.3) | copy-start | bytes 393220
  13.1 11.9 %collective-permute-start.4 = (bf16[128,2048]{1,0:T(8,128)(2,1)}, bf16[128,2048]{1,0:T(8,128)(2,1)}, u32[]{:S(2)}, u32[]{:S(2)}) collective-permute-start(bf16[128,2048]{1,0:T(8,128)(2,1)} %get-tuple-element.48.far_hbm), channel_id=1, source_target_pairs={{1,2},{3,4},{5,6},{2,1},{4,3},{6,5},{9,10},{11,12},{13,14},{10,9},... | collective-permute-start | bytes 1572872 | tf_op jit(solution)/shard_map/ppermute | solution.py:479
  21.3 3.7 %copy-start.7 = (f32[4096]{0:T(1024)S(1)}, f32[4096]{0:T(1024)}, u32[]{:S(2)}) copy-start(f32[4096]{0:T(1024)} %param.13) | copy-start | bytes 49156
  21.3 13.8 %collective-permute-start.1 = (bf16[128,2048]{1,0:T(8,128)(2,1)}, bf16[128,2048]{1,0:T(8,128)(2,1)S(1)}, u32[]{:S(2)}, u32[]{:S(2)}) collective-permute-start(bf16[128,2048]{1,0:T(8,128)(2,1)} %get-tuple-element.42.near_hbm), channel_id=1, source_target_pairs={{0,1},{1,0},{2,3},{3,2},{4,5},{5,4},{6,7},{7,6},{8,9},{9,8},{10,11... | collective-permute-start | bytes 1572872 | tf_op jit(solution)/shard_map/ppermute | solution.py:480
  21.4 13.7 %collective-permute-start.2 = (bf16[128,2048]{1,0:T(8,128)(2,1)}, bf16[128,2048]{1,0:T(8,128)(2,1)S(1)}, u32[]{:S(2)}, u32[]{:S(2)}) collective-permute-start(bf16[128,2048]{1,0:T(8,128)(2,1)} %get-tuple-element.43.far_hbm), channel_id=1, source_target_pairs={{1,2},{3,4},{5,6},{2,1},{4,3},{6,5},{9,10},{11,12},{13,14},{10,9},... | collective-permute-start | bytes 1572872 | tf_op jit(solution)/shard_map/ppermute | solution.py:479
  45.1 2.5 %collective-permute-start.6 = (bf16[4,4,32,128]{3,2,1,0:T(8,128)(2,1)S(1)}, bf16[4,4,32,128]{3,2,1,0:T(8,128)(2,1)S(1)}, u32[]{:S(2)}, u32[]{:S(2)}) collective-permute-start(bf16[4,4,32,128]{3,2,1,0:T(8,128)(2,1)S(1)} %bitcast.49), channel_id=1, source_target_pairs={{0,1},{1,0},{2,3},{3,2},{4,5},{5,4},{6,7},{7,6},{8,9},{9,8},{10,11... | collective-permute-start | bytes 393224 | tf_op jit(solution)/shard_map/ppermute | solution.py:400
  45.2 7.2 %collective-permute-start.5 = (bf16[24,4096]{1,0:T(8,128)(2,1)S(1)}, bf16[24,4096]{1,0:T(8,128)(2,1)S(1)}, u32[]{:S(2)}, u32[]{:S(2)}) collective-permute-start(bf16[24,4096]{1,0:T(8,128)(2,1)S(1)} %get-tuple-element.57), channel_id=1, source_target_pairs={{1,0},{2,1},{3,2},{4,3},{5,4},{6,5},{7,6},{9,8},{10,9},{11,10},{12... | collective-permute-start | bytes 589832 | tf_op jit(solution)/shard_map/ppermute | solution.py:507
  47.6 4.8 %copy-start.5 = (f32[7,3,4096]{2,1,0:T(4,128)S(1)}, f32[7,3,4096]{2,1,0:T(4,128)}, u32[]{:S(2)}) copy-start(f32[7,3,4096]{2,1,0:T(4,128)} %copy-done.4) | copy-start | bytes 1032196
  47.7 7.1 %collective-permute-start.7 = (bf16[4,32,128]{2,1,0:T(8,128)(2,1)S(1)}, bf16[4,32,128]{2,1,0:T(8,128)(2,1)S(1)}, u32[]{:S(2)}, u32[]{:S(2)}) collective-permute-start(bf16[4,32,128]{2,1,0:T(8,128)(2,1)S(1)} %get-tuple-element.83), channel_id=1, source_target_pairs={{0,8},{8,0},{16,24},{24,16},{1,9},{9,1},{17,25},{25,17},{2,10},{10... | collective-permute-start | bytes 98312 | tf_op jit(solution)/shard_map/ppermute | solution.py:402
  48.9 5.9 %collective-permute-start.8 = (bf16[4,32,128]{2,1,0:T(8,128)(2,1)S(1)}, bf16[4,32,128]{2,1,0:T(8,128)(2,1)S(1)}, u32[]{:S(2)}, u32[]{:S(2)}) collective-permute-start(bf16[4,32,128]{2,1,0:T(8,128)(2,1)S(1)} %get-tuple-element.82), channel_id=1, source_target_pairs={{0,16},{8,24},{16,0},{24,8},{1,17},{9,25},{17,1},{25,9},{2,18},{10... | collective-permute-start | bytes 98312 | tf_op jit(solution)/shard_map/ppermute | solution.py:402
  50.2 4.6 %collective-permute-start.9 = (bf16[4,32,128]{2,1,0:T(8,128)(2,1)S(1)}, bf16[4,32,128]{2,1,0:T(8,128)(2,1)S(1)}, u32[]{:S(2)}, u32[]{:S(2)}) collective-permute-start(bf16[4,32,128]{2,1,0:T(8,128)(2,1)S(1)} %get-tuple-element.81), channel_id=1, source_target_pairs={{0,24},{8,16},{16,8},{24,0},{1,25},{9,17},{17,9},{25,1},{2,26},{10... | collective-permute-start | bytes 98312 | tf_op jit(solution)/shard_map/ppermute | solution.py:402
  54.8 4.2 %collective-permute-start.10 = (bf16[4,32,128]{2,1,0:T(8,128)(2,1)S(1)}, bf16[4,32,128]{2,1,0:T(8,128)(2,1)S(1)}, u32[]{:S(2)}, u32[]{:S(2)}) collective-permute-start(bf16[4,32,128]{2,1,0:T(8,128)(2,1)S(1)} %get-tuple-element.64.refs_4_), channel_id=1, source_target_pairs={{0,2},{1,3},{2,0},{3,1},{4,6},{5,7},{6,4},{7,5},{8,10},{9,11},{10,... | collective-permute-start | bytes 98312 | tf_op jit(solution)/shard_map/ppermute | solution.py:406
  59.1 4.1 %collective-permute-start.11 = (bf16[4,32,128]{2,1,0:T(8,128)(2,1)S(1)}, bf16[4,32,128]{2,1,0:T(8,128)(2,1)S(1)}, u32[]{:S(2)}, u32[]{:S(2)}) collective-permute-start(bf16[4,32,128]{2,1,0:T(8,128)(2,1)S(1)} %get-tuple-element.70.refs_4_), channel_id=1, source_target_pairs={{0,4},{1,5},{2,6},{3,7},{4,0},{5,1},{6,2},{7,3},{8,12},{9,13},{10,... | collective-permute-start | bytes 98312 | tf_op jit(solution)/shard_map/ppermute | solution.py:406
  63.1 2.8 %collective-permute-start.12 = (bf16[4,32,128]{2,1,0:T(8,128)(2,1)S(1)}, bf16[4,32,128]{2,1,0:T(8,128)(2,1)S(1)}, u32[]{:S(2)}, u32[]{:S(2)}) collective-permute-start(bf16[4,32,128]{2,1,0:T(8,128)(2,1)S(1)} %add.12.refs_0_.refs_4_), channel_id=1, source_target_pairs={{0,8},{8,0},{16,24},{24,16},{1,9},{9,1},{17,25},{25,17},{2,10},{10... | collective-permute-start | bytes 98312 | tf_op jit(solution)/shard_map/ppermute | solution.py:410
  64.4 2.8 %collective-permute-start.13 = (bf16[4,32,128]{2,1,0:T(8,128)(2,1)S(1)}, bf16[4,32,128]{2,1,0:T(8,128)(2,1)S(1)}, u32[]{:S(2)}, u32[]{:S(2)}) collective-permute-start(bf16[4,32,128]{2,1,0:T(8,128)(2,1)S(1)} %add.12.refs_0_.refs_4_), channel_id=1, source_target_pairs={{0,16},{8,24},{16,0},{24,8},{1,17},{9,25},{17,1},{25,9},{2,18},{10... | collective-permute-start | bytes 98312 | tf_op jit(solution)/shard_map/ppermute | solution.py:410
  65.9 3.7 %collective-permute-start.14 = (bf16[4,32,128]{2,1,0:T(8,128)(2,1)S(1)}, bf16[4,32,128]{2,1,0:T(8,128)(2,1)S(1)}, u32[]{:S(2)}, u32[]{:S(2)}) collective-permute-start(bf16[4,32,128]{2,1,0:T(8,128)(2,1)S(1)} %add.12.refs_0_.refs_4_), channel_id=1, source_target_pairs={{0,24},{8,16},{16,8},{24,0},{1,25},{9,17},{17,9},{25,1},{2,26},{10... | collective-permute-start | bytes 98312 | tf_op jit(solution)/shard_map/ppermute | solution.py:410
  69.6 2.9 %collective-permute-start.15 = (bf16[4,4,32,128]{3,2,1,0:T(8,128)(2,1)S(1)}, bf16[4,4,32,128]{3,2,1,0:T(8,128)(2,1)S(1)}, u32[]{:S(2)}, u32[]{:S(2)}) collective-permute-start(bf16[4,4,32,128]{3,2,1,0:T(8,128)(2,1)S(1)} %join.1), channel_id=1, source_target_pairs={{0,1},{1,0},{2,3},{3,2},{4,5},{5,4},{6,7},{7,6},{8,9},{9,8},{10,11... | collective-permute-start | bytes 393224 | tf_op jit(solution)/shard_map/ppermute | solution.py:419
